TPU v7x, 256 devices: a whole 4x4x8 slice. The times are simulated.
256 devices in a mesh: rows: 16 (over z_lo, y), out: 16 (over z_hi, x, core).
Axes of the slice: x: 4, y: 4, z: 8 (z_hi: 2, z_lo: 4; z = z_hi * 4 + z_lo), core: 2. Of those that a mesh axis runs over, the one named last changes fastest.
Arguments:
- predictions: bfloat16 [131072, 4096], P('rows', 'out'), may hold values from -5 to 5
- targets: bfloat16 [131072, 4096], P('rows', 'out'), may hold values from -4.5 to 4.5
- row_weight: bfloat16 [131072], P('rows'), may hold values from 0.25 to 4
- features: int32 [131072, 256], P('rows', 'out'), may hold values from 0 to 255
- leaf: int32 [131072], P('rows'), may hold values from 0 to 63
- sketch_matrix: bfloat16 [4096, 32], P('out'), may hold values from -0.00390625 to 0.00390625
Outputs:
- hist_grad: float32 [256, 256, 32], P('rows', 'out')
- hist_hess: float32 [256, 256], P('rows', 'out')
- leaf_values: float32 [64, 4096], P('rows', 'out')
All inputs are finite; a program needn't handle non-finite values.
Results may differ from a plain program's by a relative error of at most 0.0022.
Values may be sent and summed in bfloat16 or wider, within the bound.
No kernel may reach another device: no remote copies, remote signals or barrier semaphores. Data moves between devices by JAX's collectives and lax.ppermute only.
A program may use at most 64 MiB of HBM per device.

v0:
```python
import jax
import jax.numpy as jnp
from jax import lax
from jax.sharding import PartitionSpec as P

BINS = 256
LEAVES = 64


ridge = 1.0


def per_device(predictions, targets, row_weight, features, leaf, sketch_matrix):
    rows_local = predictions.shape[0]
    weight_wide = row_weight.astype(jnp.float32)
    gradient = (
        weight_wide[:, None] * (predictions.astype(jnp.float32) - targets.astype(jnp.float32))
    ).astype(jnp.bfloat16)
    partial_value = jnp.dot(gradient, sketch_matrix, preferred_element_type=jnp.float32)
    sketch = lax.psum(partial_value, "out").astype(jnp.bfloat16)
    augmented = jnp.concatenate([sketch, row_weight[:, None]], axis=1)
    feat_local = features.shape[1]
    columns = augmented.shape[1]
    block_rows = min(1024, rows_local)
    block_count = rows_local // block_rows
    levels = lax.iota(jnp.int32, BINS // lax.axis_size("rows") * lax.axis_size("rows"))

    def add_block(position, running):
        bins_block = lax.dynamic_slice_in_dim(features, position * block_rows, block_rows, 0)
        aug_block = lax.dynamic_slice_in_dim(augmented, position * block_rows, block_rows, 0)
        onehot = (bins_block[:, :, None] == levels[None, None, :]).astype(jnp.bfloat16)
        return running + jnp.einsum(
            "rfb,rk->bfk", onehot, aug_block, preferred_element_type=jnp.float32
        )

    histogram = lax.psum_scatter(
        lax.fori_loop(
            0,
            block_count,
            add_block,
            jnp.zeros(
                (BINS // lax.axis_size("rows") * lax.axis_size("rows"), feat_local, columns),
                jnp.float32,
            ),
        ),
        "rows",
        scatter_dimension=0,
        tiled=True,
    )
    cells_all = rows_local * lax.axis_size("rows")
    hist_grad = histogram[:, :, : columns - 1]
    hist_hess = histogram[:, :, columns - 1] / (cells_all / BINS)
    leaf_onehot = (leaf[:, None] == lax.iota(jnp.int32, LEAVES)[None, :]).astype(jnp.bfloat16)
    leaf_sums = jnp.einsum("rl,rg->lg", leaf_onehot, gradient, preferred_element_type=jnp.float32)
    leaf_weights = jnp.einsum(
        "rl,r->l", leaf_onehot, row_weight, preferred_element_type=jnp.float32
    )
    total_sums, total_weights = (
        lax.psum_scatter(leaf_sums, "rows", scatter_dimension=0, tiled=True),
        lax.psum_scatter(leaf_weights, "rows", scatter_dimension=0, tiled=True),
    )
    leaf_values = -total_sums / (total_weights[:, None] + ridge)
    return (hist_grad, hist_hess, leaf_values)


def solution(mesh):
    return jax.shard_map(
        per_device,
        mesh=mesh,
        in_specs=(
            P("rows", "out"),
            P("rows", "out"),
            P("rows"),
            P("rows", "out"),
            P("rows"),
            P("out", None),
        ),
        out_specs=(P("rows", "out", None), P("rows", "out"), P("rows", "out")),
        check_vma=False,
    )
```

profile of v0, /device:TPU:6, one launch (start us, length us, event | category | flops | bytes accessed | tf_op | source)
XLA Modules:
  0.0 280.9 jit_solution(3560544876262697367)
XLA Ops:
  7.2 0.0 copy-start
  7.2 0.0 all-reduce.5.cloned.1.call-start
  7.2 0.7 convert_element_type.19
  7.9 0.0 copy-start.3
  8.0 4.2 %multiply_convert_fusion = bf16[8192,256]{1,0:T(8,128)(2,1)S(1)} fusion(bf16[8192,256]{1,0:T(8,128)(2,1)} %param.9, bf16[8192,256]{1,0:T(8,128)(2,1)} %param.8, f32[8192]{0:T(1024)S(1)} %convert_element_type.19), kind=kLoop, calls=%fused_computation.10 | loop fusion | flops 10485760 | bytes 12615680 | tf_op jit(solution)/shard_map/convert_element_type | solution.py:18
  12.1 0.0 copy-start.1
  12.1 1.9 copy-done.1
  14.1 0.0 copy-done.3
  14.1 0.0 copy-start.2
  14.1 1.3 fusion.10
  15.4 0.0 all-reduce.5.cloned.1.call-update
  15.4 0.0 reduce-scatter.2.cloned.1.call-start
  15.5 0.0 copy-done.2
  15.5 0.0 copy-done
  15.5 3.5 %fusion.16 = f32[8192,32]{0,1:T(8,128)S(1)} fusion(bf16[8192,256]{1,0:T(8,128)(2,1)} %copy-done.1, bf16[256,32]{0,1:T(8,128)(2,1)S(1)} %copy-done), kind=kOutput, calls=%fused_computation.23 | convolution fusion | flops 134217728 | bytes 5259264 | tf_op jit(solution)/shard_map/dot_general | solution.py:19
  19.0 94.2 %all-reduce.6 = bf16[8192,32]{0,1:T(8,128)(2,1)S(1)} all-reduce(f32[8192,32]{0,1:T(8,128)S(1)} %fusion.16), channel_id=1, replica_groups=mesh['rows'=16,'out'=16] {'out'}, use_global_device_ids=true, to_apply=%region_0.0 | all-reduce | flops 262144 | bytes 1572864 | tf_op jit(solution)/shard_map/psum | solution.py:20
  113.3 0.1 pad_maximum_fusion
  113.4 54.2 %while.14 = (s32[]{:T(128)}, f32[256,16,33]{0,2,1:T(8,128)S(1)}, bf16[8192,33]{0,1:T(8,128)(2,1)S(1)}, s32[8192,16]{0,1:T(8,128)}, s32[]{:T(128)}, /*index=5*/s32[]{:T(128)}, s32[]{:T(128)}, s32[]{:T(128)}) while((s32[]{:T(128)}, f32[256,16,33]{0,2,1:T(8,128)S(1)}, bf16[8192,33]{0,1:T(8,128)(2,1)S(1)}, s32[8192,16]{0,1:T(8,128)}, ...), condition=%wide.region_2.0_spmd.clone, body=%wide.region_1.0_spmd.clone.sunk | while | flops 281288704 | bytes 1474709 | solution.py:37
  113.4 0.9 constant_dynamic-slice_fusion.2
  114.2 5.9 %fusion.24 = f32[256,16,33]{0,2,1:T(8,128)S(1)} fusion(s32[1024,16]{0,1:T(8,128)S(1)} %constant_dynamic-slice_fusion.2, f32[256,16,33]{0,2,1:T(8,128)S(1)} %get-tuple-element.166, pred[]{:T(512)S(6)} %compare.3, bf16[8192,33]{0,1:T(8,128)(2,1)S(1)} %get-tuple-element.175, s32[]{:T(128)S(6)} %select_n.10), kind=kOutput, calls=%fused_computation.5.clone.1 | convolution fusion | flops 281288704 | bytes 1343493 | tf_op jit(solution)/shard_map/while/body/eval_jaxpr/rfb,rk->bfk/dot_general | solution.py:32
  120.1 0.9 constant_dynamic-slice_fusion.2
  121.0 5.9 %fusion.24 = f32[256,16,33]{0,2,1:T(8,128)S(1)} fusion(s32[1024,16]{0,1:T(8,128)S(1)} %constant_dynamic-slice_fusion.2, f32[256,16,33]{0,2,1:T(8,128)S(1)} %get-tuple-element.166, pred[]{:T(512)S(6)} %compare.3, bf16[8192,33]{0,1:T(8,128)(2,1)S(1)} %get-tuple-element.175, s32[]{:T(128)S(6)} %select_n.10), kind=kOutput, calls=%fused_computation.5.clone.1 | convolution fusion | flops 281288704 | bytes 1343493 | tf_op jit(solution)/shard_map/while/body/eval_jaxpr/rfb,rk->bfk/dot_general | solution.py:32
  126.9 0.9 constant_dynamic-slice_fusion.2
  127.8 5.9 %fusion.24 = f32[256,16,33]{0,2,1:T(8,128)S(1)} fusion(s32[1024,16]{0,1:T(8,128)S(1)} %constant_dynamic-slice_fusion.2, f32[256,16,33]{0,2,1:T(8,128)S(1)} %get-tuple-element.166, pred[]{:T(512)S(6)} %compare.3, bf16[8192,33]{0,1:T(8,128)(2,1)S(1)} %get-tuple-element.175, s32[]{:T(128)S(6)} %select_n.10), kind=kOutput, calls=%fused_computation.5.clone.1 | convolution fusion | flops 281288704 | bytes 1343493 | tf_op jit(solution)/shard_map/while/body/eval_jaxpr/rfb,rk->bfk/dot_general | solution.py:32
  133.7 0.9 constant_dynamic-slice_fusion.2
  134.5 5.9 %fusion.24 = f32[256,16,33]{0,2,1:T(8,128)S(1)} fusion(s32[1024,16]{0,1:T(8,128)S(1)} %constant_dynamic-slice_fusion.2, f32[256,16,33]{0,2,1:T(8,128)S(1)} %get-tuple-element.166, pred[]{:T(512)S(6)} %compare.3, bf16[8192,33]{0,1:T(8,128)(2,1)S(1)} %get-tuple-element.175, s32[]{:T(128)S(6)} %select_n.10), kind=kOutput, calls=%fused_computation.5.clone.1 | convolution fusion | flops 281288704 | bytes 1343493 | tf_op jit(solution)/shard_map/while/body/eval_jaxpr/rfb,rk->bfk/dot_general | solution.py:32
  140.5 0.9 constant_dynamic-slice_fusion.2
  141.3 5.9 %fusion.24 = f32[256,16,33]{0,2,1:T(8,128)S(1)} fusion(s32[1024,16]{0,1:T(8,128)S(1)} %constant_dynamic-slice_fusion.2, f32[256,16,33]{0,2,1:T(8,128)S(1)} %get-tuple-element.166, pred[]{:T(512)S(6)} %compare.3, bf16[8192,33]{0,1:T(8,128)(2,1)S(1)} %get-tuple-element.175, s32[]{:T(128)S(6)} %select_n.10), kind=kOutput, calls=%fused_computation.5.clone.1 | convolution fusion | flops 281288704 | bytes 1343493 | tf_op jit(solution)/shard_map/while/body/eval_jaxpr/rfb,rk->bfk/dot_general | solution.py:32
  147.2 0.9 constant_dynamic-slice_fusion.2
  148.1 5.9 %fusion.24 = f32[256,16,33]{0,2,1:T(8,128)S(1)} fusion(s32[1024,16]{0,1:T(8,128)S(1)} %constant_dynamic-slice_fusion.2, f32[256,16,33]{0,2,1:T(8,128)S(1)} %get-tuple-element.166, pred[]{:T(512)S(6)} %compare.3, bf16[8192,33]{0,1:T(8,128)(2,1)S(1)} %get-tuple-element.175, s32[]{:T(128)S(6)} %select_n.10), kind=kOutput, calls=%fused_computation.5.clone.1 | convolution fusion | flops 281288704 | bytes 1343493 | tf_op jit(solution)/shard_map/while/body/eval_jaxpr/rfb,rk->bfk/dot_general | solution.py:32
  154.0 0.9 constant_dynamic-slice_fusion.2
  154.9 5.9 %fusion.24 = f32[256,16,33]{0,2,1:T(8,128)S(1)} fusion(s32[1024,16]{0,1:T(8,128)S(1)} %constant_dynamic-slice_fusion.2, f32[256,16,33]{0,2,1:T(8,128)S(1)} %get-tuple-element.166, pred[]{:T(512)S(6)} %compare.3, bf16[8192,33]{0,1:T(8,128)(2,1)S(1)} %get-tuple-element.175, s32[]{:T(128)S(6)} %select_n.10), kind=kOutput, calls=%fused_computation.5.clone.1 | convolution fusion | flops 281288704 | bytes 1343493 | tf_op jit(solution)/shard_map/while/body/eval_jaxpr/rfb,rk->bfk/dot_general | solution.py:32
  160.8 0.9 constant_dynamic-slice_fusion.2
  161.6 5.9 %fusion.24 = f32[256,16,33]{0,2,1:T(8,128)S(1)} fusion(s32[1024,16]{0,1:T(8,128)S(1)} %constant_dynamic-slice_fusion.2, f32[256,16,33]{0,2,1:T(8,128)S(1)} %get-tuple-element.166, pred[]{:T(512)S(6)} %compare.3, bf16[8192,33]{0,1:T(8,128)(2,1)S(1)} %get-tuple-element.175, s32[]{:T(128)S(6)} %select_n.10), kind=kOutput, calls=%fused_computation.5.clone.1 | convolution fusion | flops 281288704 | bytes 1343493 | tf_op jit(solution)/shard_map/while/body/eval_jaxpr/rfb,rk->bfk/dot_general | solution.py:32
  167.5 0.0 copy-start.4
  167.6 2.8 copy.13
  170.3 0.0 reduce-scatter.2.cloned.1.call-update
  170.4 0.0 copy-done.4
  170.4 0.6 dynamic-slice
  171.6 0.4 fusion.11
  172.0 45.1 %all-reduce.1 = f32[64]{0:T(128)S(1)} all-reduce(f32[64]{0:T(128)S(1)} %fusion.11), channel_id=4, replica_groups=mesh['rows'=16,'out'=16] {'rows'}, use_global_device_ids=true, to_apply=%region_5.0.clone | all-reduce | flops 64 | bytes 512
  217.2 0.1 dynamic-slice_add_fusion
  217.2 0.0 all-reduce.5.cloned.1.call-done
  217.2 1.4 fusion.15
  218.6 52.4 %reduce-scatter.2.cloned.1.call-done = f32[16,16,33]{1,0,2:T(8,128)} async-done(((f32[256,16,33]{1,0,2:T(8,128)}), f32[16,16,33]{1,0,2:T(8,128)}) %reduce-scatter.2.cloned.1.call-update) | async-done | bytes 33808 | tf_op jit(solution)/shard_map/reduce_scatter | solution.py:36
  271.0 1.0 slice.8
  271.9 0.8 copy.14
  272.8 1.3 fusion.14
  (2 shorter events, 0.0 us)
Async XLA Ops:
  7.2 8.4 %copy-start = (bf16[256,32]{0,1:T(8,128)(2,1)S(1)}, bf16[256,32]{0,1:T(8,128)(2,1)}, u32[]{:S(2)}) copy-start(bf16[256,32]{0,1:T(8,128)(2,1)} %param.13) | copy-start | bytes 49156
  7.2 210.1 %all-reduce.5.cloned.1.call-start = ((), (), s32[]{:S(2)}) async-start(), calls=%async_computation.2 | async-start | bytes 131072
  7.9 6.1 %copy-start.3 = (s32[8192]{0:T(1024)S(1)}, s32[8192]{0:T(1024)}, u32[]{:S(2)}) copy-start(s32[8192]{0:T(1024)} %param.12) | copy-start | bytes 98308
  12.1 1.9 copy-start.1
  14.1 1.4 copy-start.2
  15.4 255.5 %reduce-scatter.2.cloned.1.call-start = ((), (), s32[]{:S(2)}) async-start(), calls=%async_computation.1 | async-start | bytes 4595712 | tf_op jit(solution)/shard_map/reduce_scatter | solution.py:36
  167.5 2.8 %copy-start.4 = (u32[256]{0:T(256)S(1)}, u32[256]{0:T(256)}, u32[]{:S(2)}) copy-start(u32[256]{0:T(256)} %constant.39) | copy-start | bytes 3076
Sparse Core Ops, SparseCore 0:
  15.6 149.6 all-reduce.4
  170.5 100.4 reduce-scatter.1
where the time goes:
time: 282 us; the launch traced here: 281 us
  blocking collectives  139 us (49%)
  matrix products  52.4 us (19%)
  waiting for transfers between devices  52.4 us (19%)
  between operations  14.8 us (5%)
  local copies, waits for them, and re-layouts  13.9 us (5%)
  other arithmetic  7.68 us (3%)
    psum x1, blocking collectives, per_device(): sketch = lax.psum(partial_value, 'out').astype(jnp.bfloat16)  94.2 us
    reduce_scatter x1, waiting for transfers between devices, per_device(): lax.psum_scatter(lax.fori_loop(0, block_count, add_block, jnp.zeros((BINS...  52.4 us
    dot_general x8, matrix products, add_block(): jnp.einsum('rfb,rk->bfk', onehot, aug_block, preferred_element_type=jnp.f...  47.1 us
    unnamed x1, blocking collectives  45.1 us
    dynamic_slice x8, local copies, waits for them, and re-layouts, add_block(): lax.dynamic_slice_in_dim(features, position * block_rows, block_rows, 0)  6.8 us
  transfers between devices with their start and end apart: 2, of which 1 were waited for; matrix products, arithmetic and copies ran while one was open for 22% of the time, Pallas kernels for 0%

commit v1 on v0

v1 whole, which is shorter than its diff:
```python
import functools

import jax
import jax.numpy as jnp
from jax import lax
from jax.experimental import pallas as pl
from jax.experimental.pallas import tpu as pltpu
from jax.sharding import PartitionSpec as P

BINS = 256
LEAVES = 64
RIDGE = 1.0
F32 = jnp.float32
BF16 = jnp.bfloat16
BLOCK = 1024
CONTRACT_LAST = (((1,), (1,)), ((), ()))


def gradient_kernel(where, pred, targ, weight, leaf, matrix_t, leaf_in, sketch_out, leaf_out, sums, weights, *, steps):
    step = pl.program_id(0)
    cells = pred.shape[0]

    @pl.when(step == 0)
    def _():
        sums[...] = jnp.zeros_like(sums)
        weights[...] = jnp.zeros_like(weights)

    w_row = weight[...]
    w_wide = w_row.astype(F32)
    w_tile = jnp.concatenate([w_wide[:, 128 * s : 128 * s + 128] for s in range(cells // 128)], axis=0)
    w_cols = jnp.transpose(w_tile)
    pieces = []
    for s in range(cells // 128):
        rows = slice(128 * s, 128 * s + 128)
        diff = pred[rows, :].astype(F32) - targ[rows, :].astype(F32)
        pieces.append((w_cols[:, s : s + 1] * diff).astype(BF16))
    gradient = jnp.concatenate(pieces, axis=0)
    sketch_out[...] = lax.dot_general(matrix_t[...], gradient, CONTRACT_LAST, preferred_element_type=F32)
    own = leaf[...] ^ where[2]
    place = ((own >> 2) & 3) * 16 + (own >> 4) * 4 + (own & 3)
    onehot = jnp.where(lax.broadcasted_iota(jnp.int32, (LEAVES, cells), 0) == place, 1.0, 0.0).astype(BF16)
    sums[...] += jnp.dot(onehot, gradient, preferred_element_type=F32)
    weights[...] += lax.dot_general(
        onehot, jnp.broadcast_to(w_row, (128, cells)), CONTRACT_LAST, preferred_element_type=F32
    )

    @pl.when(step == steps - 1)
    def _():
        for y in range(4):
            for z in range(4):
                top = 16 * y + 4 * z
                for h in range(2):
                    at = 8 * z + 4 * h
                    leaf_out[y, at : at + 4, :] = (
                        leaf_in[y, at : at + 4, :] + sums[top : top + 4, 128 * h : 128 * h + 128]
                    )
                    leaf_out[y, 32 + at : 36 + at, :] = leaf_in[y, 32 + at : 36 + at, :] + weights[top : top + 4, :]


def gradient_half(where, pred, targ, weight, leaf, matrix_t, leaf_in, first):
    genes = pred.shape[1]
    steps = pred.shape[0] // BLOCK // 2
    block = lambda j, where: (j + first) ^ where[0]
    return pl.pallas_call(
        functools.partial(gradient_kernel, steps=steps),
        grid_spec=pltpu.PrefetchScalarGridSpec(
            num_scalar_prefetch=1,
            grid=(steps,),
            in_specs=[
                pl.BlockSpec((BLOCK, genes), lambda j, s: (block(j, s), 0)),
                pl.BlockSpec((BLOCK, genes), lambda j, s: (block(j, s), 0)),
                pl.BlockSpec((1, BLOCK), lambda j, s: (0, block(j, s))),
                pl.BlockSpec((1, BLOCK), lambda j, s: (0, block(j, s))),
                pl.BlockSpec(matrix_t.shape, lambda j, s: (0, 0)),
                pl.BlockSpec((4, 64, 128), lambda j, s: (0, 0, 0)),
            ],
            out_specs=[
                pl.BlockSpec((matrix_t.shape[0], BLOCK), lambda j, s: (0, j)),
                pl.BlockSpec((4, 64, 128), lambda j, s: (0, 0, 0)),
            ],
            scratch_shapes=[pltpu.VMEM((LEAVES, genes), F32), pltpu.VMEM((LEAVES, 128), F32)],
        ),
        out_shape=[
            jax.ShapeDtypeStruct((matrix_t.shape[0], steps * BLOCK), F32),
            jax.ShapeDtypeStruct((4, 64, 128), F32),
        ],
        compiler_params=pltpu.CompilerParams(vmem_limit_bytes=40 * 1024 * 1024),
        cost_estimate=pl.CostEstimate(flops=2 * 4096 * 256 * 300, bytes_accessed=5000000, transcendentals=0),
        name="gradient",
    )(where, pred, targ, weight, leaf, matrix_t, leaf_in)


def histogram_kernel(where, feat, sketch, weight, leaf_part, o0, o1, o2, o3, hess, *, steps):
    step = pl.program_id(0)
    outs = (o0, o1, o2, o3)
    cells = feat.shape[1]

    @pl.when(step == 0)
    def _():
        hess[...] = jnp.zeros_like(hess)
        for y in range(4):
            outs[y][0:256, :] = jnp.zeros((256, 128), F32)
            outs[y][272:336, :] = leaf_part[y]

    sketch_all = sketch[...]
    w_all = jnp.broadcast_to(weight[...], (16, cells))
    rows64 = lax.broadcasted_iota(jnp.int32, (64, cells), 0).astype(BF16)
    rows16 = lax.broadcasted_iota(jnp.int32, (16, cells), 0).astype(BF16)
    zero = jnp.zeros((), BF16)
    one = jnp.ones((), BF16)
    for f in range(16):
        own = feat[f : f + 1, :] ^ where[1]
        low = (own & 63).astype(F32).astype(BF16)
        high = own >> 6
        group = jnp.broadcast_to(high.astype(F32).astype(BF16), (32, cells))
        left = jnp.where(rows64 == low, one, zero)
        parts = [jnp.where(group == jnp.asarray(z, BF16), sketch_all, zero) for z in range(4)]
        spot = (high * 4 + (f % 4)).astype(F32).astype(BF16)
        parts.append(jnp.where(rows16 == spot, w_all, zero))
        right = jnp.concatenate(parts, axis=0)
        both = lax.dot_general(left, right, CONTRACT_LAST, preferred_element_type=F32)
        for y in range(4):
            outs[y][16 * f : 16 * f + 16, :] += both[16 * y : 16 * y + 16, :128]
        hess[f // 4] += both[:, 128:144]

    @pl.when(step == steps - 1)
    def _():
        held = [hess[g] for g in range(4)]
        lanes = [held[g][:, 4 * z : 4 * z + 4] for z in range(4) for g in range(4)]
        whole = jnp.concatenate(lanes + [jnp.zeros((64, 64), F32)], axis=1)
        for y in range(4):
            outs[y][256:272, :] = whole[16 * y : 16 * y + 16, :]


def histogram(where, feat_t, sketch, weight, leaf_part):
    cells = feat_t.shape[1]
    steps = cells // BLOCK
    return pl.pallas_call(
        functools.partial(histogram_kernel, steps=steps),
        grid_spec=pltpu.PrefetchScalarGridSpec(
            num_scalar_prefetch=1,
            grid=(steps,),
            in_specs=[
                pl.BlockSpec((16, BLOCK), lambda j, s: (0, j ^ s[0])),
                pl.BlockSpec((32, BLOCK), lambda j, s: (0, j)),
                pl.BlockSpec((1, BLOCK), lambda j, s: (0, j ^ s[0])),
                pl.BlockSpec((4, 64, 128), lambda j, s: (0, 0, 0)),
            ],
            out_specs=[pl.BlockSpec((336, 128), lambda j, s: (0, 0))] * 4,
            scratch_shapes=[pltpu.VMEM((4, 64, 16), F32)],
        ),
        out_shape=[jax.ShapeDtypeStruct((336, 128), F32)] * 4,
        compiler_params=pltpu.CompilerParams(vmem_limit_bytes=40 * 1024 * 1024),
        cost_estimate=pl.CostEstimate(flops=2 * 8192 * 4096 * 256, bytes_accessed=1500000, transcendentals=0),
        name="histogram",
    )(where, feat_t, sketch, weight, leaf_part)


def regroup_kernel(a, b, c, d, o0, o1, o2, o3):
    outs = (o0, o1, o2, o3)
    total = a[...] + b[...] + c[...] + d[...]
    for z in range(4):
        outs[z][0:64, :] = jnp.concatenate(
            [total[64 * q : 64 * q + 64, 32 * z : 32 * z + 32] for q in range(4)], axis=1
        )
        outs[z][64:80, :] = jnp.concatenate(
            [total[256:272, 16 * z : 16 * z + 16], jnp.zeros((16, 112), F32)], axis=1
        )
        outs[z][80:88, :] = total[272 + 8 * z : 280 + 8 * z, :]
        outs[z][88:96, :] = total[304 + 8 * z : 312 + 8 * z, :]


def regroup(a, b, c, d):
    return pl.pallas_call(
        regroup_kernel,
        out_shape=[jax.ShapeDtypeStruct((96, 128), F32)] * 4,
        name="regroup",
    )(a, b, c, d)


def finish_kernel(a, b, c, d, grad_out, hess_out, leaf_out, rows, *, per_bin):
    total = a[...] + b[...] + c[...] + d[...]
    for q in range(4):
        rows[64 * q : 64 * q + 64, 0:32] = total[0:64, 32 * q : 32 * q + 32]
    for i in range(16):
        grad_out[i] = rows[pl.ds(i, 16, stride=16), :][:, 0:32]
    hess_out[...] = total[64:80, 0:16] / per_bin
    values = -total[80:88, :] / (total[88:96, :] + RIDGE)
    leaf_out[:, 0:128] = values[0:4]
    leaf_out[:, 128:256] = values[4:8]


def finish(a, b, c, d, per_bin):
    return pl.pallas_call(
        functools.partial(finish_kernel, per_bin=per_bin),
        out_shape=[
            jax.ShapeDtypeStruct((16, 16, 32), F32),
            jax.ShapeDtypeStruct((16, 16), F32),
            jax.ShapeDtypeStruct((4, 256), F32),
        ],
        scratch_shapes=[pltpu.VMEM((256, 128), F32)],
        name="finish",
    )(a, b, c, d)


def swap(value, axis, flip):
    return lax.ppermute(value, axis, [(i, i ^ flip) for i in range(16)])


def per_device(predictions, targets, row_weight, features, leaf, sketch_matrix):
    out_at = lax.axis_index("out")
    rows_at = lax.axis_index("rows")
    where = jnp.stack([(out_at & 1) * 4 + ((out_at >> 1) & 3), rows_at * 16, rows_at * 4]).astype(jnp.int32)
    cells = predictions.shape[0]
    weight = row_weight.reshape(1, cells)
    leaf_row = leaf.reshape(1, cells)
    matrix_t = sketch_matrix.T
    args = (where, predictions, targets, weight, leaf_row, matrix_t)
    other, leaf_part = gradient_half(*args, jnp.zeros((4, 64, 128), F32), 4)
    arrived = swap(other, "out", 1)
    mine, leaf_part = gradient_half(*args, leaf_part, 0)
    chip = mine + arrived
    blocks = [chip[:, BLOCK * j : BLOCK * (j + 1)] for j in range(4)]
    far = [swap(blocks[j], "out", 2 * j) for j in (2, 1, 3)]
    part = blocks[0] + far[0] + far[1] + far[2]
    own = (part + swap(part, "out", 8)).astype(BF16)
    sketch = jnp.concatenate([own] + [swap(own, "out", 2 * j) for j in (1, 2, 3)], axis=1)
    sketch = jnp.concatenate([sketch, swap(sketch, "out", 1)], axis=1)
    slices = histogram(where, features.T, sketch, weight, leaf_part)
    slices = regroup(slices[0], *[swap(slices[j], "rows", j) for j in (1, 2, 3)])
    return tuple(
        finish(slices[0], *[swap(slices[j], "rows", 4 * j) for j in (1, 2, 3)], float(cells * 16 // BINS))
    )


def solution(mesh):
    return jax.shard_map(
        per_device,
        mesh=mesh,
        in_specs=(
            P("rows", "out"),
            P("rows", "out"),
            P("rows"),
            P("rows", "out"),
            P("rows"),
            P("out", None),
        ),
        out_specs=(P("rows", "out", None), P("rows", "out"), P("rows", "out")),
        check_vma=False,
    )
```

time: 282 us -> 92.6 us (0.33)
  blocking collectives: 139 us -> 0 us
  matrix products: 52.4 us -> 0 us
  starting transfers between devices: 0.08 us -> 26.1 us
  Pallas kernels: 0 us -> 25.6 us
  waiting for transfers between devices: 52.4 us -> 30.1 us
  between operations: 14.8 us -> 0.81 us
  other arithmetic: 7.68 us -> 0.21 us
  local copies, waits for them, and re-layouts: 13.9 us -> 8.62 us
    psum x1 -> x0, blocking collectives: 94.2 us -> none  [per_device(): sketch = lax.psum(partial_value, 'out').astype(jnp.bfloat16)]
    dot_general x11 -> x0, matrix products: 52.4 us -> none  [the longest x8 47.1 us: add_block(): jnp.einsum('rfb,rk->bfk', onehot, aug_block, preferred_element_type=jnp.f...]
    reduce_scatter x1 -> x0, waiting for transfers between devices: 52.4 us -> none  [per_device(): lax.psum_scatter(lax.fori_loop(0, block_count, add_block, jnp.zeros((BINS...]
    unnamed x1 -> x0, blocking collectives: 45.1 us -> none
    ppermute x0 -> x15, waiting for transfers between devices: none -> 30.1 us  [swap(): return lax.ppermute(value, axis, [(i, i ^ flip) for i in range(16)])]
    ppermute x0 -> x15, starting transfers between devices: none -> 26.1 us  [swap(): return lax.ppermute(value, axis, [(i, i ^ flip) for i in range(16)])]
    pallas_call x0 -> x5, Pallas kernels: none -> 25.6 us  [the longest x1 15.1 us: histogram(): pl.pallas_call(functools.partial(histogram_kernel, steps=steps), grid_spe...]
    dynamic_slice x8 -> x0, local copies, waits for them, and re-layouts: 6.8 us -> none  [add_block(): lax.dynamic_slice_in_dim(features, position * block_rows, block_rows, 0)]
  transfers between devices with their start and end apart: 2 -> 15, of which waited for: 1 -> 12; matrix products, arithmetic and copies ran while one was open for 22% -> 0% of each run, Pallas kernels for 0% -> 4%
where the time goes in v1:
time: 92.6 us; the launch traced here: 91.4 us
  waiting for transfers between devices  30.1 us (33%)
  starting transfers between devices  26.1 us (28%)
  Pallas kernels  25.6 us (28%)
  local copies, waits for them, and re-layouts  8.62 us (9%)
    ppermute x15, waiting for transfers between devices, swap(): return lax.ppermute(value, axis, [(i, i ^ flip) for i in range(16)])  30.1 us
    ppermute x15, starting transfers between devices, swap(): return lax.ppermute(value, axis, [(i, i ^ flip) for i in range(16)])  26.1 us
    pallas_call x1, Pallas kernels, histogram(): pl.pallas_call(functools.partial(histogram_kernel, steps=steps), grid_spe...  15.1 us
    unnamed x27, local copies, waits for them, and re-layouts  7.82 us
    pallas_call x2, Pallas kernels, gradient_half(): pl.pallas_call(functools.partial(gradient_kernel, steps=steps), grid_spec...  6.86 us
    pallas_call x1, Pallas kernels, regroup(): pl.pallas_call(regroup_kernel, out_shape=[jax.ShapeDtypeStruct((96, 128),...  1.98 us
  transfers between devices with their start and end apart: 15, of which 12 were waited for; matrix products, arithmetic and copies ran while one was open for 0% of the time, Pallas kernels for 4%

profile of v1, /device:TPU:6, one launch (start us, length us, event | category | flops | bytes accessed | tf_op | source)
XLA Modules:
  0.0 91.4 jit_solution(13759958272483164899)
XLA Ops:
  0.6 0.7 reshape.12.weight
  1.4 0.1 pad_add_fusion.where
  1.5 0.0 copy-start
  1.5 2.2 %copy-done = bf16[8192,256]{1,0:T(8,128)(2,1)S(1)} copy-done((bf16[8192,256]{1,0:T(8,128)(2,1)S(1)}, bf16[8192,256]{1,0:T(8,128)(2,1)}, u32[]{:S(2)}) %copy-start) | copy-done | bytes 4194328
  3.7 2.2 %copy-done.1 = bf16[8192,256]{1,0:T(8,128)(2,1)S(1)} copy-done((bf16[8192,256]{1,0:T(8,128)(2,1)S(1)}, bf16[8192,256]{1,0:T(8,128)(2,1)}, u32[]{:S(2)}) %copy-start.1) | copy-done | bytes 4194328
  5.9 0.8 copy-done.3
  6.6 0.7 copy-done.4
  7.3 3.4 %gradient.2 = (f32[32,4096]{1,0:T(8,128)S(1)}, f32[4,64,128]{2,1,0:T(8,128)S(1)}) custom-call(s32[3]{0:T(128)S(1)} %pad_add_fusion.where, bf16[8192,256]{1,0:T(8,128)(2,1)S(1)} %copy-done, bf16[8192,256]{1,0:T(8,128)(2,1)S(1)} %copy-done.1, bf16[1,8192]{1,0:T(2,128)(2,1)S(1)} %reshape.12.weight, s32[1,8192]{1,0:T(1,128)S(1)} %bitcast.6, ...), custom_call_target="tpu_custom_call" | custom-call | flops 629145600 | bytes 5000000 | tf_op jit(solution)/shard_map/gradient/pallas_call | solution.py:64
  10.8 0.1 collective-permute-start
  10.9 3.4 %gradient.3 = (f32[32,4096]{1,0:T(8,128)S(1)}, f32[4,64,128]{2,1,0:T(8,128)S(1)}) custom-call(s32[3]{0:T(128)S(1)} %pad_add_fusion.where, bf16[8192,256]{1,0:T(8,128)(2,1)S(1)} %copy-done, bf16[8192,256]{1,0:T(8,128)(2,1)S(1)} %copy-done.1, bf16[1,8192]{1,0:T(2,128)(2,1)S(1)} %reshape.12.weight, s32[1,8192]{1,0:T(1,128)S(1)} %bitcast.7, ...), custom_call_target="tpu_custom_call" | custom-call | flops 629145600 | bytes 5000000 | tf_op jit(solution)/shard_map/gradient/pallas_call | solution.py:64
  14.3 0.0 copy-start.5
  14.3 0.0 collective-permute-done
  14.3 0.1 add.19
  14.4 1.5 %collective-permute-start.1 = (f32[32,1024]{1,0:T(8,128)S(1)}, f32[32,1024]{1,0:T(8,128)S(1)}, u32[]{:S(2)}, u32[]{:S(2)}) collective-permute-start(f32[32,1024]{1,0:T(8,128)S(1)} %get-tuple-element.29), channel_id=1, source_target_pairs={{0,4},{1,5},{2,6},{3,7},{4,0},{5,1},{6,2},{7,3},{8,12},{9,13},{10,... | collective-permute-start | bytes 393224 | tf_op jit(solution)/shard_map/ppermute | solution.py:207
  15.9 2.1 %collective-permute-start.3 = (f32[32,1024]{1,0:T(8,128)S(1)}, f32[32,1024]{1,0:T(8,128)S(1)}, u32[]{:S(2)}, u32[]{:S(2)}) collective-permute-start(f32[32,1024]{1,0:T(8,128)S(1)} %get-tuple-element.30), channel_id=1, source_target_pairs={{0,6},{1,7},{2,4},{3,5},{4,2},{5,3},{6,0},{7,1},{8,14},{9,15},{10,... | collective-permute-start | bytes 393224 | tf_op jit(solution)/shard_map/ppermute | solution.py:207
  18.0 0.0 collective-permute-start.2
  18.0 4.3 %collective-permute-done.1 = f32[32,1024]{1,0:T(8,128)S(1)} collective-permute-done((f32[32,1024]{1,0:T(8,128)S(1)}, f32[32,1024]{1,0:T(8,128)S(1)}, u32[]{:S(2)}, u32[]{:S(2)}) %collective-permute-start.1) | collective-permute-done | bytes 131104 | tf_op jit(solution)/shard_map/ppermute | solution.py:207
  22.3 2.4 %collective-permute-done.3 = f32[32,1024]{1,0:T(8,128)S(1)} collective-permute-done((f32[32,1024]{1,0:T(8,128)S(1)}, f32[32,1024]{1,0:T(8,128)S(1)}, u32[]{:S(2)}, u32[]{:S(2)}) %collective-permute-start.3) | collective-permute-done | bytes 131104 | tf_op jit(solution)/shard_map/ppermute | solution.py:207
  24.7 0.0 collective-permute-done.2
  24.8 7.3 %collective-permute-start.4 = (f32[32,1024]{1,0:T(8,128)S(1)}, f32[32,1024]{1,0:T(8,128)S(1)}, u32[]{:S(2)}, u32[]{:S(2)}) collective-permute-start(f32[32,1024]{1,0:T(8,128)S(1)} %fusion.1), channel_id=1, source_target_pairs={{0,8},{1,9},{2,10},{3,11},{4,12},{5,13},{6,14},{7,15},{8,0},{9,1},... | collective-permute-start | bytes 393224 | tf_op jit(solution)/shard_map/ppermute | solution.py:207
  32.0 3.8 %collective-permute-done.4 = f32[32,1024]{1,0:T(8,128)S(1)} collective-permute-done((f32[32,1024]{1,0:T(8,128)S(1)}, f32[32,1024]{1,0:T(8,128)S(1)}, u32[]{:S(2)}, u32[]{:S(2)}) %collective-permute-start.4) | collective-permute-done | bytes 131104 | tf_op jit(solution)/shard_map/ppermute | solution.py:207
  35.9 0.8 collective-permute-start.7
  36.6 1.0 %collective-permute-start.6 = (bf16[32,1024]{1,0:T(8,128)(2,1)S(1)}, bf16[32,1024]{1,0:T(8,128)(2,1)S(1)}, u32[]{:S(2)}, u32[]{:S(2)}) collective-permute-start(bf16[32,1024]{1,0:T(8,128)(2,1)S(1)} %get-tuple-element.28), channel_id=1, source_target_pairs={{0,4},{1,5},{2,6},{3,7},{4,0},{5,1},{6,2},{7,3},{8,12},{9,13},{10,... | collective-permute-start | bytes 196616 | tf_op jit(solution)/shard_map/ppermute | solution.py:207
  37.7 2.4 %collective-permute-start.5 = (bf16[32,1024]{1,0:T(8,128)(2,1)S(1)}, bf16[32,1024]{1,0:T(8,128)(2,1)S(1)}, u32[]{:S(2)}, u32[]{:S(2)}) collective-permute-start(bf16[32,1024]{1,0:T(8,128)(2,1)S(1)} %get-tuple-element.28), channel_id=1, source_target_pairs={{0,2},{1,3},{2,0},{3,1},{4,6},{5,7},{6,4},{7,5},{8,10},{9,11},{10,... | collective-permute-start | bytes 196616 | tf_op jit(solution)/shard_map/ppermute | solution.py:207
  40.1 1.4 %collective-permute-done.7 = bf16[32,1024]{1,0:T(8,128)(2,1)S(1)} collective-permute-done((bf16[32,1024]{1,0:T(8,128)(2,1)S(1)}, bf16[32,1024]{1,0:T(8,128)(2,1)S(1)}, u32[]{:S(2)}, u32[]{:S(2)}) %collective-permute-start.7) | collective-permute-done | bytes 65568 | tf_op jit(solution)/shard_map/ppermute | solution.py:207
  41.4 1.0 %collective-permute-done.6 = bf16[32,1024]{1,0:T(8,128)(2,1)S(1)} collective-permute-done((bf16[32,1024]{1,0:T(8,128)(2,1)S(1)}, bf16[32,1024]{1,0:T(8,128)(2,1)S(1)}, u32[]{:S(2)}, u32[]{:S(2)}) %collective-permute-start.6) | collective-permute-done | bytes 65568 | tf_op jit(solution)/shard_map/ppermute | solution.py:207
  42.4 0.6 collective-permute-done.5
  43.0 0.1 collective-permute-start.8
  43.2 1.5 %collective-permute-done.8 = bf16[32,4096]{1,0:T(8,128)(2,1)S(1)} collective-permute-done((bf16[32,4096]{1,0:T(8,128)(2,1)S(1)}, bf16[32,4096]{1,0:T(8,128)(2,1)S(1)}, u32[]{:S(2)}, u32[]{:S(2)}) %collective-permute-start.8) | collective-permute-done | bytes 262176 | tf_op jit(solution)/shard_map/ppermute | solution.py:207
  44.7 15.1 %histogram.1 = (f32[336,128]{1,0:T(8,128)S(1)}, f32[336,128]{1,0:T(8,128)S(1)}, f32[336,128]{1,0:T(8,128)S(1)}, f32[336,128]{1,0:T(8,128)S(1)}) custom-call(s32[3]{0:T(128)S(1)} %pad_add_fusion.where, s32[16,8192]{1,0:T(8,128)S(1)} %bitcast.10, bf16[32,8192]{1,0:T(8,128)(2,1)S(1)} %constant_dynamic-update-slice_fusion.sketch, ...), custom_call_target="tpu_custom_call" | custom-call | flops 17179869184 | bytes 1500000 | tf_op jit(solution)/shard_map/histogram/pallas_call | solution.py:138
  59.8 0.7 copy-done.2
  60.5 1.6 %collective-permute-start.9 = (f32[336,128]{1,0:T(8,128)S(1)}, f32[336,128]{1,0:T(8,128)S(1)}, u32[]{:S(2)}, u32[]{:S(2)}) collective-permute-start(f32[336,128]{1,0:T(8,128)S(1)} %get-tuple-element.20), channel_id=1, source_target_pairs={{0,16},{16,0},{32,48},{48,32},{64,80},{80,64},{96,112},{112,96},{1... | collective-permute-start | bytes 516104 | tf_op jit(solution)/shard_map/ppermute | solution.py:207
  62.0 2.9 %collective-permute-start.10 = (f32[336,128]{1,0:T(8,128)S(1)}, f32[336,128]{1,0:T(8,128)S(1)}, u32[]{:S(2)}, u32[]{:S(2)}) collective-permute-start(f32[336,128]{1,0:T(8,128)S(1)} %get-tuple-element.21), channel_id=1, source_target_pairs={{0,32},{16,48},{32,0},{48,16},{64,96},{80,112},{96,64},{112,80},{1... | collective-permute-start | bytes 516104 | tf_op jit(solution)/shard_map/ppermute | solution.py:207
  64.9 0.2 collective-permute-start.11
  65.2 2.5 %collective-permute-done.9.b = f32[336,128]{1,0:T(8,128)S(1)} collective-permute-done((f32[336,128]{1,0:T(8,128)S(1)}, f32[336,128]{1,0:T(8,128)S(1)}, u32[]{:S(2)}, u32[]{:S(2)}) %collective-permute-start.9) | collective-permute-done | bytes 172064 | tf_op jit(solution)/shard_map/ppermute | solution.py:207
  67.7 5.4 %collective-permute-done.10.c = f32[336,128]{1,0:T(8,128)S(1)} collective-permute-done((f32[336,128]{1,0:T(8,128)S(1)}, f32[336,128]{1,0:T(8,128)S(1)}, u32[]{:S(2)}, u32[]{:S(2)}) %collective-permute-start.10) | collective-permute-done | bytes 172064 | tf_op jit(solution)/shard_map/ppermute | solution.py:207
  73.1 2.6 %collective-permute-done.11.d = f32[336,128]{1,0:T(8,128)S(1)} collective-permute-done((f32[336,128]{1,0:T(8,128)S(1)}, f32[336,128]{1,0:T(8,128)S(1)}, u32[]{:S(2)}, u32[]{:S(2)}) %collective-permute-start.11) | collective-permute-done | bytes 172064 | tf_op jit(solution)/shard_map/ppermute | solution.py:207
  75.7 0.0 copy-done.7
  75.7 0.7 copy-done.8
  76.4 2.0 %regroup.1 = (f32[96,128]{1,0:T(8,128)}, f32[96,128]{1,0:T(8,128)}, f32[96,128]{1,0:T(8,128)}, f32[96,128]{1,0:T(8,128)}) custom-call(f32[336,128]{1,0:T(8,128)} %copy-done.2, f32[336,128]{1,0:T(8,128)} %copy-done.6, f32[336,128]{1,0:T(8,128)} %copy-done.7, f32[336,128]{1,0:T(8,128)} %copy-done.8), custom_call_target="tpu_custom_call" | custom-call | tf_op jit(solution)/shard_map/regroup/pallas_call | solution.py:174
  78.3 3.8 %collective-permute-start.12 = (f32[96,128]{1,0:T(8,128)}, f32[96,128]{1,0:T(8,128)S(1)}, u32[]{:S(2)}, u32[]{:S(2)}) collective-permute-start(f32[96,128]{1,0:T(8,128)} %get-tuple-element.24), channel_id=1, source_target_pairs={{0,64},{16,80},{32,96},{48,112},{64,0},{80,16},{96,32},{112,48},{1... | collective-permute-start | bytes 147464 | tf_op jit(solution)/shard_map/ppermute | solution.py:207
  82.1 0.8 collective-permute-start.13
  83.0 1.6 %collective-permute-start.14 = (f32[96,128]{1,0:T(8,128)}, f32[96,128]{1,0:T(8,128)S(1)}, u32[]{:S(2)}, u32[]{:S(2)}) collective-permute-start(f32[96,128]{1,0:T(8,128)} %get-tuple-element.26), channel_id=1, source_target_pairs={{0,192},{16,208},{32,224},{48,240},{64,128},{80,144},{96,160},{112... | collective-permute-start | bytes 147464 | tf_op jit(solution)/shard_map/ppermute | solution.py:207
  84.5 0.0 collective-permute-done.12.b
  84.5 3.7 %collective-permute-done.13.c = f32[96,128]{1,0:T(8,128)S(1)} collective-permute-done((f32[96,128]{1,0:T(8,128)}, f32[96,128]{1,0:T(8,128)S(1)}, u32[]{:S(2)}, u32[]{:S(2)}) %collective-permute-start.13) | collective-permute-done | bytes 49184 | tf_op jit(solution)/shard_map/ppermute | solution.py:207
  88.2 1.0 %collective-permute-done.14.d = f32[96,128]{1,0:T(8,128)S(1)} collective-permute-done((f32[96,128]{1,0:T(8,128)}, f32[96,128]{1,0:T(8,128)S(1)}, u32[]{:S(2)}, u32[]{:S(2)}) %collective-permute-start.14) | collective-permute-done | bytes 49184 | tf_op jit(solution)/shard_map/ppermute | solution.py:207
  89.2 0.6 copy-done.11
  89.8 1.6 %finish.1 = (f32[16,16,32]{2,1,0:T(8,128)}, f32[16,16]{1,0:T(8,128)}, f32[4,256]{1,0:T(4,128)}) custom-call(f32[96,128]{1,0:T(8,128)} %get-tuple-element.23.a, f32[96,128]{1,0:T(8,128)} %copy-done.9, f32[96,128]{1,0:T(8,128)} %copy-done.10, f32[96,128]{1,0:T(8,128)} %copy-done.11), custom_call_target="tpu_custom_call" | custom-call | tf_op jit(solution)/shard_map/finish/pallas_call | solution.py:194
  (23 shorter events, 0.2 us)
Async XLA Ops:
  1.5 2.2 %copy-start = (bf16[8192,256]{1,0:T(8,128)(2,1)S(1)}, bf16[8192,256]{1,0:T(8,128)(2,1)}, u32[]{:S(2)}) copy-start(bf16[8192,256]{1,0:T(8,128)(2,1)} %pred_.3) | copy-start | bytes 12582916
  3.7 2.2 %copy-start.1 = (bf16[8192,256]{1,0:T(8,128)(2,1)S(1)}, bf16[8192,256]{1,0:T(8,128)(2,1)}, u32[]{:S(2)}) copy-start(bf16[8192,256]{1,0:T(8,128)(2,1)} %targ.3) | copy-start | bytes 12582916
  5.9 0.8 copy-start.3
  6.6 0.7 copy-start.4
  10.8 3.6 %collective-permute-start = (f32[32,4096]{1,0:T(8,128)S(1)}, f32[32,4096]{1,0:T(8,128)S(1)}, u32[]{:S(2)}, u32[]{:S(2)}) collective-permute-start(f32[32,4096]{1,0:T(8,128)S(1)} %get-tuple-element.17), channel_id=1, source_target_pairs={{0,1},{1,0},{2,3},{3,2},{4,5},{5,4},{6,7},{7,6},{8,9},{9,8},{10,11... | collective-permute-start | bytes 1572872 | tf_op jit(solution)/shard_map/ppermute | solution.py:207
  14.3 30.4 %copy-start.5 = (s32[8192,16]{0,1:T(8,128)S(1)}, s32[8192,16]{0,1:T(8,128)}, u32[]{:S(2)}) copy-start(s32[8192,16]{0,1:T(8,128)} %param.9) | copy-start | bytes 1572868
  14.4 7.9 %collective-permute-start.1 = (f32[32,1024]{1,0:T(8,128)S(1)}, f32[32,1024]{1,0:T(8,128)S(1)}, u32[]{:S(2)}, u32[]{:S(2)}) collective-permute-start(f32[32,1024]{1,0:T(8,128)S(1)} %get-tuple-element.29), channel_id=1, source_target_pairs={{0,4},{1,5},{2,6},{3,7},{4,0},{5,1},{6,2},{7,3},{8,12},{9,13},{10,... | collective-permute-start | bytes 393224 | tf_op jit(solution)/shard_map/ppermute | solution.py:207
  15.9 8.8 %collective-permute-start.3 = (f32[32,1024]{1,0:T(8,128)S(1)}, f32[32,1024]{1,0:T(8,128)S(1)}, u32[]{:S(2)}, u32[]{:S(2)}) collective-permute-start(f32[32,1024]{1,0:T(8,128)S(1)} %get-tuple-element.30), channel_id=1, source_target_pairs={{0,6},{1,7},{2,4},{3,5},{4,2},{5,3},{6,0},{7,1},{8,14},{9,15},{10,... | collective-permute-start | bytes 393224 | tf_op jit(solution)/shard_map/ppermute | solution.py:207
  18.0 6.7 %collective-permute-start.2 = (f32[32,1024]{1,0:T(8,128)S(1)}, f32[32,1024]{1,0:T(8,128)S(1)}, u32[]{:S(2)}, u32[]{:S(2)}) collective-permute-start(f32[32,1024]{1,0:T(8,128)S(1)} %get-tuple-element.31), channel_id=1, source_target_pairs={{0,2},{1,3},{2,0},{3,1},{4,6},{5,7},{6,4},{7,5},{8,10},{9,11},{10,... | collective-permute-start | bytes 393224 | tf_op jit(solution)/shard_map/ppermute | solution.py:207
  24.8 11.1 %collective-permute-start.4 = (f32[32,1024]{1,0:T(8,128)S(1)}, f32[32,1024]{1,0:T(8,128)S(1)}, u32[]{:S(2)}, u32[]{:S(2)}) collective-permute-start(f32[32,1024]{1,0:T(8,128)S(1)} %fusion.1), channel_id=1, source_target_pairs={{0,8},{1,9},{2,10},{3,11},{4,12},{5,13},{6,14},{7,15},{8,0},{9,1},... | collective-permute-start | bytes 393224 | tf_op jit(solution)/shard_map/ppermute | solution.py:207
  35.9 5.6 %collective-permute-start.7 = (bf16[32,1024]{1,0:T(8,128)(2,1)S(1)}, bf16[32,1024]{1,0:T(8,128)(2,1)S(1)}, u32[]{:S(2)}, u32[]{:S(2)}) collective-permute-start(bf16[32,1024]{1,0:T(8,128)(2,1)S(1)} %get-tuple-element.28), channel_id=1, source_target_pairs={{0,6},{1,7},{2,4},{3,5},{4,2},{5,3},{6,0},{7,1},{8,14},{9,15},{10,... | collective-permute-start | bytes 196616 | tf_op jit(solution)/shard_map/ppermute | solution.py:207
  36.6 5.8 %collective-permute-start.6 = (bf16[32,1024]{1,0:T(8,128)(2,1)S(1)}, bf16[32,1024]{1,0:T(8,128)(2,1)S(1)}, u32[]{:S(2)}, u32[]{:S(2)}) collective-permute-start(bf16[32,1024]{1,0:T(8,128)(2,1)S(1)} %get-tuple-element.28), channel_id=1, source_target_pairs={{0,4},{1,5},{2,6},{3,7},{4,0},{5,1},{6,2},{7,3},{8,12},{9,13},{10,... | collective-permute-start | bytes 196616 | tf_op jit(solution)/shard_map/ppermute | solution.py:207
  37.7 5.3 %collective-permute-start.5 = (bf16[32,1024]{1,0:T(8,128)(2,1)S(1)}, bf16[32,1024]{1,0:T(8,128)(2,1)S(1)}, u32[]{:S(2)}, u32[]{:S(2)}) collective-permute-start(bf16[32,1024]{1,0:T(8,128)(2,1)S(1)} %get-tuple-element.28), channel_id=1, source_target_pairs={{0,2},{1,3},{2,0},{3,1},{4,6},{5,7},{6,4},{7,5},{8,10},{9,11},{10,... | collective-permute-start | bytes 196616 | tf_op jit(solution)/shard_map/ppermute | solution.py:207
  43.0 1.6 %collective-permute-start.8 = (bf16[32,4096]{1,0:T(8,128)(2,1)S(1)}, bf16[32,4096]{1,0:T(8,128)(2,1)S(1)}, u32[]{:S(2)}, u32[]{:S(2)}) collective-permute-start(bf16[32,4096]{1,0:T(8,128)(2,1)S(1)} %pad_maximum_fusion), channel_id=1, source_target_pairs={{0,1},{1,0},{2,3},{3,2},{4,5},{5,4},{6,7},{7,6},{8,9},{9,8},{10,11... | collective-permute-start | bytes 786440 | tf_op jit(solution)/shard_map/ppermute | solution.py:207
  59.8 0.7 copy-start.2
  60.5 7.2 %collective-permute-start.9 = (f32[336,128]{1,0:T(8,128)S(1)}, f32[336,128]{1,0:T(8,128)S(1)}, u32[]{:S(2)}, u32[]{:S(2)}) collective-permute-start(f32[336,128]{1,0:T(8,128)S(1)} %get-tuple-element.20), channel_id=1, source_target_pairs={{0,16},{16,0},{32,48},{48,32},{64,80},{80,64},{96,112},{112,96},{1... | collective-permute-start | bytes 516104 | tf_op jit(solution)/shard_map/ppermute | solution.py:207
  62.0 11.1 %collective-permute-start.10 = (f32[336,128]{1,0:T(8,128)S(1)}, f32[336,128]{1,0:T(8,128)S(1)}, u32[]{:S(2)}, u32[]{:S(2)}) collective-permute-start(f32[336,128]{1,0:T(8,128)S(1)} %get-tuple-element.21), channel_id=1, source_target_pairs={{0,32},{16,48},{32,0},{48,16},{64,96},{80,112},{96,64},{112,80},{1... | collective-permute-start | bytes 516104 | tf_op jit(solution)/shard_map/ppermute | solution.py:207
  64.9 10.8 %collective-permute-start.11 = (f32[336,128]{1,0:T(8,128)S(1)}, f32[336,128]{1,0:T(8,128)S(1)}, u32[]{:S(2)}, u32[]{:S(2)}) collective-permute-start(f32[336,128]{1,0:T(8,128)S(1)} %get-tuple-element.22), channel_id=1, source_target_pairs={{0,48},{16,32},{32,16},{48,0},{64,112},{80,96},{96,80},{112,64},{1... | collective-permute-start | bytes 516104 | tf_op jit(solution)/shard_map/ppermute | solution.py:207
  67.7 8.0 %copy-start.6 = (f32[336,128]{1,0:T(8,128)}, f32[336,128]{1,0:T(8,128)S(1)}, u32[]{:S(2)}) copy-start(f32[336,128]{1,0:T(8,128)S(1)} %collective-permute-done.9.b) | copy-start | bytes 516100
  73.1 2.6 %copy-start.7 = (f32[336,128]{1,0:T(8,128)}, f32[336,128]{1,0:T(8,128)S(1)}, u32[]{:S(2)}) copy-start(f32[336,128]{1,0:T(8,128)S(1)} %collective-permute-done.10.c) | copy-start | bytes 516100
  75.7 0.7 copy-start.8
  78.3 6.2 %collective-permute-start.12 = (f32[96,128]{1,0:T(8,128)}, f32[96,128]{1,0:T(8,128)S(1)}, u32[]{:S(2)}, u32[]{:S(2)}) collective-permute-start(f32[96,128]{1,0:T(8,128)} %get-tuple-element.24), channel_id=1, source_target_pairs={{0,64},{16,80},{32,96},{48,112},{64,0},{80,16},{96,32},{112,48},{1... | collective-permute-start | bytes 147464 | tf_op jit(solution)/shard_map/ppermute | solution.py:207
  82.1 6.1 %collective-permute-start.13 = (f32[96,128]{1,0:T(8,128)}, f32[96,128]{1,0:T(8,128)S(1)}, u32[]{:S(2)}, u32[]{:S(2)}) collective-permute-start(f32[96,128]{1,0:T(8,128)} %get-tuple-element.25), channel_id=1, source_target_pairs={{0,128},{16,144},{32,160},{48,176},{64,192},{80,208},{96,224},{112... | collective-permute-start | bytes 147464 | tf_op jit(solution)/shard_map/ppermute | solution.py:207
  83.0 6.2 %collective-permute-start.14 = (f32[96,128]{1,0:T(8,128)}, f32[96,128]{1,0:T(8,128)S(1)}, u32[]{:S(2)}, u32[]{:S(2)}) collective-permute-start(f32[96,128]{1,0:T(8,128)} %get-tuple-element.26), channel_id=1, source_target_pairs={{0,192},{16,208},{32,224},{48,240},{64,128},{80,144},{96,160},{112... | collective-permute-start | bytes 147464 | tf_op jit(solution)/shard_map/ppermute | solution.py:207
  84.5 4.7 %copy-start.9 = (f32[96,128]{1,0:T(8,128)}, f32[96,128]{1,0:T(8,128)S(1)}, u32[]{:S(2)}) copy-start(f32[96,128]{1,0:T(8,128)S(1)} %collective-permute-done.12.b) | copy-start | bytes 147460
  88.2 1.0 %copy-start.10 = (f32[96,128]{1,0:T(8,128)}, f32[96,128]{1,0:T(8,128)S(1)}, u32[]{:S(2)}) copy-start(f32[96,128]{1,0:T(8,128)S(1)} %collective-permute-done.13.c) | copy-start | bytes 147460
  89.2 0.6 copy-start.11

commit v2 on v0

v2 whole, which is shorter than its diff:
```python
import functools

import jax
import jax.numpy as jnp
from jax import lax
from jax.experimental import pallas as pl
from jax.experimental.pallas import tpu as pltpu
from jax.sharding import PartitionSpec as P

BINS = 256
LEAVES = 64
RIDGE = 1.0
F32 = jnp.float32
BF16 = jnp.bfloat16
BLOCK = 1024
CONTRACT_LAST = (((1,), (1,)), ((), ()))


def own_block():
    out_at = lax.axis_index("out")
    return (out_at & 1) * 4 + ((out_at >> 1) & 3)


def lanes_of(block):
    return pl.ds(pl.multiple_of(block * BLOCK, BLOCK), BLOCK)


def gradient_kernel(*refs, first, parts):
    pred, targ, weight, leaf, matrix_t = refs[:5]
    leaf_in = refs[5] if len(refs) == 13 else None
    sketch_out, leaf_out, pred_here, targ_here, sums, weights = refs[-7:-1]
    arrived = refs[-1]
    me = own_block()
    leaf_flip = lax.axis_index("rows") * 4
    size = BLOCK // parts
    copies = []
    for j in range(4):
        for part in range(parts):
            n = j * parts + part
            rows = pl.ds(pl.multiple_of(((j + first) ^ me) * BLOCK + part * size, size), size)
            pair = [
                pltpu.make_async_copy(pred.at[rows, :], pred_here.at[n], arrived.at[0, n]),
                pltpu.make_async_copy(targ.at[rows, :], targ_here.at[n], arrived.at[1, n]),
            ]
            for copy in pair:
                copy.start()
            copies.append(pair)
    for j in range(4):
        w_wide = weight[:, lanes_of((j + first) ^ me)]
        own = leaf[:, lanes_of((j + first) ^ me)] ^ leaf_flip
        place = ((own >> 2) & 3) * 16 + (own >> 4) * 4 + (own & 3)
        onehot = jnp.where(lax.broadcasted_iota(jnp.int32, (LEAVES, BLOCK), 0) == place, 1.0, 0.0).astype(BF16)
        w_cols = jnp.transpose(
            jnp.concatenate([w_wide[:, 128 * s : 128 * s + 128] for s in range(BLOCK // 128)], axis=0)
        )
        added = None
        for part in range(parts):
            n = j * parts + part
            for copy in copies[n]:
                copy.wait()
            pieces = []
            for s in range(size // 128):
                rows = slice(128 * s, 128 * s + 128)
                diff = pred_here[n, rows, :].astype(F32) - targ_here[n, rows, :].astype(F32)
                at = part * (size // 128) + s
                pieces.append((w_cols[:, at : at + 1] * diff).astype(BF16))
            gradient = jnp.concatenate(pieces, axis=0)
            sketch_out[:, n * size : n * size + size] = lax.dot_general(
                matrix_t[...], gradient, CONTRACT_LAST, preferred_element_type=F32
            )
            piece = jnp.dot(onehot[:, part * size : part * size + size], gradient, preferred_element_type=F32)
            added = piece if added is None else added + piece
        w_rows = jnp.broadcast_to(w_wide.astype(BF16), (16, BLOCK))
        w_added = lax.dot_general(onehot, w_rows, CONTRACT_LAST, preferred_element_type=F32)
        if j == 0:
            sums[...] = added
            weights[...] = w_added
        else:
            sums[...] += added
            weights[...] += w_added
    for y in range(4):
        for z in range(4):
            top = 16 * y + 4 * z
            pieces = [sums[top : top + 4, 0:128], sums[top : top + 4, 128:256]]
            pieces += [jnp.broadcast_to(weights[top : top + 4, 0:1], (4, 128))] * 2
            for value, at in zip(pieces, (8 * z, 8 * z + 4, 32 + 8 * z, 36 + 8 * z)):
                leaf_out[y, at : at + 4, :] = value if leaf_in is None else value + leaf_in[y, at : at + 4, :]


def gradient_half(pred, targ, weight, leaf, matrix_t, leaf_in, first):
    genes = pred.shape[1]
    half = pred.shape[0] // 2
    parts = 2
    given = [pred, targ, weight, leaf, matrix_t] + ([] if leaf_in is None else [leaf_in])
    whole = pl.BlockSpec(memory_space=pltpu.VMEM)
    return pl.pallas_call(
        functools.partial(gradient_kernel, first=first, parts=parts),
        in_specs=[pl.BlockSpec(memory_space=pltpu.HBM)] * 2 + [whole] * (len(given) - 2),
        out_specs=[whole, whole],
        scratch_shapes=[
            pltpu.VMEM((4 * parts, BLOCK // parts, genes), BF16),
            pltpu.VMEM((4 * parts, BLOCK // parts, genes), BF16),
            pltpu.VMEM((LEAVES, genes), F32),
            pltpu.VMEM((LEAVES, 16), F32),
            pltpu.SemaphoreType.DMA((2, 4 * parts)),
        ],
        out_shape=[
            jax.ShapeDtypeStruct((matrix_t.shape[0], half), F32),
            jax.ShapeDtypeStruct((4, 64, 128), F32),
        ],
        compiler_params=pltpu.CompilerParams(vmem_limit_bytes=61 * 1024 * 1024),
        cost_estimate=pl.CostEstimate(flops=2 * half * 256 * 300, bytes_accessed=5000000, transcendentals=0),
        name="gradient",
    )(*given)


def histogram_kernel(feat, sketch, weight, leaf_part, o0, o1, o2, o3, held, hess, *, steps):
    step = pl.program_id(0)
    outs = (o0, o1, o2, o3)
    wide = sketch.shape[1]
    blocks = wide // BLOCK
    me = own_block()
    bin_flip = lax.axis_index("rows") * 16

    @pl.when(step == 0)
    def _():
        held[...] = jnp.zeros_like(held)
        hess[...] = jnp.zeros_like(hess)

    places = [lanes_of((step * blocks + b) ^ me) for b in range(blocks)]
    sketch_all = sketch[...]
    w_row = jnp.concatenate([weight[:, place] for place in places], axis=1)
    w_all = jnp.broadcast_to(w_row.astype(BF16), (16, wide))
    rows128 = lax.broadcasted_iota(jnp.int32, (128, wide), 0).astype(BF16)
    rows16 = lax.broadcasted_iota(jnp.int32, (16, wide), 0).astype(BF16)
    zero = jnp.zeros((), BF16)
    one = jnp.ones((), BF16)
    for f in range(16):
        own = jnp.concatenate([feat[f : f + 1, place] for place in places], axis=1) ^ bin_flip
        low = (own & 127).astype(F32).astype(BF16)
        top = own >> 7
        group = jnp.broadcast_to(top.astype(F32).astype(BF16), (32, wide))
        left = jnp.where(rows128 == low, one, zero)
        spot = (top * 8 + (f % 8)).astype(F32).astype(BF16)
        right = jnp.concatenate(
            [
                jnp.where(group == zero, sketch_all, zero),
                jnp.where(group == zero, zero, sketch_all),
                jnp.where(rows16 == spot, w_all, zero),
            ],
            axis=0,
        )
        both = lax.dot_general(left, right, CONTRACT_LAST, preferred_element_type=F32)
        held[f] += both[:, 0:64]
        hess[f // 8] += both[:, 64:80]

    @pl.when(step == steps - 1)
    def _():
        for y in range(4):
            near, far = slice(16 * y, 16 * y + 16), slice(64 + 16 * y, 80 + 16 * y)
            for f in range(16):
                outs[y][16 * f : 16 * f + 16, :] = jnp.concatenate([held[f, near, :], held[f, far, :]], axis=1)
            lanes = [
                hess[g, (far if z & 1 else near), 8 * (z >> 1) : 8 * (z >> 1) + 8] for z in range(4) for g in range(2)
            ]
            outs[y][256:272, :] = jnp.concatenate(lanes + [jnp.zeros((16, 64), F32)], axis=1)
            outs[y][272:336, :] = leaf_part[y]


def histogram(feat_t, sketch, weight, leaf_part):
    cells = feat_t.shape[1]
    wide = 2 * BLOCK
    steps = cells // wide
    whole = pl.BlockSpec(memory_space=pltpu.VMEM)
    return pl.pallas_call(
        functools.partial(histogram_kernel, steps=steps),
        grid=(steps,),
        in_specs=[whole, pl.BlockSpec((32, wide), lambda j: (0, j)), whole, whole],
        out_specs=[whole] * 4,
        scratch_shapes=[pltpu.VMEM((16, 128, 64), F32), pltpu.VMEM((2, 128, 16), F32)],
        out_shape=[jax.ShapeDtypeStruct((336, 128), F32)] * 4,
        compiler_params=pltpu.CompilerParams(vmem_limit_bytes=24 * 1024 * 1024),
        cost_estimate=pl.CostEstimate(flops=2 * 8192 * 4096 * 256, bytes_accessed=1500000, transcendentals=0),
        name="histogram",
    )(feat_t, sketch, weight, leaf_part)


def regroup_kernel(a, b, c, d, o0, o1, o2, o3):
    outs = (o0, o1, o2, o3)
    total = a[...] + b[...] + c[...] + d[...]
    for z in range(4):
        lane = 64 * (z & 1) + 32 * (z >> 1)
        outs[z][0:64, :] = jnp.concatenate(
            [total[64 * q : 64 * q + 64, lane : lane + 32] for q in range(4)], axis=1
        )
        outs[z][64:80, :] = jnp.concatenate(
            [total[256:272, 16 * z : 16 * z + 16], jnp.zeros((16, 112), F32)], axis=1
        )
        outs[z][80:88, :] = total[272 + 8 * z : 280 + 8 * z, :]
        outs[z][88:96, :] = total[304 + 8 * z : 312 + 8 * z, :]


def regroup(a, b, c, d):
    return pl.pallas_call(
        regroup_kernel,
        out_shape=[jax.ShapeDtypeStruct((96, 128), F32)] * 4,
        compiler_params=pltpu.CompilerParams(vmem_limit_bytes=8 * 1024 * 1024),
        name="regroup",
    )(a, b, c, d)


def finish_kernel(a, b, c, d, grad_out, hess_out, leaf_out, rows, *, per_bin):
    total = a[...] + b[...] + c[...] + d[...]
    for q in range(4):
        rows[64 * q : 64 * q + 64, 0:32] = total[0:64, 32 * q : 32 * q + 32]
    for i in range(16):
        grad_out[i] = rows[pl.ds(i, 16, stride=16), :][:, 0:32]
    hess_out[...] = total[64:80, 0:16] / per_bin
    values = -total[80:88, :] / (total[88:96, :] + RIDGE)
    leaf_out[:, 0:128] = values[0:4]
    leaf_out[:, 128:256] = values[4:8]


def finish(a, b, c, d, per_bin):
    return pl.pallas_call(
        functools.partial(finish_kernel, per_bin=per_bin),
        out_shape=[
            jax.ShapeDtypeStruct((16, 16, 32), F32),
            jax.ShapeDtypeStruct((16, 16), F32),
            jax.ShapeDtypeStruct((4, 256), F32),
        ],
        scratch_shapes=[pltpu.VMEM((256, 128), F32)],
        compiler_params=pltpu.CompilerParams(vmem_limit_bytes=8 * 1024 * 1024),
        name="finish",
    )(a, b, c, d)


def swap(value, axis, flip):
    return lax.ppermute(value, axis, [(i, i ^ flip) for i in range(16)])


def per_device(predictions, targets, row_weight, features, leaf, sketch_matrix):
    cells = predictions.shape[0]
    weight = row_weight.astype(F32).reshape(1, cells)
    args = (predictions, targets, weight, leaf.reshape(1, cells), sketch_matrix.T)
    other, leaf_part = gradient_half(*args, None, 4)
    arrived = swap(other, "out", 1)
    mine, leaf_part = gradient_half(*args, leaf_part, 0)
    chip = mine + arrived
    blocks = [chip[:, BLOCK * j : BLOCK * (j + 1)] for j in range(4)]
    far = [swap(blocks[j], "out", 2 * j) for j in (2, 1, 3)]
    part = blocks[0] + far[0] + far[1] + far[2]
    own = (part + swap(part, "out", 8)).astype(BF16)
    sketch = jnp.concatenate([own] + [swap(own, "out", 2 * j) for j in (1, 2, 3)], axis=1)
    sketch = jnp.concatenate([sketch, swap(sketch, "out", 1)], axis=1)
    slices = histogram(features.T, sketch, weight, leaf_part)
    slices = regroup(slices[0], *[swap(slices[j], "rows", j) for j in (1, 2, 3)])
    return tuple(
        finish(slices[0], *[swap(slices[j], "rows", 4 * j) for j in (1, 2, 3)], float(cells * 16 // BINS))
    )


def solution(mesh):
    return jax.shard_map(
        per_device,
        mesh=mesh,
        in_specs=(
            P("rows", "out"),
            P("rows", "out"),
            P("rows"),
            P("rows", "out"),
            P("rows"),
            P("out", None),
        ),
        out_specs=(P("rows", "out", None), P("rows", "out"), P("rows", "out")),
        check_vma=False,
    )
```

time: 282 us -> 83.4 us (0.30)
  blocking collectives: 139 us -> 0 us
  matrix products: 52.4 us -> 0 us
  starting transfers between devices: 0.08 us -> 26.5 us
  Pallas kernels: 0 us -> 22.5 us
  waiting for transfers between devices: 52.4 us -> 29.9 us
  between operations: 14.8 us -> 0.79 us
  local copies, waits for them, and re-layouts: 13.9 us -> 0.08 us
  other arithmetic: 7.68 us -> 2.54 us
    psum x1 -> x0, blocking collectives: 94.2 us -> none  [per_device(): sketch = lax.psum(partial_value, 'out').astype(jnp.bfloat16)]
    dot_general x11 -> x0, matrix products: 52.4 us -> none  [the longest x8 47.1 us: add_block(): jnp.einsum('rfb,rk->bfk', onehot, aug_block, preferred_element_type=jnp.f...]
    reduce_scatter x1 -> x0, waiting for transfers between devices: 52.4 us -> none  [per_device(): lax.psum_scatter(lax.fori_loop(0, block_count, add_block, jnp.zeros((BINS...]
    unnamed x1 -> x0, blocking collectives: 45.1 us -> none
    ppermute x0 -> x15, waiting for transfers between devices: none -> 29.9 us  [swap(): return lax.ppermute(value, axis, [(i, i ^ flip) for i in range(16)])]
    ppermute x0 -> x15, starting transfers between devices: none -> 26.5 us  [swap(): return lax.ppermute(value, axis, [(i, i ^ flip) for i in range(16)])]
    pallas_call x0 -> x5, Pallas kernels: none -> 22.5 us  [the longest x2 11.1 us: gradient_half(): pl.pallas_call(functools.partial(gradient_kernel, first=first, parts=part...]
    dynamic_slice x8 -> x0, local copies, waits for them, and re-layouts: 6.8 us -> none  [add_block(): lax.dynamic_slice_in_dim(features, position * block_rows, block_rows, 0)]
  transfers between devices with their start and end apart: 2 -> 15, of which waited for: 1 -> 12; matrix products, arithmetic and copies ran while one was open for 22% -> 0% of each run, Pallas kernels for 0% -> 7%
where the time goes in v2:
time: 83.4 us; the launch traced here: 82.3 us
  waiting for transfers between devices  29.9 us (36%)
  starting transfers between devices  26.5 us (32%)
  Pallas kernels  22.5 us (27%)
  other arithmetic  2.54 us (3%)
    ppermute x15, waiting for transfers between devices, swap(): return lax.ppermute(value, axis, [(i, i ^ flip) for i in range(16)])  29.9 us
    ppermute x15, starting transfers between devices, swap(): return lax.ppermute(value, axis, [(i, i ^ flip) for i in range(16)])  26.5 us
    pallas_call x2, Pallas kernels, gradient_half(): pl.pallas_call(functools.partial(gradient_kernel, first=first, parts=part...  11.1 us
    pallas_call x1, Pallas kernels, histogram(): pl.pallas_call(functools.partial(histogram_kernel, steps=steps), grid=(st...  10.5 us
  transfers between devices with their start and end apart: 15, of which 12 were waited for; matrix products, arithmetic and copies ran while one was open for 0% of the time, Pallas kernels for 7%

profile of v2, /device:TPU:6, one launch (start us, length us, event | category | flops | bytes accessed | tf_op | source)
XLA Modules:
  0.0 82.3 jit_solution(12259865996454573125)
XLA Ops:
  0.6 1.3 %reshape.17 = f32[8192]{0:T(1024)} convert(bf16[8192]{0:T(1024)(128)(2,1)} %param.8) | non-fusion elementwise | flops 8192 | bytes 49152 | tf_op jit(solution)/shard_map/reshape | solution.py:244
  1.9 5.4 %gradient.2 = (f32[32,4096]{1,0:T(8,128)}, f32[4,64,128]{2,1,0:T(8,128)}) custom-call(bf16[8192,256]{1,0:T(8,128)(2,1)} %refs_0_.3, bf16[8192,256]{1,0:T(8,128)(2,1)} %refs_1_.3, f32[1,8192]{1,0:T(1,128)} %bitcast.4, s32[1,8192]{1,0:T(1,128)} %bitcast.8, bf16[32,256]{1,0:T(8,128)(2,1)} %bitcast.10), custom_call_target="tpu_custom_call" | custom-call | flops 629145600 | bytes 5000000 | tf_op jit(solution)/shard_map/gradient/pallas_call | solution.py:96
  7.4 0.1 collective-permute-start
  7.5 5.6 %gradient.3 = (f32[32,4096]{1,0:T(8,128)}, f32[4,64,128]{2,1,0:T(8,128)}) custom-call(bf16[8192,256]{1,0:T(8,128)(2,1)} %refs_0_.3, bf16[8192,256]{1,0:T(8,128)(2,1)} %refs_1_.3, f32[1,8192]{1,0:T(1,128)} %bitcast.5, s32[1,8192]{1,0:T(1,128)} %bitcast.9, bf16[32,256]{1,0:T(8,128)(2,1)} %bitcast.11, f32[4,64,128]{2,1,0:T(8,128)} %get-tuple-element.15.refs_5_), custom_call_target="tpu_custom_call" | custom-call | flops 629145600 | bytes 5000000 | tf_op jit(solution)/shard_map/gradient/pallas_call | solution.py:96
  13.1 0.0 copy-start
  13.1 0.0 copy-start.1
  13.1 0.0 copy-start.2
  13.2 0.0 collective-permute-done
  13.2 1.2 %add.15 = f32[32,4096]{1,0:T(8,128)S(1)} add(f32[32,4096]{1,0:T(8,128)} %get-tuple-element.16, f32[32,4096]{1,0:T(8,128)S(1)} %collective-permute-done) | non-fusion elementwise | flops 131072 | bytes 1572864 | tf_op jit(solution)/shard_map/add | solution.py:249
  14.4 1.5 %collective-permute-start.1 = (f32[32,1024]{1,0:T(8,128)S(1)}, f32[32,1024]{1,0:T(8,128)S(1)}, u32[]{:S(2)}, u32[]{:S(2)}) collective-permute-start(f32[32,1024]{1,0:T(8,128)S(1)} %get-tuple-element.29), channel_id=1, source_target_pairs={{0,4},{1,5},{2,6},{3,7},{4,0},{5,1},{6,2},{7,3},{8,12},{9,13},{10,... | collective-permute-start | bytes 393224 | tf_op jit(solution)/shard_map/ppermute | solution.py:239
  15.9 2.1 %collective-permute-start.3 = (f32[32,1024]{1,0:T(8,128)S(1)}, f32[32,1024]{1,0:T(8,128)S(1)}, u32[]{:S(2)}, u32[]{:S(2)}) collective-permute-start(f32[32,1024]{1,0:T(8,128)S(1)} %get-tuple-element.30), channel_id=1, source_target_pairs={{0,6},{1,7},{2,4},{3,5},{4,2},{5,3},{6,0},{7,1},{8,14},{9,15},{10,... | collective-permute-start | bytes 393224 | tf_op jit(solution)/shard_map/ppermute | solution.py:239
  17.9 0.0 collective-permute-start.2
  18.0 4.3 %collective-permute-done.1 = f32[32,1024]{1,0:T(8,128)S(1)} collective-permute-done((f32[32,1024]{1,0:T(8,128)S(1)}, f32[32,1024]{1,0:T(8,128)S(1)}, u32[]{:S(2)}, u32[]{:S(2)}) %collective-permute-start.1) | collective-permute-done | bytes 131104 | tf_op jit(solution)/shard_map/ppermute | solution.py:239
  22.3 2.4 %collective-permute-done.3 = f32[32,1024]{1,0:T(8,128)S(1)} collective-permute-done((f32[32,1024]{1,0:T(8,128)S(1)}, f32[32,1024]{1,0:T(8,128)S(1)}, u32[]{:S(2)}, u32[]{:S(2)}) %collective-permute-start.3) | collective-permute-done | bytes 131104 | tf_op jit(solution)/shard_map/ppermute | solution.py:239
  24.7 0.0 collective-permute-done.2
  24.7 7.3 %collective-permute-start.4 = (f32[32,1024]{1,0:T(8,128)S(1)}, f32[32,1024]{1,0:T(8,128)S(1)}, u32[]{:S(2)}, u32[]{:S(2)}) collective-permute-start(f32[32,1024]{1,0:T(8,128)S(1)} %fusion.1), channel_id=1, source_target_pairs={{0,8},{1,9},{2,10},{3,11},{4,12},{5,13},{6,14},{7,15},{8,0},{9,1},... | collective-permute-start | bytes 393224 | tf_op jit(solution)/shard_map/ppermute | solution.py:239
  32.0 3.8 %collective-permute-done.4 = f32[32,1024]{1,0:T(8,128)S(1)} collective-permute-done((f32[32,1024]{1,0:T(8,128)S(1)}, f32[32,1024]{1,0:T(8,128)S(1)}, u32[]{:S(2)}, u32[]{:S(2)}) %collective-permute-start.4) | collective-permute-done | bytes 131104 | tf_op jit(solution)/shard_map/ppermute | solution.py:239
  35.8 0.8 collective-permute-start.7
  36.6 1.0 %collective-permute-start.6 = (bf16[32,1024]{1,0:T(8,128)(2,1)S(1)}, bf16[32,1024]{1,0:T(8,128)(2,1)S(1)}, u32[]{:S(2)}, u32[]{:S(2)}) collective-permute-start(bf16[32,1024]{1,0:T(8,128)(2,1)S(1)} %get-tuple-element.28), channel_id=1, source_target_pairs={{0,4},{1,5},{2,6},{3,7},{4,0},{5,1},{6,2},{7,3},{8,12},{9,13},{10,... | collective-permute-start | bytes 196616 | tf_op jit(solution)/shard_map/ppermute | solution.py:239
  37.6 2.4 %collective-permute-start.5 = (bf16[32,1024]{1,0:T(8,128)(2,1)S(1)}, bf16[32,1024]{1,0:T(8,128)(2,1)S(1)}, u32[]{:S(2)}, u32[]{:S(2)}) collective-permute-start(bf16[32,1024]{1,0:T(8,128)(2,1)S(1)} %get-tuple-element.28), channel_id=1, source_target_pairs={{0,2},{1,3},{2,0},{3,1},{4,6},{5,7},{6,4},{7,5},{8,10},{9,11},{10,... | collective-permute-start | bytes 196616 | tf_op jit(solution)/shard_map/ppermute | solution.py:239
  40.0 1.4 %collective-permute-done.7 = bf16[32,1024]{1,0:T(8,128)(2,1)S(1)} collective-permute-done((bf16[32,1024]{1,0:T(8,128)(2,1)S(1)}, bf16[32,1024]{1,0:T(8,128)(2,1)S(1)}, u32[]{:S(2)}, u32[]{:S(2)}) %collective-permute-start.7) | collective-permute-done | bytes 65568 | tf_op jit(solution)/shard_map/ppermute | solution.py:239
  41.4 1.0 %collective-permute-done.6 = bf16[32,1024]{1,0:T(8,128)(2,1)S(1)} collective-permute-done((bf16[32,1024]{1,0:T(8,128)(2,1)S(1)}, bf16[32,1024]{1,0:T(8,128)(2,1)S(1)}, u32[]{:S(2)}, u32[]{:S(2)}) %collective-permute-start.6) | collective-permute-done | bytes 65568 | tf_op jit(solution)/shard_map/ppermute | solution.py:239
  42.3 0.6 collective-permute-done.5
  42.9 0.1 collective-permute-start.8
  43.1 1.5 %collective-permute-done.8 = bf16[32,4096]{1,0:T(8,128)(2,1)S(1)} collective-permute-done((bf16[32,4096]{1,0:T(8,128)(2,1)S(1)}, bf16[32,4096]{1,0:T(8,128)(2,1)S(1)}, u32[]{:S(2)}, u32[]{:S(2)}) %collective-permute-start.8) | collective-permute-done | bytes 262176 | tf_op jit(solution)/shard_map/ppermute | solution.py:239
  44.6 0.0 copy-done
  44.6 0.0 copy-done.1
  44.6 0.0 copy-done.2
  44.6 10.5 %histogram.1 = (f32[336,128]{1,0:T(8,128)S(1)}, f32[336,128]{1,0:T(8,128)S(1)}, f32[336,128]{1,0:T(8,128)S(1)}, f32[336,128]{1,0:T(8,128)S(1)}) custom-call(s32[16,8192]{1,0:T(8,128)S(1)} %bitcast.7, bf16[32,8192]{1,0:T(8,128)(2,1)S(1)} %constant_dynamic-update-slice_fusion.sketch, f32[1,8192]{1,0:T(1,128)S(1)} %bitcast.6, f32[4,64,128]{2,1,0:T(8,128)S(1)} %copy-done.2), custom_call_target="tpu_custom_call" | custom-call | flops 17179869184 | bytes 1500000 | tf_op jit(solution)/shard_map/histogram/pallas_call | solution.py:175
  55.1 1.8 %collective-permute-start.9 = (f32[336,128]{1,0:T(8,128)S(1)}, f32[336,128]{1,0:T(8,128)S(1)}, u32[]{:S(2)}, u32[]{:S(2)}) collective-permute-start(f32[336,128]{1,0:T(8,128)S(1)} %get-tuple-element.20), channel_id=1, source_target_pairs={{0,16},{16,0},{32,48},{48,32},{64,80},{80,64},{96,112},{112,96},{1... | collective-permute-start | bytes 516104 | tf_op jit(solution)/shard_map/ppermute | solution.py:239
  57.0 2.9 %collective-permute-start.10 = (f32[336,128]{1,0:T(8,128)S(1)}, f32[336,128]{1,0:T(8,128)S(1)}, u32[]{:S(2)}, u32[]{:S(2)}) collective-permute-start(f32[336,128]{1,0:T(8,128)S(1)} %get-tuple-element.21), channel_id=1, source_target_pairs={{0,32},{16,48},{32,0},{48,16},{64,96},{80,112},{96,64},{112,80},{1... | collective-permute-start | bytes 516104 | tf_op jit(solution)/shard_map/ppermute | solution.py:239
  59.9 0.2 collective-permute-start.11
  60.1 2.5 %collective-permute-done.9.b = f32[336,128]{1,0:T(8,128)S(1)} collective-permute-done((f32[336,128]{1,0:T(8,128)S(1)}, f32[336,128]{1,0:T(8,128)S(1)}, u32[]{:S(2)}, u32[]{:S(2)}) %collective-permute-start.9) | collective-permute-done | bytes 172064 | tf_op jit(solution)/shard_map/ppermute | solution.py:239
  62.6 5.4 %collective-permute-done.10.c = f32[336,128]{1,0:T(8,128)S(1)} collective-permute-done((f32[336,128]{1,0:T(8,128)S(1)}, f32[336,128]{1,0:T(8,128)S(1)}, u32[]{:S(2)}, u32[]{:S(2)}) %collective-permute-start.10) | collective-permute-done | bytes 172064 | tf_op jit(solution)/shard_map/ppermute | solution.py:239
  68.0 2.6 %collective-permute-done.11.d = f32[336,128]{1,0:T(8,128)S(1)} collective-permute-done((f32[336,128]{1,0:T(8,128)S(1)}, f32[336,128]{1,0:T(8,128)S(1)}, u32[]{:S(2)}, u32[]{:S(2)}) %collective-permute-start.11) | collective-permute-done | bytes 172064 | tf_op jit(solution)/shard_map/ppermute | solution.py:239
  70.6 0.2 regroup.1
  70.8 3.9 %collective-permute-start.12 = (f32[96,128]{1,0:T(8,128)S(1)}, f32[96,128]{1,0:T(8,128)S(1)}, u32[]{:S(2)}, u32[]{:S(2)}) collective-permute-start(f32[96,128]{1,0:T(8,128)S(1)} %get-tuple-element.24), channel_id=1, source_target_pairs={{0,64},{16,80},{32,96},{48,112},{64,0},{80,16},{96,32},{112,48},{1... | collective-permute-start | bytes 147464 | tf_op jit(solution)/shard_map/ppermute | solution.py:239
  74.7 0.9 %collective-permute-start.13 = (f32[96,128]{1,0:T(8,128)S(1)}, f32[96,128]{1,0:T(8,128)S(1)}, u32[]{:S(2)}, u32[]{:S(2)}) collective-permute-start(f32[96,128]{1,0:T(8,128)S(1)} %get-tuple-element.25), channel_id=1, source_target_pairs={{0,128},{16,144},{32,160},{48,176},{64,192},{80,208},{96,224},{112... | collective-permute-start | bytes 147464 | tf_op jit(solution)/shard_map/ppermute | solution.py:239
  75.6 1.6 %collective-permute-start.14 = (f32[96,128]{1,0:T(8,128)S(1)}, f32[96,128]{1,0:T(8,128)S(1)}, u32[]{:S(2)}, u32[]{:S(2)}) collective-permute-start(f32[96,128]{1,0:T(8,128)S(1)} %get-tuple-element.26), channel_id=1, source_target_pairs={{0,192},{16,208},{32,224},{48,240},{64,128},{80,144},{96,160},{112... | collective-permute-start | bytes 147464 | tf_op jit(solution)/shard_map/ppermute | solution.py:239
  77.1 0.0 collective-permute-done.12.b
  77.1 3.4 %collective-permute-done.13.c = f32[96,128]{1,0:T(8,128)S(1)} collective-permute-done((f32[96,128]{1,0:T(8,128)S(1)}, f32[96,128]{1,0:T(8,128)S(1)}, u32[]{:S(2)}, u32[]{:S(2)}) %collective-permute-start.13) | collective-permute-done | bytes 49184 | tf_op jit(solution)/shard_map/ppermute | solution.py:239
  80.6 1.0 %collective-permute-done.14.d = f32[96,128]{1,0:T(8,128)S(1)} collective-permute-done((f32[96,128]{1,0:T(8,128)S(1)}, f32[96,128]{1,0:T(8,128)S(1)}, u32[]{:S(2)}, u32[]{:S(2)}) %collective-permute-start.14) | collective-permute-done | bytes 49184 | tf_op jit(solution)/shard_map/ppermute | solution.py:239
  81.6 0.8 finish.1
  (8 shorter events, 0.1 us)
Async XLA Ops:
  7.4 5.8 %collective-permute-start = (f32[32,4096]{1,0:T(8,128)}, f32[32,4096]{1,0:T(8,128)S(1)}, u32[]{:S(2)}, u32[]{:S(2)}) collective-permute-start(f32[32,4096]{1,0:T(8,128)} %get-tuple-element.17), channel_id=1, source_target_pairs={{0,1},{1,0},{2,3},{3,2},{4,5},{5,4},{6,7},{7,6},{8,9},{9,8},{10,11... | collective-permute-start | bytes 1572872 | tf_op jit(solution)/shard_map/ppermute | solution.py:239
  13.1 31.5 %copy-start = (f32[8192]{0:T(1024)S(1)}, f32[8192]{0:T(1024)}, u32[]{:S(2)}) copy-start(f32[8192]{0:T(1024)} %reshape.17) | copy-start | bytes 98308
  13.1 31.5 %copy-start.1 = (s32[8192,16]{0,1:T(8,128)S(1)}, s32[8192,16]{0,1:T(8,128)}, u32[]{:S(2)}) copy-start(s32[8192,16]{0,1:T(8,128)} %param.9) | copy-start | bytes 1572868
  13.1 31.5 %copy-start.2 = (f32[4,64,128]{2,1,0:T(8,128)S(1)}, f32[4,64,128]{2,1,0:T(8,128)}, u32[]{:S(2)}) copy-start(f32[4,64,128]{2,1,0:T(8,128)} %get-tuple-element.18.leaf_part) | copy-start | bytes 393220
  14.4 7.9 %collective-permute-start.1 = (f32[32,1024]{1,0:T(8,128)S(1)}, f32[32,1024]{1,0:T(8,128)S(1)}, u32[]{:S(2)}, u32[]{:S(2)}) collective-permute-start(f32[32,1024]{1,0:T(8,128)S(1)} %get-tuple-element.29), channel_id=1, source_target_pairs={{0,4},{1,5},{2,6},{3,7},{4,0},{5,1},{6,2},{7,3},{8,12},{9,13},{10,... | collective-permute-start | bytes 393224 | tf_op jit(solution)/shard_map/ppermute | solution.py:239
  15.9 8.8 %collective-permute-start.3 = (f32[32,1024]{1,0:T(8,128)S(1)}, f32[32,1024]{1,0:T(8,128)S(1)}, u32[]{:S(2)}, u32[]{:S(2)}) collective-permute-start(f32[32,1024]{1,0:T(8,128)S(1)} %get-tuple-element.30), channel_id=1, source_target_pairs={{0,6},{1,7},{2,4},{3,5},{4,2},{5,3},{6,0},{7,1},{8,14},{9,15},{10,... | collective-permute-start | bytes 393224 | tf_op jit(solution)/shard_map/ppermute | solution.py:239
  17.9 6.7 %collective-permute-start.2 = (f32[32,1024]{1,0:T(8,128)S(1)}, f32[32,1024]{1,0:T(8,128)S(1)}, u32[]{:S(2)}, u32[]{:S(2)}) collective-permute-start(f32[32,1024]{1,0:T(8,128)S(1)} %get-tuple-element.31), channel_id=1, source_target_pairs={{0,2},{1,3},{2,0},{3,1},{4,6},{5,7},{6,4},{7,5},{8,10},{9,11},{10,... | collective-permute-start | bytes 393224 | tf_op jit(solution)/shard_map/ppermute | solution.py:239
  24.7 11.1 %collective-permute-start.4 = (f32[32,1024]{1,0:T(8,128)S(1)}, f32[32,1024]{1,0:T(8,128)S(1)}, u32[]{:S(2)}, u32[]{:S(2)}) collective-permute-start(f32[32,1024]{1,0:T(8,128)S(1)} %fusion.1), channel_id=1, source_target_pairs={{0,8},{1,9},{2,10},{3,11},{4,12},{5,13},{6,14},{7,15},{8,0},{9,1},... | collective-permute-start | bytes 393224 | tf_op jit(solution)/shard_map/ppermute | solution.py:239
  35.8 5.6 %collective-permute-start.7 = (bf16[32,1024]{1,0:T(8,128)(2,1)S(1)}, bf16[32,1024]{1,0:T(8,128)(2,1)S(1)}, u32[]{:S(2)}, u32[]{:S(2)}) collective-permute-start(bf16[32,1024]{1,0:T(8,128)(2,1)S(1)} %get-tuple-element.28), channel_id=1, source_target_pairs={{0,6},{1,7},{2,4},{3,5},{4,2},{5,3},{6,0},{7,1},{8,14},{9,15},{10,... | collective-permute-start | bytes 196616 | tf_op jit(solution)/shard_map/ppermute | solution.py:239
  36.6 5.8 %collective-permute-start.6 = (bf16[32,1024]{1,0:T(8,128)(2,1)S(1)}, bf16[32,1024]{1,0:T(8,128)(2,1)S(1)}, u32[]{:S(2)}, u32[]{:S(2)}) collective-permute-start(bf16[32,1024]{1,0:T(8,128)(2,1)S(1)} %get-tuple-element.28), channel_id=1, source_target_pairs={{0,4},{1,5},{2,6},{3,7},{4,0},{5,1},{6,2},{7,3},{8,12},{9,13},{10,... | collective-permute-start | bytes 196616 | tf_op jit(solution)/shard_map/ppermute | solution.py:239
  37.6 5.3 %collective-permute-start.5 = (bf16[32,1024]{1,0:T(8,128)(2,1)S(1)}, bf16[32,1024]{1,0:T(8,128)(2,1)S(1)}, u32[]{:S(2)}, u32[]{:S(2)}) collective-permute-start(bf16[32,1024]{1,0:T(8,128)(2,1)S(1)} %get-tuple-element.28), channel_id=1, source_target_pairs={{0,2},{1,3},{2,0},{3,1},{4,6},{5,7},{6,4},{7,5},{8,10},{9,11},{10,... | collective-permute-start | bytes 196616 | tf_op jit(solution)/shard_map/ppermute | solution.py:239
  42.9 1.6 %collective-permute-start.8 = (bf16[32,4096]{1,0:T(8,128)(2,1)S(1)}, bf16[32,4096]{1,0:T(8,128)(2,1)S(1)}, u32[]{:S(2)}, u32[]{:S(2)}) collective-permute-start(bf16[32,4096]{1,0:T(8,128)(2,1)S(1)} %pad_maximum_fusion), channel_id=1, source_target_pairs={{0,1},{1,0},{2,3},{3,2},{4,5},{5,4},{6,7},{7,6},{8,9},{9,8},{10,11... | collective-permute-start | bytes 786440 | tf_op jit(solution)/shard_map/ppermute | solution.py:239
  55.1 7.5 %collective-permute-start.9 = (f32[336,128]{1,0:T(8,128)S(1)}, f32[336,128]{1,0:T(8,128)S(1)}, u32[]{:S(2)}, u32[]{:S(2)}) collective-permute-start(f32[336,128]{1,0:T(8,128)S(1)} %get-tuple-element.20), channel_id=1, source_target_pairs={{0,16},{16,0},{32,48},{48,32},{64,80},{80,64},{96,112},{112,96},{1... | collective-permute-start | bytes 516104 | tf_op jit(solution)/shard_map/ppermute | solution.py:239
  57.0 11.1 %collective-permute-start.10 = (f32[336,128]{1,0:T(8,128)S(1)}, f32[336,128]{1,0:T(8,128)S(1)}, u32[]{:S(2)}, u32[]{:S(2)}) collective-permute-start(f32[336,128]{1,0:T(8,128)S(1)} %get-tuple-element.21), channel_id=1, source_target_pairs={{0,32},{16,48},{32,0},{48,16},{64,96},{80,112},{96,64},{112,80},{1... | collective-permute-start | bytes 516104 | tf_op jit(solution)/shard_map/ppermute | solution.py:239
  59.9 10.8 %collective-permute-start.11 = (f32[336,128]{1,0:T(8,128)S(1)}, f32[336,128]{1,0:T(8,128)S(1)}, u32[]{:S(2)}, u32[]{:S(2)}) collective-permute-start(f32[336,128]{1,0:T(8,128)S(1)} %get-tuple-element.22), channel_id=1, source_target_pairs={{0,48},{16,32},{32,16},{48,0},{64,112},{80,96},{96,80},{112,64},{1... | collective-permute-start | bytes 516104 | tf_op jit(solution)/shard_map/ppermute | solution.py:239
  70.8 6.3 %collective-permute-start.12 = (f32[96,128]{1,0:T(8,128)S(1)}, f32[96,128]{1,0:T(8,128)S(1)}, u32[]{:S(2)}, u32[]{:S(2)}) collective-permute-start(f32[96,128]{1,0:T(8,128)S(1)} %get-tuple-element.24), channel_id=1, source_target_pairs={{0,64},{16,80},{32,96},{48,112},{64,0},{80,16},{96,32},{112,48},{1... | collective-permute-start | bytes 147464 | tf_op jit(solution)/shard_map/ppermute | solution.py:239
  74.7 5.9 %collective-permute-start.13 = (f32[96,128]{1,0:T(8,128)S(1)}, f32[96,128]{1,0:T(8,128)S(1)}, u32[]{:S(2)}, u32[]{:S(2)}) collective-permute-start(f32[96,128]{1,0:T(8,128)S(1)} %get-tuple-element.25), channel_id=1, source_target_pairs={{0,128},{16,144},{32,160},{48,176},{64,192},{80,208},{96,224},{112... | collective-permute-start | bytes 147464 | tf_op jit(solution)/shard_map/ppermute | solution.py:239
  75.6 6.0 %collective-permute-start.14 = (f32[96,128]{1,0:T(8,128)S(1)}, f32[96,128]{1,0:T(8,128)S(1)}, u32[]{:S(2)}, u32[]{:S(2)}) collective-permute-start(f32[96,128]{1,0:T(8,128)S(1)} %get-tuple-element.26), channel_id=1, source_target_pairs={{0,192},{16,208},{32,224},{48,240},{64,128},{80,144},{96,160},{112... | collective-permute-start | bytes 147464 | tf_op jit(solution)/shard_map/ppermute | solution.py:239

commit v3 on v2

--- a/solution.py
+++ b/solution.py
@@ -14,6 +14,35 @@
 BF16 = jnp.bfloat16
 BLOCK = 1024
 CONTRACT_LAST = (((1,), (1,)), ((), ()))
+
+
+def group_count(rows):
+    return rows // 16
+
+
+def encoded_rows(rows):
+    return rows + -(-group_count(rows) // 16) * 16
+
+
+def encode_into(out, value):
+    rows = value.shape[0]
+    count = group_count(rows)
+    padded = encoded_rows(rows) - rows
+    tops = [jnp.max(jnp.abs(value[16 * g : 16 * g + 16, :]), axis=0, keepdims=True) for g in range(count)]
+    tops.append(jnp.zeros((padded - count, 128), F32))
+    exponent = jnp.ceil(jnp.log2(jnp.maximum(jnp.concatenate(tops, axis=0), 1e-30)))
+    scale = jnp.exp2(14.0 - exponent)
+    for g in range(count):
+        scaled = value[16 * g : 16 * g + 16, :] * scale[g : g + 1, :]
+        out[16 * g : 16 * g + 16, :] = jnp.round(scaled).astype(jnp.int32).astype(jnp.int16)
+    out[rows : rows + padded, :] = exponent.astype(jnp.int32).astype(jnp.int16)
+
+
+def decode(code, rows):
+    count = group_count(rows)
+    whole = code[...].astype(jnp.int32).astype(F32)
+    scale = jnp.exp2(whole[rows:, :] - 14.0)
+    return jnp.concatenate([whole[16 * g : 16 * g + 16, :] * scale[g : g + 1, :] for g in range(count)], axis=0)
 
 
 def own_block():
@@ -108,15 +137,15 @@
             jax.ShapeDtypeStruct((matrix_t.shape[0], half), F32),
             jax.ShapeDtypeStruct((4, 64, 128), F32),
         ],
-        compiler_params=pltpu.CompilerParams(vmem_limit_bytes=61 * 1024 * 1024),
+        compiler_params=pltpu.CompilerParams(vmem_limit_bytes=51 * 1024 * 1024),
         cost_estimate=pl.CostEstimate(flops=2 * half * 256 * 300, bytes_accessed=5000000, transcendentals=0),
         name="gradient",
     )(*given)
 
 
-def histogram_kernel(feat, sketch, weight, leaf_part, o0, o1, o2, o3, held, hess, *, steps):
+def histogram_kernel(feat, sketch, weight, leaf_part, o0, o1, o2, o3, held, hess, slab, *, steps):
     step = pl.program_id(0)
-    outs = (o0, o1, o2, o3)
+    codes = (o1, o2, o3)
     wide = sketch.shape[1]
     blocks = wide // BLOCK
     me = own_block()
@@ -158,13 +187,16 @@
     def _():
         for y in range(4):
             near, far = slice(16 * y, 16 * y + 16), slice(64 + 16 * y, 80 + 16 * y)
+            target = slab if y else o0
             for f in range(16):
-                outs[y][16 * f : 16 * f + 16, :] = jnp.concatenate([held[f, near, :], held[f, far, :]], axis=1)
+                target[16 * f : 16 * f + 16, :] = jnp.concatenate([held[f, near, :], held[f, far, :]], axis=1)
             lanes = [
                 hess[g, (far if z & 1 else near), 8 * (z >> 1) : 8 * (z >> 1) + 8] for z in range(4) for g in range(2)
             ]
-            outs[y][256:272, :] = jnp.concatenate(lanes + [jnp.zeros((16, 64), F32)], axis=1)
-            outs[y][272:336, :] = leaf_part[y]
+            target[256:272, :] = jnp.concatenate(lanes + [jnp.zeros((16, 64), F32)], axis=1)
+            target[272:336, :] = leaf_part[y]
+            if y:
+                encode_into(codes[y - 1], slab[...])
 
 
 def histogram(feat_t, sketch, weight, leaf_part):
@@ -177,8 +209,9 @@
         grid=(steps,),
         in_specs=[whole, pl.BlockSpec((32, wide), lambda j: (0, j)), whole, whole],
         out_specs=[whole] * 4,
-        scratch_shapes=[pltpu.VMEM((16, 128, 64), F32), pltpu.VMEM((2, 128, 16), F32)],
-        out_shape=[jax.ShapeDtypeStruct((336, 128), F32)] * 4,
+        scratch_shapes=[pltpu.VMEM((16, 128, 64), F32), pltpu.VMEM((2, 128, 16), F32), pltpu.VMEM((336, 128), F32)],
+        out_shape=[jax.ShapeDtypeStruct((336, 128), F32)]
+        + [jax.ShapeDtypeStruct((encoded_rows(336), 128), jnp.int16)] * 3,
         compiler_params=pltpu.CompilerParams(vmem_limit_bytes=24 * 1024 * 1024),
         cost_estimate=pl.CostEstimate(flops=2 * 8192 * 4096 * 256, bytes_accessed=1500000, transcendentals=0),
         name="histogram",
@@ -186,31 +219,37 @@
 
 
 def regroup_kernel(a, b, c, d, o0, o1, o2, o3):
-    outs = (o0, o1, o2, o3)
-    total = a[...] + b[...] + c[...] + d[...]
+    codes = (o1, o2, o3)
+    total = a[...] + decode(b, 336) + decode(c, 336) + decode(d, 336)
     for z in range(4):
         lane = 64 * (z & 1) + 32 * (z >> 1)
-        outs[z][0:64, :] = jnp.concatenate(
-            [total[64 * q : 64 * q + 64, lane : lane + 32] for q in range(4)], axis=1
+        value = jnp.concatenate(
+            [
+                jnp.concatenate([total[64 * q : 64 * q + 64, lane : lane + 32] for q in range(4)], axis=1),
+                jnp.concatenate([total[256:272, 16 * z : 16 * z + 16], jnp.zeros((16, 112), F32)], axis=1),
+                total[272 + 8 * z : 280 + 8 * z, :],
+                total[304 + 8 * z : 312 + 8 * z, :],
+            ],
+            axis=0,
         )
-        outs[z][64:80, :] = jnp.concatenate(
-            [total[256:272, 16 * z : 16 * z + 16], jnp.zeros((16, 112), F32)], axis=1
-        )
-        outs[z][80:88, :] = total[272 + 8 * z : 280 + 8 * z, :]
-        outs[z][88:96, :] = total[304 + 8 * z : 312 + 8 * z, :]
+        if z:
+            encode_into(codes[z - 1], value)
+        else:
+            o0[...] = value
 
 
 def regroup(a, b, c, d):
     return pl.pallas_call(
         regroup_kernel,
-        out_shape=[jax.ShapeDtypeStruct((96, 128), F32)] * 4,
+        out_shape=[jax.ShapeDtypeStruct((96, 128), F32)]
+        + [jax.ShapeDtypeStruct((encoded_rows(96), 128), jnp.int16)] * 3,
         compiler_params=pltpu.CompilerParams(vmem_limit_bytes=8 * 1024 * 1024),
         name="regroup",
     )(a, b, c, d)
 
 
 def finish_kernel(a, b, c, d, grad_out, hess_out, leaf_out, rows, *, per_bin):
-    total = a[...] + b[...] + c[...] + d[...]
+    total = a[...] + decode(b, 96) + decode(c, 96) + decode(d, 96)
     for q in range(4):
         rows[64 * q : 64 * q + 64, 0:32] = total[0:64, 32 * q : 32 * q + 32]
     for i in range(16):
@@ -239,6 +278,17 @@
     return lax.ppermute(value, axis, [(i, i ^ flip) for i in range(16)])
 
 
+def pack(value):
+    top = jnp.max(jnp.abs(value), axis=0, keepdims=True)
+    exponent = jnp.ceil(jnp.log2(jnp.maximum(top, 1e-30)))
+    return jnp.concatenate([value * jnp.exp2(-exponent), exponent], axis=0).astype(jnp.float16)
+
+
+def unpack(code):
+    whole = code.astype(F32)
+    return whole[:-1] * jnp.exp2(whole[-1:])
+
+
 def per_device(predictions, targets, row_weight, features, leaf, sketch_matrix):
     cells = predictions.shape[0]
     weight = row_weight.astype(F32).reshape(1, cells)
@@ -248,9 +298,9 @@
     mine, leaf_part = gradient_half(*args, leaf_part, 0)
     chip = mine + arrived
     blocks = [chip[:, BLOCK * j : BLOCK * (j + 1)] for j in range(4)]
-    far = [swap(blocks[j], "out", 2 * j) for j in (2, 1, 3)]
+    far = [unpack(swap(pack(blocks[j]), "out", 2 * j)) for j in (2, 1, 3)]
     part = blocks[0] + far[0] + far[1] + far[2]
-    own = (part + swap(part, "out", 8)).astype(BF16)
+    own = (part + unpack(swap(pack(part), "out", 8))).astype(BF16)
     sketch = jnp.concatenate([own] + [swap(own, "out", 2 * j) for j in (1, 2, 3)], axis=1)
     sketch = jnp.concatenate([sketch, swap(sketch, "out", 1)], axis=1)
     slices = histogram(features.T, sketch, weight, leaf_part)

time: 83.4 us -> 73.2 us (0.88)
  waiting for transfers between devices: 29.9 us -> 23.5 us
  Pallas kernels: 22.5 us -> 19.6 us
  local copies, waits for them, and re-layouts: 0.08 us -> 1.55 us
  other arithmetic: 2.54 us -> 1.22 us
  starting transfers between devices: 26.5 us -> 25.4 us
    ppermute x15, waiting for transfers between devices: 29.9 us -> 23.5 us  [swap(): return lax.ppermute(value, axis, [(i, i ^ flip) for i in range(16)])]
    pallas_call x2, Pallas kernels: 11.1 us -> 7.99 us  [gradient_half(): pl.pallas_call(functools.partial(gradient_kernel, first=first, parts=part...]
    unnamed x9, local copies, waits for them, and re-layouts: 0.04 us -> 1.5 us
    add x1, other arithmetic: 1.16 us -> 0.06 us  [per_device(): chip = mine + arrived]
    ppermute x15, starting transfers between devices: 26.5 us -> 25.4 us  [swap(): return lax.ppermute(value, axis, [(i, i ^ flip) for i in range(16)])]
  transfers between devices with their start and end apart: 15 -> 15, of which waited for: 12 -> 11; matrix products, arithmetic and copies ran while one was open for 0% -> 0% of each run, Pallas kernels for 7% -> 6%
where the time goes in v3:
time: 73.2 us; the launch traced here: 72.2 us
  starting transfers between devices  25.4 us (35%)
  waiting for transfers between devices  23.5 us (32%)
  Pallas kernels  19.6 us (27%)
  local copies, waits for them, and re-layouts  1.55 us (2%)
  other arithmetic  1.22 us (2%)
  between operations  0.9 us (1%)
    ppermute x15, starting transfers between devices, swap(): return lax.ppermute(value, axis, [(i, i ^ flip) for i in range(16)])  25.4 us
    ppermute x15, waiting for transfers between devices, swap(): return lax.ppermute(value, axis, [(i, i ^ flip) for i in range(16)])  23.5 us
    pallas_call x1, Pallas kernels, histogram(): pl.pallas_call(functools.partial(histogram_kernel, steps=steps), grid=(st...  10.6 us
    pallas_call x2, Pallas kernels, gradient_half(): pl.pallas_call(functools.partial(gradient_kernel, first=first, parts=part...  7.99 us
    unnamed x9, local copies, waits for them, and re-layouts  1.5 us
  transfers between devices with their start and end apart: 15, of which 11 were waited for; matrix products, arithmetic and copies ran while one was open for 0% of the time, Pallas kernels for 6%

profile of v3, /device:TPU:6, one launch (start us, length us, event | category | flops | bytes accessed | tf_op | source)
XLA Modules:
  0.0 72.2 jit_solution(11516935420612735943)
XLA Ops:
  0.6 0.7 %reshape.157 = f32[8192]{0:T(1024)S(1)} convert(bf16[8192]{0:T(1024)(128)(2,1)} %param.8) | non-fusion elementwise | flops 8192 | bytes 49152 | tf_op jit(solution)/shard_map/reshape | solution.py:294
  1.4 0.0 copy-start
  1.4 0.8 %copy-done = s32[8192]{0:T(1024)S(1)} copy-done((s32[8192]{0:T(1024)S(1)}, s32[8192]{0:T(1024)}, u32[]{:S(2)}) %copy-start) | copy-done | bytes 32792
  2.1 0.0 copy-start.1
  2.1 0.7 copy-done.1
  2.8 4.0 %gradient.2 = (f32[32,4096]{1,0:T(8,128)S(1)}, f32[4,64,128]{2,1,0:T(8,128)S(1)}) custom-call(bf16[8192,256]{1,0:T(8,128)(2,1)} %refs_0_.3, bf16[8192,256]{1,0:T(8,128)(2,1)} %refs_1_.3, f32[1,8192]{1,0:T(1,128)S(1)} %bitcast.8, s32[1,8192]{1,0:T(1,128)S(1)} %bitcast.11, bf16[32,256]{1,0:T(8,128)(2,1)S(1)} %bitcast.13), custom_call_target="tpu_custom_call" | custom-call | flops 629145600 | bytes 5000000 | tf_op jit(solution)/shard_map/gradient/pallas_call | solution.py:125
  6.8 0.1 collective-permute-start
  6.9 4.0 %gradient.3 = (f32[32,4096]{1,0:T(8,128)S(1)}, f32[4,64,128]{2,1,0:T(8,128)S(1)}) custom-call(bf16[8192,256]{1,0:T(8,128)(2,1)} %refs_0_.3, bf16[8192,256]{1,0:T(8,128)(2,1)} %refs_1_.3, f32[1,8192]{1,0:T(1,128)S(1)} %bitcast.9, s32[1,8192]{1,0:T(1,128)S(1)} %bitcast.12, bf16[32,256]{1,0:T(8,128)(2,1)S(1)} %bitcast.14, ...), custom_call_target="tpu_custom_call" | custom-call | flops 629145600 | bytes 5000000 | tf_op jit(solution)/shard_map/gradient/pallas_call | solution.py:125
  10.9 0.0 copy-start.2
  10.9 0.0 collective-permute-done
  11.0 0.1 add.15
  11.2 0.9 %collective-permute-start.2 = (f16[33,1024]{1,0:T(8,128)(2,1)S(1)}, f16[33,1024]{1,0:T(8,128)(2,1)S(1)}, u32[]{:S(2)}, u32[]{:S(2)}) collective-permute-start(f16[33,1024]{1,0:T(8,128)(2,1)S(1)} %pad_maximum_fusion.2), channel_id=1, source_target_pairs={{0,2},{1,3},{2,0},{3,1},{4,6},{5,7},{6,4},{7,5},{8,10},{9,11},{10,... | collective-permute-start | bytes 202760 | tf_op jit(solution)/shard_map/ppermute | solution.py:278
  12.2 1.5 %collective-permute-start.3 = (f16[33,1024]{1,0:T(8,128)(2,1)S(1)}, f16[33,1024]{1,0:T(8,128)(2,1)S(1)}, u32[]{:S(2)}, u32[]{:S(2)}) collective-permute-start(f16[33,1024]{1,0:T(8,128)(2,1)S(1)} %pad_maximum_fusion.3), channel_id=1, source_target_pairs={{0,6},{1,7},{2,4},{3,5},{4,2},{5,3},{6,0},{7,1},{8,14},{9,15},{10,... | collective-permute-start | bytes 202760 | tf_op jit(solution)/shard_map/ppermute | solution.py:278
  13.7 1.9 %collective-permute-start.1 = (f16[33,1024]{1,0:T(8,128)(2,1)S(1)}, f16[33,1024]{1,0:T(8,128)(2,1)S(1)}, u32[]{:S(2)}, u32[]{:S(2)}) collective-permute-start(f16[33,1024]{1,0:T(8,128)(2,1)S(1)} %pad_maximum_fusion.1), channel_id=1, source_target_pairs={{0,4},{1,5},{2,6},{3,7},{4,0},{5,1},{6,2},{7,3},{8,12},{9,13},{10,... | collective-permute-start | bytes 202760 | tf_op jit(solution)/shard_map/ppermute | solution.py:278
  15.6 0.5 collective-permute-done.2
  16.2 1.8 %collective-permute-done.3 = f16[33,1024]{1,0:T(8,128)(2,1)S(1)} collective-permute-done((f16[33,1024]{1,0:T(8,128)(2,1)S(1)}, f16[33,1024]{1,0:T(8,128)(2,1)S(1)}, u32[]{:S(2)}, u32[]{:S(2)}) %collective-permute-start.3) | collective-permute-done | bytes 67616 | tf_op jit(solution)/shard_map/ppermute | solution.py:278
  18.1 1.8 %collective-permute-done.1 = f16[33,1024]{1,0:T(8,128)(2,1)S(1)} collective-permute-done((f16[33,1024]{1,0:T(8,128)(2,1)S(1)}, f16[33,1024]{1,0:T(8,128)(2,1)S(1)}, u32[]{:S(2)}, u32[]{:S(2)}) %collective-permute-start.1) | collective-permute-done | bytes 67616 | tf_op jit(solution)/shard_map/ppermute | solution.py:278
  19.9 0.1 abs_reduce_fusion
  20.0 7.3 %collective-permute-start.4 = (f16[33,1024]{1,0:T(8,128)(2,1)S(1)}, f16[33,1024]{1,0:T(8,128)(2,1)S(1)}, u32[]{:S(2)}, u32[]{:S(2)}) collective-permute-start(f16[33,1024]{1,0:T(8,128)(2,1)S(1)} %pad_maximum_fusion.4), channel_id=1, source_target_pairs={{0,8},{1,9},{2,10},{3,11},{4,12},{5,13},{6,14},{7,15},{8,0},{9,1},... | collective-permute-start | bytes 202760 | tf_op jit(solution)/shard_map/ppermute | solution.py:278
  27.3 2.5 %collective-permute-done.4 = f16[33,1024]{1,0:T(8,128)(2,1)S(1)} collective-permute-done((f16[33,1024]{1,0:T(8,128)(2,1)S(1)}, f16[33,1024]{1,0:T(8,128)(2,1)S(1)}, u32[]{:S(2)}, u32[]{:S(2)}) %collective-permute-start.4) | collective-permute-done | bytes 67616 | tf_op jit(solution)/shard_map/ppermute | solution.py:278
  29.9 1.8 %collective-permute-start.7 = (bf16[32,1024]{1,0:T(8,128)(2,1)S(1)}, bf16[32,1024]{1,0:T(8,128)(2,1)S(1)}, u32[]{:S(2)}, u32[]{:S(2)}) collective-permute-start(bf16[32,1024]{1,0:T(8,128)(2,1)S(1)} %get-tuple-element.31), channel_id=1, source_target_pairs={{0,6},{1,7},{2,4},{3,5},{4,2},{5,3},{6,0},{7,1},{8,14},{9,15},{10,... | collective-permute-start | bytes 196616 | tf_op jit(solution)/shard_map/ppermute | solution.py:278
  31.7 0.4 collective-permute-start.6
  32.1 2.0 %collective-permute-start.5 = (bf16[32,1024]{1,0:T(8,128)(2,1)S(1)}, bf16[32,1024]{1,0:T(8,128)(2,1)S(1)}, u32[]{:S(2)}, u32[]{:S(2)}) collective-permute-start(bf16[32,1024]{1,0:T(8,128)(2,1)S(1)} %get-tuple-element.31), channel_id=1, source_target_pairs={{0,2},{1,3},{2,0},{3,1},{4,6},{5,7},{6,4},{7,5},{8,10},{9,11},{10,... | collective-permute-start | bytes 196616 | tf_op jit(solution)/shard_map/ppermute | solution.py:278
  34.1 1.4 %collective-permute-done.7 = bf16[32,1024]{1,0:T(8,128)(2,1)S(1)} collective-permute-done((bf16[32,1024]{1,0:T(8,128)(2,1)S(1)}, bf16[32,1024]{1,0:T(8,128)(2,1)S(1)}, u32[]{:S(2)}, u32[]{:S(2)}) %collective-permute-start.7) | collective-permute-done | bytes 65568 | tf_op jit(solution)/shard_map/ppermute | solution.py:278
  35.5 2.0 %collective-permute-done.6 = bf16[32,1024]{1,0:T(8,128)(2,1)S(1)} collective-permute-done((bf16[32,1024]{1,0:T(8,128)(2,1)S(1)}, bf16[32,1024]{1,0:T(8,128)(2,1)S(1)}, u32[]{:S(2)}, u32[]{:S(2)}) %collective-permute-start.6) | collective-permute-done | bytes 65568 | tf_op jit(solution)/shard_map/ppermute | solution.py:278
  37.5 0.0 collective-permute-done.5
  37.5 0.3 collective-permute-start.8
  37.8 1.5 %collective-permute-done.8 = bf16[32,4096]{1,0:T(8,128)(2,1)S(1)} collective-permute-done((bf16[32,4096]{1,0:T(8,128)(2,1)S(1)}, bf16[32,4096]{1,0:T(8,128)(2,1)S(1)}, u32[]{:S(2)}, u32[]{:S(2)}) %collective-permute-start.8) | collective-permute-done | bytes 262176 | tf_op jit(solution)/shard_map/ppermute | solution.py:278
  39.3 0.0 copy-done.2
  39.3 10.6 %histogram.1 = (f32[336,128]{1,0:T(8,128)S(1)}, s16[368,128]{1,0:T(8,128)(2,1)S(1)}, s16[368,128]{1,0:T(8,128)(2,1)S(1)}, s16[368,128]{1,0:T(8,128)(2,1)S(1)}) custom-call(s32[16,8192]{1,0:T(8,128)S(1)} %bitcast.15, bf16[32,8192]{1,0:T(8,128)(2,1)S(1)} %constant_dynamic-update-slice_fusion.sketch, f32[1,8192]{1,0:T(1,128)S(1)} %bitcast.10, ...), custom_call_target="tpu_custom_call" | custom-call | flops 17179869184 | bytes 1500000 | tf_op jit(solution)/shard_map/histogram/pallas_call | solution.py:207
  49.9 1.7 %collective-permute-start.9 = (s16[368,128]{1,0:T(8,128)(2,1)S(1)}, s16[368,128]{1,0:T(8,128)(2,1)S(1)}, u32[]{:S(2)}, u32[]{:S(2)}) collective-permute-start(s16[368,128]{1,0:T(8,128)(2,1)S(1)} %get-tuple-element.20), channel_id=1, source_target_pairs={{0,16},{16,0},{32,48},{48,32},{64,80},{80,64},{96,112},{112,96},{1... | collective-permute-start | bytes 282632 | tf_op jit(solution)/shard_map/ppermute | solution.py:278
  51.6 2.9 %collective-permute-start.10 = (s16[368,128]{1,0:T(8,128)(2,1)S(1)}, s16[368,128]{1,0:T(8,128)(2,1)S(1)}, u32[]{:S(2)}, u32[]{:S(2)}) collective-permute-start(s16[368,128]{1,0:T(8,128)(2,1)S(1)} %get-tuple-element.21), channel_id=1, source_target_pairs={{0,32},{16,48},{32,0},{48,16},{64,96},{80,112},{96,64},{112,80},{1... | collective-permute-start | bytes 282632 | tf_op jit(solution)/shard_map/ppermute | solution.py:278
  54.5 0.2 collective-permute-start.11
  54.7 0.1 collective-permute-done.9.b
  54.7 4.6 %collective-permute-done.10.c = s16[368,128]{1,0:T(8,128)(2,1)S(1)} collective-permute-done((s16[368,128]{1,0:T(8,128)(2,1)S(1)}, s16[368,128]{1,0:T(8,128)(2,1)S(1)}, u32[]{:S(2)}, u32[]{:S(2)}) %collective-permute-start.10) | collective-permute-done | bytes 94240 | tf_op jit(solution)/shard_map/ppermute | solution.py:278
  59.3 1.8 %collective-permute-done.11.d = s16[368,128]{1,0:T(8,128)(2,1)S(1)} collective-permute-done((s16[368,128]{1,0:T(8,128)(2,1)S(1)}, s16[368,128]{1,0:T(8,128)(2,1)S(1)}, u32[]{:S(2)}, u32[]{:S(2)}) %collective-permute-start.11) | collective-permute-done | bytes 94240 | tf_op jit(solution)/shard_map/ppermute | solution.py:278
  61.2 0.2 regroup.1
  61.4 1.9 %collective-permute-start.12 = (s16[112,128]{1,0:T(8,128)(2,1)S(1)}, s16[112,128]{1,0:T(8,128)(2,1)S(1)}, u32[]{:S(2)}, u32[]{:S(2)}) collective-permute-start(s16[112,128]{1,0:T(8,128)(2,1)S(1)} %get-tuple-element.24), channel_id=1, source_target_pairs={{0,64},{16,80},{32,96},{48,112},{64,0},{80,16},{96,32},{112,48},{1... | collective-permute-start | bytes 86024 | tf_op jit(solution)/shard_map/ppermute | solution.py:278
  63.3 2.4 %collective-permute-start.13 = (s16[112,128]{1,0:T(8,128)(2,1)S(1)}, s16[112,128]{1,0:T(8,128)(2,1)S(1)}, u32[]{:S(2)}, u32[]{:S(2)}) collective-permute-start(s16[112,128]{1,0:T(8,128)(2,1)S(1)} %get-tuple-element.25), channel_id=1, source_target_pairs={{0,128},{16,144},{32,160},{48,176},{64,192},{80,208},{96,224},{112... | collective-permute-start | bytes 86024 | tf_op jit(solution)/shard_map/ppermute | solution.py:278
  65.7 0.2 collective-permute-start.14
  65.9 0.0 collective-permute-done.12.b
  65.9 2.7 %collective-permute-done.13.c = s16[112,128]{1,0:T(8,128)(2,1)S(1)} collective-permute-done((s16[112,128]{1,0:T(8,128)(2,1)S(1)}, s16[112,128]{1,0:T(8,128)(2,1)S(1)}, u32[]{:S(2)}, u32[]{:S(2)}) %collective-permute-start.13) | collective-permute-done | bytes 28704 | tf_op jit(solution)/shard_map/ppermute | solution.py:278
  68.6 2.8 %collective-permute-done.14.d = s16[112,128]{1,0:T(8,128)(2,1)S(1)} collective-permute-done((s16[112,128]{1,0:T(8,128)(2,1)S(1)}, s16[112,128]{1,0:T(8,128)(2,1)S(1)}, u32[]{:S(2)}, u32[]{:S(2)}) %collective-permute-start.14) | collective-permute-done | bytes 28704 | tf_op jit(solution)/shard_map/ppermute | solution.py:278
  71.4 0.8 %finish.1 = (f32[16,16,32]{2,1,0:T(8,128)}, f32[16,16]{1,0:T(8,128)}, f32[4,256]{1,0:T(4,128)}) custom-call(f32[96,128]{1,0:T(8,128)S(1)} %get-tuple-element.23.a, s16[112,128]{1,0:T(8,128)(2,1)S(1)} %collective-permute-done.12.b, s16[112,128]{1,0:T(8,128)(2,1)S(1)} %collective-permute-done.13.c, s16[112,128]{1,0:T(8,128)(2,1)S(1)} %collective-permute-done.14.d), custom_call_target="tpu_custom_call" | custom-call | tf_op jit(solution)/shard_map/finish/pallas_call | solution.py:264
  (28 shorter events, 0.5 us)
Async XLA Ops:
  1.4 0.8 %copy-start = (s32[8192]{0:T(1024)S(1)}, s32[8192]{0:T(1024)}, u32[]{:S(2)}) copy-start(s32[8192]{0:T(1024)} %param.10) | copy-start | bytes 98308
  2.1 0.7 copy-start.1
  6.8 4.1 %collective-permute-start = (f32[32,4096]{1,0:T(8,128)S(1)}, f32[32,4096]{1,0:T(8,128)S(1)}, u32[]{:S(2)}, u32[]{:S(2)}) collective-permute-start(f32[32,4096]{1,0:T(8,128)S(1)} %get-tuple-element.17), channel_id=1, source_target_pairs={{0,1},{1,0},{2,3},{3,2},{4,5},{5,4},{6,7},{7,6},{8,9},{9,8},{10,11... | collective-permute-start | bytes 1572872 | tf_op jit(solution)/shard_map/ppermute | solution.py:278
  10.9 28.4 %copy-start.2 = (s32[8192,16]{0,1:T(8,128)S(1)}, s32[8192,16]{0,1:T(8,128)}, u32[]{:S(2)}) copy-start(s32[8192,16]{0,1:T(8,128)} %param.9) | copy-start | bytes 1572868
  11.2 4.9 %collective-permute-start.2 = (f16[33,1024]{1,0:T(8,128)(2,1)S(1)}, f16[33,1024]{1,0:T(8,128)(2,1)S(1)}, u32[]{:S(2)}, u32[]{:S(2)}) collective-permute-start(f16[33,1024]{1,0:T(8,128)(2,1)S(1)} %pad_maximum_fusion.2), channel_id=1, source_target_pairs={{0,2},{1,3},{2,0},{3,1},{4,6},{5,7},{6,4},{7,5},{8,10},{9,11},{10,... | collective-permute-start | bytes 202760 | tf_op jit(solution)/shard_map/ppermute | solution.py:278
  12.2 5.9 %collective-permute-start.3 = (f16[33,1024]{1,0:T(8,128)(2,1)S(1)}, f16[33,1024]{1,0:T(8,128)(2,1)S(1)}, u32[]{:S(2)}, u32[]{:S(2)}) collective-permute-start(f16[33,1024]{1,0:T(8,128)(2,1)S(1)} %pad_maximum_fusion.3), channel_id=1, source_target_pairs={{0,6},{1,7},{2,4},{3,5},{4,2},{5,3},{6,0},{7,1},{8,14},{9,15},{10,... | collective-permute-start | bytes 202760 | tf_op jit(solution)/shard_map/ppermute | solution.py:278
  13.7 6.1 %collective-permute-start.1 = (f16[33,1024]{1,0:T(8,128)(2,1)S(1)}, f16[33,1024]{1,0:T(8,128)(2,1)S(1)}, u32[]{:S(2)}, u32[]{:S(2)}) collective-permute-start(f16[33,1024]{1,0:T(8,128)(2,1)S(1)} %pad_maximum_fusion.1), channel_id=1, source_target_pairs={{0,4},{1,5},{2,6},{3,7},{4,0},{5,1},{6,2},{7,3},{8,12},{9,13},{10,... | collective-permute-start | bytes 202760 | tf_op jit(solution)/shard_map/ppermute | solution.py:278
  20.0 9.8 %collective-permute-start.4 = (f16[33,1024]{1,0:T(8,128)(2,1)S(1)}, f16[33,1024]{1,0:T(8,128)(2,1)S(1)}, u32[]{:S(2)}, u32[]{:S(2)}) collective-permute-start(f16[33,1024]{1,0:T(8,128)(2,1)S(1)} %pad_maximum_fusion.4), channel_id=1, source_target_pairs={{0,8},{1,9},{2,10},{3,11},{4,12},{5,13},{6,14},{7,15},{8,0},{9,1},... | collective-permute-start | bytes 202760 | tf_op jit(solution)/shard_map/ppermute | solution.py:278
  29.9 5.6 %collective-permute-start.7 = (bf16[32,1024]{1,0:T(8,128)(2,1)S(1)}, bf16[32,1024]{1,0:T(8,128)(2,1)S(1)}, u32[]{:S(2)}, u32[]{:S(2)}) collective-permute-start(bf16[32,1024]{1,0:T(8,128)(2,1)S(1)} %get-tuple-element.31), channel_id=1, source_target_pairs={{0,6},{1,7},{2,4},{3,5},{4,2},{5,3},{6,0},{7,1},{8,14},{9,15},{10,... | collective-permute-start | bytes 196616 | tf_op jit(solution)/shard_map/ppermute | solution.py:278
  31.7 5.8 %collective-permute-start.6 = (bf16[32,1024]{1,0:T(8,128)(2,1)S(1)}, bf16[32,1024]{1,0:T(8,128)(2,1)S(1)}, u32[]{:S(2)}, u32[]{:S(2)}) collective-permute-start(bf16[32,1024]{1,0:T(8,128)(2,1)S(1)} %get-tuple-element.31), channel_id=1, source_target_pairs={{0,4},{1,5},{2,6},{3,7},{4,0},{5,1},{6,2},{7,3},{8,12},{9,13},{10,... | collective-permute-start | bytes 196616 | tf_op jit(solution)/shard_map/ppermute | solution.py:278
  32.1 5.4 %collective-permute-start.5 = (bf16[32,1024]{1,0:T(8,128)(2,1)S(1)}, bf16[32,1024]{1,0:T(8,128)(2,1)S(1)}, u32[]{:S(2)}, u32[]{:S(2)}) collective-permute-start(bf16[32,1024]{1,0:T(8,128)(2,1)S(1)} %get-tuple-element.31), channel_id=1, source_target_pairs={{0,2},{1,3},{2,0},{3,1},{4,6},{5,7},{6,4},{7,5},{8,10},{9,11},{10,... | collective-permute-start | bytes 196616 | tf_op jit(solution)/shard_map/ppermute | solution.py:278
  37.5 1.8 %collective-permute-start.8 = (bf16[32,4096]{1,0:T(8,128)(2,1)S(1)}, bf16[32,4096]{1,0:T(8,128)(2,1)S(1)}, u32[]{:S(2)}, u32[]{:S(2)}) collective-permute-start(bf16[32,4096]{1,0:T(8,128)(2,1)S(1)} %pad_maximum_fusion), channel_id=1, source_target_pairs={{0,1},{1,0},{2,3},{3,2},{4,5},{5,4},{6,7},{7,6},{8,9},{9,8},{10,11... | collective-permute-start | bytes 786440 | tf_op jit(solution)/shard_map/ppermute | solution.py:278
  49.9 4.8 %collective-permute-start.9 = (s16[368,128]{1,0:T(8,128)(2,1)S(1)}, s16[368,128]{1,0:T(8,128)(2,1)S(1)}, u32[]{:S(2)}, u32[]{:S(2)}) collective-permute-start(s16[368,128]{1,0:T(8,128)(2,1)S(1)} %get-tuple-element.20), channel_id=1, source_target_pairs={{0,16},{16,0},{32,48},{48,32},{64,80},{80,64},{96,112},{112,96},{1... | collective-permute-start | bytes 282632 | tf_op jit(solution)/shard_map/ppermute | solution.py:278
  51.6 7.7 %collective-permute-start.10 = (s16[368,128]{1,0:T(8,128)(2,1)S(1)}, s16[368,128]{1,0:T(8,128)(2,1)S(1)}, u32[]{:S(2)}, u32[]{:S(2)}) collective-permute-start(s16[368,128]{1,0:T(8,128)(2,1)S(1)} %get-tuple-element.21), channel_id=1, source_target_pairs={{0,32},{16,48},{32,0},{48,16},{64,96},{80,112},{96,64},{112,80},{1... | collective-permute-start | bytes 282632 | tf_op jit(solution)/shard_map/ppermute | solution.py:278
  54.5 6.7 %collective-permute-start.11 = (s16[368,128]{1,0:T(8,128)(2,1)S(1)}, s16[368,128]{1,0:T(8,128)(2,1)S(1)}, u32[]{:S(2)}, u32[]{:S(2)}) collective-permute-start(s16[368,128]{1,0:T(8,128)(2,1)S(1)} %get-tuple-element.22), channel_id=1, source_target_pairs={{0,48},{16,32},{32,16},{48,0},{64,112},{80,96},{96,80},{112,64},{1... | collective-permute-start | bytes 282632 | tf_op jit(solution)/shard_map/ppermute | solution.py:278
  61.4 4.5 %collective-permute-start.12 = (s16[112,128]{1,0:T(8,128)(2,1)S(1)}, s16[112,128]{1,0:T(8,128)(2,1)S(1)}, u32[]{:S(2)}, u32[]{:S(2)}) collective-permute-start(s16[112,128]{1,0:T(8,128)(2,1)S(1)} %get-tuple-element.24), channel_id=1, source_target_pairs={{0,64},{16,80},{32,96},{48,112},{64,0},{80,16},{96,32},{112,48},{1... | collective-permute-start | bytes 86024 | tf_op jit(solution)/shard_map/ppermute | solution.py:278
  63.3 5.3 %collective-permute-start.13 = (s16[112,128]{1,0:T(8,128)(2,1)S(1)}, s16[112,128]{1,0:T(8,128)(2,1)S(1)}, u32[]{:S(2)}, u32[]{:S(2)}) collective-permute-start(s16[112,128]{1,0:T(8,128)(2,1)S(1)} %get-tuple-element.25), channel_id=1, source_target_pairs={{0,128},{16,144},{32,160},{48,176},{64,192},{80,208},{96,224},{112... | collective-permute-start | bytes 86024 | tf_op jit(solution)/shard_map/ppermute | solution.py:278
  65.7 5.7 %collective-permute-start.14 = (s16[112,128]{1,0:T(8,128)(2,1)S(1)}, s16[112,128]{1,0:T(8,128)(2,1)S(1)}, u32[]{:S(2)}, u32[]{:S(2)}) collective-permute-start(s16[112,128]{1,0:T(8,128)(2,1)S(1)} %get-tuple-element.26), channel_id=1, source_target_pairs={{0,192},{16,208},{32,224},{48,240},{64,128},{80,144},{96,160},{112... | collective-permute-start | bytes 86024 | tf_op jit(solution)/shard_map/ppermute | solution.py:278

commit v4 on v3

--- a/solution.py
+++ b/solution.py
@@ -45,28 +45,28 @@
     return jnp.concatenate([whole[16 * g : 16 * g + 16, :] * scale[g : g + 1, :] for g in range(count)], axis=0)
 
 
-def own_block():
+def cells_of(block):
     out_at = lax.axis_index("out")
-    return (out_at & 1) * 4 + ((out_at >> 1) & 3)
-
-
-def lanes_of(block):
-    return pl.ds(pl.multiple_of(block * BLOCK, BLOCK), BLOCK)
+    place = ((out_at & 1) ^ (block // 4)) * 4 + (((out_at >> 1) + block % 4) & 3)
+    return pl.multiple_of(place * BLOCK, BLOCK)
+
+
+def relative(value, size):
+    rows_at = lax.axis_index("rows")
+    return ((value - (rows_at >> 2) * (4 * size)) & (16 * size - 1)) ^ ((rows_at & 3) * size)
 
 
 def gradient_kernel(*refs, first, parts):
-    pred, targ, weight, leaf, matrix_t = refs[:5]
-    leaf_in = refs[5] if len(refs) == 13 else None
+    pred, targ, per_cell, matrix_t = refs[:4]
+    leaf_in = refs[4] if len(refs) == 12 else None
     sketch_out, leaf_out, pred_here, targ_here, sums, weights = refs[-7:-1]
     arrived = refs[-1]
-    me = own_block()
-    leaf_flip = lax.axis_index("rows") * 4
     size = BLOCK // parts
     copies = []
     for j in range(4):
         for part in range(parts):
             n = j * parts + part
-            rows = pl.ds(pl.multiple_of(((j + first) ^ me) * BLOCK + part * size, size), size)
+            rows = pl.ds(pl.multiple_of(cells_of(j + first) + part * size, size), size)
             pair = [
                 pltpu.make_async_copy(pred.at[rows, :], pred_here.at[n], arrived.at[0, n]),
                 pltpu.make_async_copy(targ.at[rows, :], targ_here.at[n], arrived.at[1, n]),
@@ -75,8 +75,9 @@
                 copy.start()
             copies.append(pair)
     for j in range(4):
-        w_wide = weight[:, lanes_of((j + first) ^ me)]
-        own = leaf[:, lanes_of((j + first) ^ me)] ^ leaf_flip
+        lanes = pl.ds(cells_of(j + first), BLOCK)
+        w_wide = per_cell[0:1, lanes]
+        own = relative(per_cell[1:2, lanes].astype(jnp.int32), 4)
         place = ((own >> 2) & 3) * 16 + (own >> 4) * 4 + (own & 3)
         onehot = jnp.where(lax.broadcasted_iota(jnp.int32, (LEAVES, BLOCK), 0) == place, 1.0, 0.0).astype(BF16)
         w_cols = jnp.transpose(
@@ -116,11 +117,11 @@
                 leaf_out[y, at : at + 4, :] = value if leaf_in is None else value + leaf_in[y, at : at + 4, :]
 
 
-def gradient_half(pred, targ, weight, leaf, matrix_t, leaf_in, first):
+def gradient_half(pred, targ, per_cell, matrix_t, leaf_in, first):
     genes = pred.shape[1]
     half = pred.shape[0] // 2
     parts = 2
-    given = [pred, targ, weight, leaf, matrix_t] + ([] if leaf_in is None else [leaf_in])
+    given = [pred, targ, per_cell, matrix_t] + ([] if leaf_in is None else [leaf_in])
     whole = pl.BlockSpec(memory_space=pltpu.VMEM)
     return pl.pallas_call(
         functools.partial(gradient_kernel, first=first, parts=parts),
@@ -143,32 +144,21 @@
     )(*given)
 
 
-def histogram_kernel(feat, sketch, weight, leaf_part, o0, o1, o2, o3, held, hess, slab, *, steps):
-    step = pl.program_id(0)
-    codes = (o1, o2, o3)
-    wide = sketch.shape[1]
-    blocks = wide // BLOCK
-    me = own_block()
-    bin_flip = lax.axis_index("rows") * 16
-
-    @pl.when(step == 0)
-    def _():
-        held[...] = jnp.zeros_like(held)
-        hess[...] = jnp.zeros_like(hess)
-
-    places = [lanes_of((step * blocks + b) ^ me) for b in range(blocks)]
+def histogram_products(feat, sketch, per_cell, first):
+    half = 4 * BLOCK
+    places = [pl.ds(cells_of(first + b), BLOCK) for b in range(4)]
     sketch_all = sketch[...]
-    w_row = jnp.concatenate([weight[:, place] for place in places], axis=1)
-    w_all = jnp.broadcast_to(w_row.astype(BF16), (16, wide))
-    rows128 = lax.broadcasted_iota(jnp.int32, (128, wide), 0).astype(BF16)
-    rows16 = lax.broadcasted_iota(jnp.int32, (16, wide), 0).astype(BF16)
+    w_row = jnp.concatenate([per_cell[0:1, place] for place in places], axis=1)
+    w_all = jnp.broadcast_to(w_row.astype(BF16), (16, half))
+    rows128 = lax.broadcasted_iota(jnp.int32, (128, half), 0).astype(BF16)
+    rows16 = lax.broadcasted_iota(jnp.int32, (16, half), 0).astype(BF16)
     zero = jnp.zeros((), BF16)
     one = jnp.ones((), BF16)
     for f in range(16):
-        own = jnp.concatenate([feat[f : f + 1, place] for place in places], axis=1) ^ bin_flip
+        own = relative(jnp.concatenate([feat[f : f + 1, place] for place in places], axis=1), 16)
         low = (own & 127).astype(F32).astype(BF16)
         top = own >> 7
-        group = jnp.broadcast_to(top.astype(F32).astype(BF16), (32, wide))
+        group = jnp.broadcast_to(top.astype(F32).astype(BF16), (32, half))
         left = jnp.where(rows128 == low, one, zero)
         spot = (top * 8 + (f % 8)).astype(F32).astype(BF16)
         right = jnp.concatenate(
@@ -179,43 +169,62 @@
             ],
             axis=0,
         )
-        both = lax.dot_general(left, right, CONTRACT_LAST, preferred_element_type=F32)
-        held[f] += both[:, 0:64]
+        yield f, lax.dot_general(left, right, CONTRACT_LAST, preferred_element_type=F32)
+
+
+def histogram_first_kernel(feat, sketch, per_cell, held, hess):
+    for f, both in histogram_products(feat, sketch, per_cell, 0):
+        held[f] = both[:, 0:64]
+        if f % 8 == 0:
+            hess[f // 8] = both[:, 64:80]
+        else:
+            hess[f // 8] += both[:, 64:80]
+
+
+def histogram_second_kernel(feat, sketch, per_cell, held, hess_in, leaf_part, o0, o1, o2, o3, hess, s1, s2, s3):
+    targets = (o0, s1, s2, s3)
+    hess[...] = hess_in[...]
+    for f, both in histogram_products(feat, sketch, per_cell, 4):
+        total = held[f] + both[:, 0:64]
+        for y in range(4):
+            lanes = [total[16 * y : 16 * y + 16, :], total[64 + 16 * y : 80 + 16 * y, :]]
+            targets[y][16 * f : 16 * f + 16, :] = jnp.concatenate(lanes, axis=1)
         hess[f // 8] += both[:, 64:80]
-
-    @pl.when(step == steps - 1)
-    def _():
-        for y in range(4):
-            near, far = slice(16 * y, 16 * y + 16), slice(64 + 16 * y, 80 + 16 * y)
-            target = slab if y else o0
-            for f in range(16):
-                target[16 * f : 16 * f + 16, :] = jnp.concatenate([held[f, near, :], held[f, far, :]], axis=1)
-            lanes = [
-                hess[g, (far if z & 1 else near), 8 * (z >> 1) : 8 * (z >> 1) + 8] for z in range(4) for g in range(2)
-            ]
-            target[256:272, :] = jnp.concatenate(lanes + [jnp.zeros((16, 64), F32)], axis=1)
-            target[272:336, :] = leaf_part[y]
-            if y:
-                encode_into(codes[y - 1], slab[...])
-
-
-def histogram(feat_t, sketch, weight, leaf_part):
-    cells = feat_t.shape[1]
-    wide = 2 * BLOCK
-    steps = cells // wide
-    whole = pl.BlockSpec(memory_space=pltpu.VMEM)
-    return pl.pallas_call(
-        functools.partial(histogram_kernel, steps=steps),
-        grid=(steps,),
-        in_specs=[whole, pl.BlockSpec((32, wide), lambda j: (0, j)), whole, whole],
-        out_specs=[whole] * 4,
-        scratch_shapes=[pltpu.VMEM((16, 128, 64), F32), pltpu.VMEM((2, 128, 16), F32), pltpu.VMEM((336, 128), F32)],
+    for y in range(4):
+        near, far = slice(16 * y, 16 * y + 16), slice(64 + 16 * y, 80 + 16 * y)
+        lanes = [
+            hess[g, (far if z & 1 else near), 8 * (z >> 1) : 8 * (z >> 1) + 8] for z in range(4) for g in range(2)
+        ]
+        targets[y][256:272, :] = jnp.concatenate(lanes + [jnp.zeros((16, 64), F32)], axis=1)
+        targets[y][272:336, :] = leaf_part[y]
+        if y:
+            encode_into((o1, o2, o3)[y - 1], targets[y][...])
+
+
+HISTOGRAM_OPTIONS = dict(
+    compiler_params=pltpu.CompilerParams(vmem_limit_bytes=24 * 1024 * 1024),
+    cost_estimate=pl.CostEstimate(flops=4096 * 4096 * 256, bytes_accessed=1500000, transcendentals=0),
+)
+
+
+def histogram_first(feat_t, sketch, per_cell):
+    return pl.pallas_call(
+        histogram_first_kernel,
+        out_shape=[jax.ShapeDtypeStruct((16, 128, 64), F32), jax.ShapeDtypeStruct((2, 128, 16), F32)],
+        name="histogram_first",
+        **HISTOGRAM_OPTIONS,
+    )(feat_t, sketch, per_cell)
+
+
+def histogram_second(feat_t, sketch, per_cell, held, hess, leaf_part):
+    return pl.pallas_call(
+        histogram_second_kernel,
+        scratch_shapes=[pltpu.VMEM((2, 128, 16), F32)] + [pltpu.VMEM((336, 128), F32)] * 3,
         out_shape=[jax.ShapeDtypeStruct((336, 128), F32)]
         + [jax.ShapeDtypeStruct((encoded_rows(336), 128), jnp.int16)] * 3,
-        compiler_params=pltpu.CompilerParams(vmem_limit_bytes=24 * 1024 * 1024),
-        cost_estimate=pl.CostEstimate(flops=2 * 8192 * 4096 * 256, bytes_accessed=1500000, transcendentals=0),
-        name="histogram",
-    )(feat_t, sketch, weight, leaf_part)
+        name="histogram_second",
+        **HISTOGRAM_OPTIONS,
+    )(feat_t, sketch, per_cell, held, hess, leaf_part)
 
 
 def regroup_kernel(a, b, c, d, o0, o1, o2, o3):
@@ -278,6 +287,13 @@
     return lax.ppermute(value, axis, [(i, i ^ flip) for i in range(16)])
 
 
+def shift(value, axis, unit, step):
+    place = lambda i: (i // unit) % 4
+    return lax.ppermute(
+        value, axis, [(i, i + ((place(i) + step) % 4 - place(i)) * unit) for i in range(16)]
+    )
+
+
 def pack(value):
     top = jnp.max(jnp.abs(value), axis=0, keepdims=True)
     exponent = jnp.ceil(jnp.log2(jnp.maximum(top, 1e-30)))
@@ -291,22 +307,24 @@
 
 def per_device(predictions, targets, row_weight, features, leaf, sketch_matrix):
     cells = predictions.shape[0]
-    weight = row_weight.astype(F32).reshape(1, cells)
-    args = (predictions, targets, weight, leaf.reshape(1, cells), sketch_matrix.T)
+    per_cell = jnp.stack([row_weight.astype(F32), leaf.astype(F32)])
+    features_t = features.T
+    args = (predictions, targets, per_cell, sketch_matrix.T)
     other, leaf_part = gradient_half(*args, None, 4)
     arrived = swap(other, "out", 1)
     mine, leaf_part = gradient_half(*args, leaf_part, 0)
     chip = mine + arrived
     blocks = [chip[:, BLOCK * j : BLOCK * (j + 1)] for j in range(4)]
-    far = [unpack(swap(pack(blocks[j]), "out", 2 * j)) for j in (2, 1, 3)]
+    far = [unpack(shift(pack(blocks[j]), "out", 2, j)) for j in (2, 1, 3)]
     part = blocks[0] + far[0] + far[1] + far[2]
     own = (part + unpack(swap(pack(part), "out", 8))).astype(BF16)
-    sketch = jnp.concatenate([own] + [swap(own, "out", 2 * j) for j in (1, 2, 3)], axis=1)
-    sketch = jnp.concatenate([sketch, swap(sketch, "out", 1)], axis=1)
-    slices = histogram(features.T, sketch, weight, leaf_part)
+    near_half = jnp.concatenate([own] + [shift(own, "out", 2, -j) for j in (1, 2, 3)], axis=1)
+    far_half = swap(near_half, "out", 1)
+    held = histogram_first(features_t, near_half, per_cell)
+    slices = histogram_second(features_t, far_half, per_cell, *held, leaf_part)
     slices = regroup(slices[0], *[swap(slices[j], "rows", j) for j in (1, 2, 3)])
     return tuple(
-        finish(slices[0], *[swap(slices[j], "rows", 4 * j) for j in (1, 2, 3)], float(cells * 16 // BINS))
+        finish(slices[0], *[shift(slices[j], "rows", 4, j) for j in (1, 2, 3)], float(cells * 16 // BINS))
     )
 
 

time: 73.2 us -> 68.7 us (0.939); the launches traced: 72.2 us -> 68.4 us
  starting transfers between devices: 25.4 us -> 23.7 us
  Pallas kernels: 19.6 us -> 18.5 us
  waiting for transfers between devices: 23.5 us -> 22.4 us
  other arithmetic: 1.22 us -> 2.05 us
  local copies, waits for them, and re-layouts: 1.55 us -> 0.75 us
    ppermute x15 -> x6, starting transfers between devices: 25.4 us -> 10.7 us  [swap(): return lax.ppermute(value, axis, [(i, i ^ flip) for i in range(16)])]
    ppermute x15 -> x6, waiting for transfers between devices: 23.5 us -> 9.54 us  [swap(): return lax.ppermute(value, axis, [(i, i ^ flip) for i in range(16)])]
    ppermute x0 -> x9, starting transfers between devices: none -> 13 us  [shift(): lax.ppermute(value, axis, [(i, i + ((place(i) + step) % 4 - place(i)) * u...]
    ppermute x0 -> x9, waiting for transfers between devices: none -> 12.9 us  [shift(): lax.ppermute(value, axis, [(i, i + ((place(i) + step) % 4 - place(i)) * u...]
    pallas_call x1 -> x2, Pallas kernels: 10.6 us -> 9.52 us  [the longest x1 4.85 us: histogram_second(): pl.pallas_call(histogram_second_kernel, scratch_shapes=[pltpu.VMEM((2, 12...]
    another operation x2 -> x4, other arithmetic: 0.06 us -> 0.84 us  [the longest x2 0.79 us: per_device(): per_cell = jnp.stack([row_weight.astype(F32), leaf.astype(F32)])]
    convert_element_type x0 -> x2, other arithmetic: none -> 0.78 us  [the longest x1 0.76 us: per_device(): per_cell = jnp.stack([row_weight.astype(F32), leaf.astype(F32)])]
    unnamed x9 -> x4, local copies, waits for them, and re-layouts: 1.5 us -> 0.72 us
  transfers between devices with their start and end apart: 15 -> 15, of which waited for: 11 -> 11; matrix products, arithmetic and copies ran while one was open for 0% -> 0% of each run, Pallas kernels for 6% -> 13%
where the time goes in v4:
time: 68.7 us; the launch traced here: 68.4 us
  starting transfers between devices  23.7 us (34%)
  waiting for transfers between devices  22.4 us (33%)
  Pallas kernels  18.5 us (27%)
  other arithmetic  2.05 us (3%)
  between operations  0.92 us (1%)
  local copies, waits for them, and re-layouts  0.75 us (1%)
    ppermute x9, starting transfers between devices, shift(): lax.ppermute(value, axis, [(i, i + ((place(i) + step) % 4 - place(i)) * u...  13 us
    ppermute x9, waiting for transfers between devices, shift(): lax.ppermute(value, axis, [(i, i + ((place(i) + step) % 4 - place(i)) * u...  12.9 us
    ppermute x6, starting transfers between devices, swap(): return lax.ppermute(value, axis, [(i, i ^ flip) for i in range(16)])  10.7 us
    ppermute x6, waiting for transfers between devices, swap(): return lax.ppermute(value, axis, [(i, i ^ flip) for i in range(16)])  9.54 us
    pallas_call x2, Pallas kernels, gradient_half(): pl.pallas_call(functools.partial(gradient_kernel, first=first, parts=part...  7.99 us
    pallas_call x1, Pallas kernels, histogram_second(): pl.pallas_call(histogram_second_kernel, scratch_shapes=[pltpu.VMEM((2, 12...  4.85 us
    pallas_call x1, Pallas kernels, histogram_first(): pl.pallas_call(histogram_first_kernel, out_shape=[jax.ShapeDtypeStruct((1...  4.67 us
  transfers between devices with their start and end apart: 15, of which 11 were waited for; matrix products, arithmetic and copies ran while one was open for 0% of the time, Pallas kernels for 13%

profile of v4, /device:TPU:6, one launch (start us, length us, event | category | flops | bytes accessed | tf_op | source)
XLA Modules:
  0.0 68.4 jit_solution(1395356812433265039)
XLA Ops:
  0.6 0.7 %stack.16 = f32[8192]{0:T(1024)S(1)} convert(bf16[8192]{0:T(1024)(128)(2,1)} %param.8) | non-fusion elementwise | flops 8192 | bytes 49152 | tf_op jit(solution)/shard_map/stack | solution.py:310
  1.4 0.8 %convert_element_type.23 = f32[8192]{0:T(1024)S(1)} convert(s32[8192]{0:T(1024)} %param.10) | non-fusion elementwise | flops 8192 | bytes 65536 | tf_op jit(solution)/shard_map/convert_element_type | solution.py:310
  2.1 0.1 pad_maximum_fusion.5.refs_2_.per_cell
  2.2 0.0 copy-start
  2.2 0.7 %copy-done = bf16[256,32]{0,1:T(8,128)(2,1)S(1)} copy-done((bf16[256,32]{0,1:T(8,128)(2,1)S(1)}, bf16[256,32]{0,1:T(8,128)(2,1)}, u32[]{:S(2)}) %copy-start) | copy-done | bytes 16408
  2.9 4.0 %gradient.2 = (f32[32,4096]{1,0:T(8,128)S(1)}, f32[4,64,128]{2,1,0:T(8,128)S(1)}) custom-call(bf16[8192,256]{1,0:T(8,128)(2,1)} %refs_0_.3, bf16[8192,256]{1,0:T(8,128)(2,1)} %refs_1_.3, f32[2,8192]{1,0:T(2,128)S(1)} %pad_maximum_fusion.5.refs_2_.per_cell, bf16[32,256]{1,0:T(8,128)(2,1)S(1)} %bitcast.8), custom_call_target="tpu_custom_call" | custom-call | flops 629145600 | bytes 5000000 | tf_op jit(solution)/shard_map/gradient/pallas_call | solution.py:126
  6.9 0.1 collective-permute-start
  7.0 4.0 %gradient.3 = (f32[32,4096]{1,0:T(8,128)S(1)}, f32[4,64,128]{2,1,0:T(8,128)S(1)}) custom-call(bf16[8192,256]{1,0:T(8,128)(2,1)} %refs_0_.3, bf16[8192,256]{1,0:T(8,128)(2,1)} %refs_1_.3, f32[2,8192]{1,0:T(2,128)S(1)} %pad_maximum_fusion.5.refs_2_.per_cell, bf16[32,256]{1,0:T(8,128)(2,1)S(1)} %bitcast.9, f32[4,64,128]{2,1,0:T(8,128)S(1)} %get-tuple-element.17.refs_4_), custom_call_target="tpu_custom_call" | custom-call | flops 629145600 | bytes 5000000 | tf_op jit(solution)/shard_map/gradient/pallas_call | solution.py:126
  11.0 0.0 copy-start.1
  11.0 0.0 collective-permute-done
  11.0 0.1 add.15
  11.3 2.3 %collective-permute-start.2 = (f16[33,1024]{1,0:T(8,128)(2,1)S(1)}, f16[33,1024]{1,0:T(8,128)(2,1)S(1)}, u32[]{:S(2)}, u32[]{:S(2)}) collective-permute-start(f16[33,1024]{1,0:T(8,128)(2,1)S(1)} %pad_maximum_fusion.2), channel_id=1, source_target_pairs={{0,2},{1,3},{2,4},{3,5},{4,6},{5,7},{6,0},{7,1},{8,10},{9,11},{10,... | collective-permute-start | bytes 202760 | tf_op jit(solution)/shard_map/ppermute | solution.py:292
  13.6 0.1 collective-permute-start.3
  13.8 1.5 %collective-permute-start.1 = (f16[33,1024]{1,0:T(8,128)(2,1)S(1)}, f16[33,1024]{1,0:T(8,128)(2,1)S(1)}, u32[]{:S(2)}, u32[]{:S(2)}) collective-permute-start(f16[33,1024]{1,0:T(8,128)(2,1)S(1)} %pad_maximum_fusion.1), channel_id=1, source_target_pairs={{0,4},{1,5},{2,6},{3,7},{4,0},{5,1},{6,2},{7,3},{8,12},{9,13},{10,... | collective-permute-start | bytes 202760 | tf_op jit(solution)/shard_map/ppermute | solution.py:292
  15.3 0.9 %collective-permute-done.2 = f16[33,1024]{1,0:T(8,128)(2,1)S(1)} collective-permute-done((f16[33,1024]{1,0:T(8,128)(2,1)S(1)}, f16[33,1024]{1,0:T(8,128)(2,1)S(1)}, u32[]{:S(2)}, u32[]{:S(2)}) %collective-permute-start.2) | collective-permute-done | bytes 67616 | tf_op jit(solution)/shard_map/ppermute | solution.py:292
  16.3 5.0 %collective-permute-done.3 = f16[33,1024]{1,0:T(8,128)(2,1)S(1)} collective-permute-done((f16[33,1024]{1,0:T(8,128)(2,1)S(1)}, f16[33,1024]{1,0:T(8,128)(2,1)S(1)}, u32[]{:S(2)}, u32[]{:S(2)}) %collective-permute-start.3) | collective-permute-done | bytes 67616 | tf_op jit(solution)/shard_map/ppermute | solution.py:292
  21.3 0.0 collective-permute-done.1
  21.3 0.1 abs_reduce_fusion
  21.5 5.6 %collective-permute-start.4 = (f16[33,1024]{1,0:T(8,128)(2,1)S(1)}, f16[33,1024]{1,0:T(8,128)(2,1)S(1)}, u32[]{:S(2)}, u32[]{:S(2)}) collective-permute-start(f16[33,1024]{1,0:T(8,128)(2,1)S(1)} %pad_maximum_fusion.4), channel_id=1, source_target_pairs={{0,8},{1,9},{2,10},{3,11},{4,12},{5,13},{6,14},{7,15},{8,0},{9,1},... | collective-permute-start | bytes 202760 | tf_op jit(solution)/shard_map/ppermute | solution.py:287
  27.1 2.9 %collective-permute-done.4 = f16[33,1024]{1,0:T(8,128)(2,1)S(1)} collective-permute-done((f16[33,1024]{1,0:T(8,128)(2,1)S(1)}, f16[33,1024]{1,0:T(8,128)(2,1)S(1)}, u32[]{:S(2)}, u32[]{:S(2)}) %collective-permute-start.4) | collective-permute-done | bytes 67616 | tf_op jit(solution)/shard_map/ppermute | solution.py:287
  30.0 1.8 %collective-permute-start.7 = (bf16[32,1024]{1,0:T(8,128)(2,1)S(1)}, bf16[32,1024]{1,0:T(8,128)(2,1)S(1)}, u32[]{:S(2)}, u32[]{:S(2)}) collective-permute-start(bf16[32,1024]{1,0:T(8,128)(2,1)S(1)} %fusion.1), channel_id=1, source_target_pairs={{0,2},{1,3},{2,4},{3,5},{4,6},{5,7},{6,0},{7,1},{8,10},{9,11},{10,... | collective-permute-start | bytes 196616 | tf_op jit(solution)/shard_map/ppermute | solution.py:292
  31.8 0.8 %collective-permute-start.6 = (bf16[32,1024]{1,0:T(8,128)(2,1)S(1)}, bf16[32,1024]{1,0:T(8,128)(2,1)S(1)}, u32[]{:S(2)}, u32[]{:S(2)}) collective-permute-start(bf16[32,1024]{1,0:T(8,128)(2,1)S(1)} %fusion.1), channel_id=1, source_target_pairs={{0,4},{1,5},{2,6},{3,7},{4,0},{5,1},{6,2},{7,3},{8,12},{9,13},{10,... | collective-permute-start | bytes 196616 | tf_op jit(solution)/shard_map/ppermute | solution.py:292
  32.6 0.6 collective-permute-start.5
  33.2 1.1 %collective-permute-done.7 = bf16[32,1024]{1,0:T(8,128)(2,1)S(1)} collective-permute-done((bf16[32,1024]{1,0:T(8,128)(2,1)S(1)}, bf16[32,1024]{1,0:T(8,128)(2,1)S(1)}, u32[]{:S(2)}, u32[]{:S(2)}) %collective-permute-start.7) | collective-permute-done | bytes 65568 | tf_op jit(solution)/shard_map/ppermute | solution.py:292
  34.3 3.3 %collective-permute-done.6 = bf16[32,1024]{1,0:T(8,128)(2,1)S(1)} collective-permute-done((bf16[32,1024]{1,0:T(8,128)(2,1)S(1)}, bf16[32,1024]{1,0:T(8,128)(2,1)S(1)}, u32[]{:S(2)}, u32[]{:S(2)}) %collective-permute-start.6) | collective-permute-done | bytes 65568 | tf_op jit(solution)/shard_map/ppermute | solution.py:292
  37.6 0.7 collective-permute-done.5
  38.3 0.3 collective-permute-start.8
  38.6 0.0 copy-done.1
  38.6 4.7 %histogram_first.1 = (f32[16,128,64]{2,1,0:T(8,128)S(1)}, f32[2,128,16]{2,1,0:T(8,128)S(1)}) custom-call(s32[16,8192]{1,0:T(8,128)S(1)} %bitcast.10, bf16[32,4096]{1,0:T(8,128)(2,1)S(1)} %pad_maximum_fusion.sketch, f32[2,8192]{1,0:T(2,128)S(1)} %pad_maximum_fusion.5.refs_2_.per_cell), custom_call_target="tpu_custom_call" | custom-call | flops 4294967296 | bytes 1500000 | tf_op jit(solution)/shard_map/histogram_first/pallas_call | solution.py:211
  43.3 0.0 collective-permute-done.8.sketch
  43.3 4.8 %histogram_second.1 = (f32[336,128]{1,0:T(8,128)S(1)}, s16[368,128]{1,0:T(8,128)(2,1)S(1)}, s16[368,128]{1,0:T(8,128)(2,1)S(1)}, s16[368,128]{1,0:T(8,128)(2,1)S(1)}) custom-call(s32[16,8192]{1,0:T(8,128)S(1)} %bitcast.11, bf16[32,4096]{1,0:T(8,128)(2,1)S(1)} %collective-permute-done.8.sketch, f32[2,8192]{1,0:T(2,128)S(1)} %pad_maximum_fusion.5.refs_2_.per_cell, ...), custom_call_target="tpu_custom_call" | custom-call | flops 4294967296 | bytes 1500000 | tf_op jit(solution)/shard_map/histogram_second/pallas_call | solution.py:220
  48.2 1.5 %collective-permute-start.9 = (s16[368,128]{1,0:T(8,128)(2,1)S(1)}, s16[368,128]{1,0:T(8,128)(2,1)S(1)}, u32[]{:S(2)}, u32[]{:S(2)}) collective-permute-start(s16[368,128]{1,0:T(8,128)(2,1)S(1)} %get-tuple-element.24), channel_id=1, source_target_pairs={{0,16},{16,0},{32,48},{48,32},{64,80},{80,64},{96,112},{112,96},{1... | collective-permute-start | bytes 282632 | tf_op jit(solution)/shard_map/ppermute | solution.py:287
  49.6 2.9 %collective-permute-start.10 = (s16[368,128]{1,0:T(8,128)(2,1)S(1)}, s16[368,128]{1,0:T(8,128)(2,1)S(1)}, u32[]{:S(2)}, u32[]{:S(2)}) collective-permute-start(s16[368,128]{1,0:T(8,128)(2,1)S(1)} %get-tuple-element.25), channel_id=1, source_target_pairs={{0,32},{16,48},{32,0},{48,16},{64,96},{80,112},{96,64},{112,80},{1... | collective-permute-start | bytes 282632 | tf_op jit(solution)/shard_map/ppermute | solution.py:287
  52.5 0.4 collective-permute-start.11
  52.9 0.4 collective-permute-done.9.b
  53.3 4.4 %collective-permute-done.10.c = s16[368,128]{1,0:T(8,128)(2,1)S(1)} collective-permute-done((s16[368,128]{1,0:T(8,128)(2,1)S(1)}, s16[368,128]{1,0:T(8,128)(2,1)S(1)}, u32[]{:S(2)}, u32[]{:S(2)}) %collective-permute-start.10) | collective-permute-done | bytes 94240 | tf_op jit(solution)/shard_map/ppermute | solution.py:287
  57.7 1.9 %collective-permute-done.11.d = s16[368,128]{1,0:T(8,128)(2,1)S(1)} collective-permute-done((s16[368,128]{1,0:T(8,128)(2,1)S(1)}, s16[368,128]{1,0:T(8,128)(2,1)S(1)}, u32[]{:S(2)}, u32[]{:S(2)}) %collective-permute-start.11) | collective-permute-done | bytes 94240 | tf_op jit(solution)/shard_map/ppermute | solution.py:287
  59.6 0.2 regroup.1
  59.9 1.9 %collective-permute-start.12 = (s16[112,128]{1,0:T(8,128)(2,1)S(1)}, s16[112,128]{1,0:T(8,128)(2,1)S(1)}, u32[]{:S(2)}, u32[]{:S(2)}) collective-permute-start(s16[112,128]{1,0:T(8,128)(2,1)S(1)} %get-tuple-element.28), channel_id=1, source_target_pairs={{0,64},{16,80},{32,96},{48,112},{64,128},{80,144},{96,160},{112,17... | collective-permute-start | bytes 86024 | tf_op jit(solution)/shard_map/ppermute | solution.py:292
  61.8 2.0 %collective-permute-start.13 = (s16[112,128]{1,0:T(8,128)(2,1)S(1)}, s16[112,128]{1,0:T(8,128)(2,1)S(1)}, u32[]{:S(2)}, u32[]{:S(2)}) collective-permute-start(s16[112,128]{1,0:T(8,128)(2,1)S(1)} %get-tuple-element.29), channel_id=1, source_target_pairs={{0,128},{16,144},{32,160},{48,176},{64,192},{80,208},{96,224},{112... | collective-permute-start | bytes 86024 | tf_op jit(solution)/shard_map/ppermute | solution.py:292
  63.8 2.0 %collective-permute-start.14 = (s16[112,128]{1,0:T(8,128)(2,1)S(1)}, s16[112,128]{1,0:T(8,128)(2,1)S(1)}, u32[]{:S(2)}, u32[]{:S(2)}) collective-permute-start(s16[112,128]{1,0:T(8,128)(2,1)S(1)} %get-tuple-element.30), channel_id=1, source_target_pairs={{0,192},{16,208},{32,224},{48,240},{64,0},{80,16},{96,32},{112,48}... | collective-permute-start | bytes 86024 | tf_op jit(solution)/shard_map/ppermute | solution.py:292
  65.8 0.0 collective-permute-done.12.b
  65.8 1.0 %collective-permute-done.13.c = s16[112,128]{1,0:T(8,128)(2,1)S(1)} collective-permute-done((s16[112,128]{1,0:T(8,128)(2,1)S(1)}, s16[112,128]{1,0:T(8,128)(2,1)S(1)}, u32[]{:S(2)}, u32[]{:S(2)}) %collective-permute-start.13) | collective-permute-done | bytes 28704 | tf_op jit(solution)/shard_map/ppermute | solution.py:292
  66.7 0.9 %collective-permute-done.14.d = s16[112,128]{1,0:T(8,128)(2,1)S(1)} collective-permute-done((s16[112,128]{1,0:T(8,128)(2,1)S(1)}, s16[112,128]{1,0:T(8,128)(2,1)S(1)}, u32[]{:S(2)}, u32[]{:S(2)}) %collective-permute-start.14) | collective-permute-done | bytes 28704 | tf_op jit(solution)/shard_map/ppermute | solution.py:292
  67.6 0.8 %finish.1 = (f32[16,16,32]{2,1,0:T(8,128)}, f32[16,16]{1,0:T(8,128)}, f32[4,256]{1,0:T(4,128)}) custom-call(f32[96,128]{1,0:T(8,128)S(1)} %get-tuple-element.27.a, s16[112,128]{1,0:T(8,128)(2,1)S(1)} %collective-permute-done.12.b, s16[112,128]{1,0:T(8,128)(2,1)S(1)} %collective-permute-done.13.c, s16[112,128]{1,0:T(8,128)(2,1)S(1)} %collective-permute-done.14.d), custom_call_target="tpu_custom_call" | custom-call | tf_op jit(solution)/shard_map/finish/pallas_call | solution.py:273
  (24 shorter events, 0.4 us)
Async XLA Ops:
  2.2 0.7 %copy-start = (bf16[256,32]{0,1:T(8,128)(2,1)S(1)}, bf16[256,32]{0,1:T(8,128)(2,1)}, u32[]{:S(2)}) copy-start(bf16[256,32]{0,1:T(8,128)(2,1)} %param.11) | copy-start | bytes 49156
  6.9 4.1 %collective-permute-start = (f32[32,4096]{1,0:T(8,128)S(1)}, f32[32,4096]{1,0:T(8,128)S(1)}, u32[]{:S(2)}, u32[]{:S(2)}) collective-permute-start(f32[32,4096]{1,0:T(8,128)S(1)} %get-tuple-element.19), channel_id=1, source_target_pairs={{0,1},{1,0},{2,3},{3,2},{4,5},{5,4},{6,7},{7,6},{8,9},{9,8},{10,11... | collective-permute-start | bytes 1572872 | tf_op jit(solution)/shard_map/ppermute | solution.py:287
  11.0 27.6 %copy-start.1 = (s32[8192,16]{0,1:T(8,128)S(1)}, s32[8192,16]{0,1:T(8,128)}, u32[]{:S(2)}) copy-start(s32[8192,16]{0,1:T(8,128)} %param.9) | copy-start | bytes 1572868
  11.3 4.9 %collective-permute-start.2 = (f16[33,1024]{1,0:T(8,128)(2,1)S(1)}, f16[33,1024]{1,0:T(8,128)(2,1)S(1)}, u32[]{:S(2)}, u32[]{:S(2)}) collective-permute-start(f16[33,1024]{1,0:T(8,128)(2,1)S(1)} %pad_maximum_fusion.2), channel_id=1, source_target_pairs={{0,2},{1,3},{2,4},{3,5},{4,6},{5,7},{6,0},{7,1},{8,10},{9,11},{10,... | collective-permute-start | bytes 202760 | tf_op jit(solution)/shard_map/ppermute | solution.py:292
  13.6 7.6 %collective-permute-start.3 = (f16[33,1024]{1,0:T(8,128)(2,1)S(1)}, f16[33,1024]{1,0:T(8,128)(2,1)S(1)}, u32[]{:S(2)}, u32[]{:S(2)}) collective-permute-start(f16[33,1024]{1,0:T(8,128)(2,1)S(1)} %pad_maximum_fusion.3), channel_id=1, source_target_pairs={{0,6},{1,7},{2,0},{3,1},{4,2},{5,3},{6,4},{7,5},{8,14},{9,15},{10,... | collective-permute-start | bytes 202760 | tf_op jit(solution)/shard_map/ppermute | solution.py:292
  13.8 7.5 %collective-permute-start.1 = (f16[33,1024]{1,0:T(8,128)(2,1)S(1)}, f16[33,1024]{1,0:T(8,128)(2,1)S(1)}, u32[]{:S(2)}, u32[]{:S(2)}) collective-permute-start(f16[33,1024]{1,0:T(8,128)(2,1)S(1)} %pad_maximum_fusion.1), channel_id=1, source_target_pairs={{0,4},{1,5},{2,6},{3,7},{4,0},{5,1},{6,2},{7,3},{8,12},{9,13},{10,... | collective-permute-start | bytes 202760 | tf_op jit(solution)/shard_map/ppermute | solution.py:292
  21.5 8.4 %collective-permute-start.4 = (f16[33,1024]{1,0:T(8,128)(2,1)S(1)}, f16[33,1024]{1,0:T(8,128)(2,1)S(1)}, u32[]{:S(2)}, u32[]{:S(2)}) collective-permute-start(f16[33,1024]{1,0:T(8,128)(2,1)S(1)} %pad_maximum_fusion.4), channel_id=1, source_target_pairs={{0,8},{1,9},{2,10},{3,11},{4,12},{5,13},{6,14},{7,15},{8,0},{9,1},... | collective-permute-start | bytes 202760 | tf_op jit(solution)/shard_map/ppermute | solution.py:287
  30.0 4.3 %collective-permute-start.7 = (bf16[32,1024]{1,0:T(8,128)(2,1)S(1)}, bf16[32,1024]{1,0:T(8,128)(2,1)S(1)}, u32[]{:S(2)}, u32[]{:S(2)}) collective-permute-start(bf16[32,1024]{1,0:T(8,128)(2,1)S(1)} %fusion.1), channel_id=1, source_target_pairs={{0,2},{1,3},{2,4},{3,5},{4,6},{5,7},{6,0},{7,1},{8,10},{9,11},{10,... | collective-permute-start | bytes 196616 | tf_op jit(solution)/shard_map/ppermute | solution.py:292
  31.8 5.8 %collective-permute-start.6 = (bf16[32,1024]{1,0:T(8,128)(2,1)S(1)}, bf16[32,1024]{1,0:T(8,128)(2,1)S(1)}, u32[]{:S(2)}, u32[]{:S(2)}) collective-permute-start(bf16[32,1024]{1,0:T(8,128)(2,1)S(1)} %fusion.1), channel_id=1, source_target_pairs={{0,4},{1,5},{2,6},{3,7},{4,0},{5,1},{6,2},{7,3},{8,12},{9,13},{10,... | collective-permute-start | bytes 196616 | tf_op jit(solution)/shard_map/ppermute | solution.py:292
  32.6 5.7 %collective-permute-start.5 = (bf16[32,1024]{1,0:T(8,128)(2,1)S(1)}, bf16[32,1024]{1,0:T(8,128)(2,1)S(1)}, u32[]{:S(2)}, u32[]{:S(2)}) collective-permute-start(bf16[32,1024]{1,0:T(8,128)(2,1)S(1)} %fusion.1), channel_id=1, source_target_pairs={{0,6},{1,7},{2,0},{3,1},{4,2},{5,3},{6,4},{7,5},{8,14},{9,15},{10,... | collective-permute-start | bytes 196616 | tf_op jit(solution)/shard_map/ppermute | solution.py:292
  38.3 5.0 %collective-permute-start.8 = (bf16[32,4096]{1,0:T(8,128)(2,1)S(1)}, bf16[32,4096]{1,0:T(8,128)(2,1)S(1)}, u32[]{:S(2)}, u32[]{:S(2)}) collective-permute-start(bf16[32,4096]{1,0:T(8,128)(2,1)S(1)} %pad_maximum_fusion.sketch), channel_id=1, source_target_pairs={{0,1},{1,0},{2,3},{3,2},{4,5},{5,4},{6,7},{7,6},{8,9},{9,8},{10,11... | collective-permute-start | bytes 786440 | tf_op jit(solution)/shard_map/ppermute | solution.py:287
  48.2 5.2 %collective-permute-start.9 = (s16[368,128]{1,0:T(8,128)(2,1)S(1)}, s16[368,128]{1,0:T(8,128)(2,1)S(1)}, u32[]{:S(2)}, u32[]{:S(2)}) collective-permute-start(s16[368,128]{1,0:T(8,128)(2,1)S(1)} %get-tuple-element.24), channel_id=1, source_target_pairs={{0,16},{16,0},{32,48},{48,32},{64,80},{80,64},{96,112},{112,96},{1... | collective-permute-start | bytes 282632 | tf_op jit(solution)/shard_map/ppermute | solution.py:287
  49.6 8.1 %collective-permute-start.10 = (s16[368,128]{1,0:T(8,128)(2,1)S(1)}, s16[368,128]{1,0:T(8,128)(2,1)S(1)}, u32[]{:S(2)}, u32[]{:S(2)}) collective-permute-start(s16[368,128]{1,0:T(8,128)(2,1)S(1)} %get-tuple-element.25), channel_id=1, source_target_pairs={{0,32},{16,48},{32,0},{48,16},{64,96},{80,112},{96,64},{112,80},{1... | collective-permute-start | bytes 282632 | tf_op jit(solution)/shard_map/ppermute | solution.py:287
  52.5 7.1 %collective-permute-start.11 = (s16[368,128]{1,0:T(8,128)(2,1)S(1)}, s16[368,128]{1,0:T(8,128)(2,1)S(1)}, u32[]{:S(2)}, u32[]{:S(2)}) collective-permute-start(s16[368,128]{1,0:T(8,128)(2,1)S(1)} %get-tuple-element.26), channel_id=1, source_target_pairs={{0,48},{16,32},{32,16},{48,0},{64,112},{80,96},{96,80},{112,64},{1... | collective-permute-start | bytes 282632 | tf_op jit(solution)/shard_map/ppermute | solution.py:287
  59.9 5.9 %collective-permute-start.12 = (s16[112,128]{1,0:T(8,128)(2,1)S(1)}, s16[112,128]{1,0:T(8,128)(2,1)S(1)}, u32[]{:S(2)}, u32[]{:S(2)}) collective-permute-start(s16[112,128]{1,0:T(8,128)(2,1)S(1)} %get-tuple-element.28), channel_id=1, source_target_pairs={{0,64},{16,80},{32,96},{48,112},{64,128},{80,144},{96,160},{112,17... | collective-permute-start | bytes 86024 | tf_op jit(solution)/shard_map/ppermute | solution.py:292
  61.8 5.0 %collective-permute-start.13 = (s16[112,128]{1,0:T(8,128)(2,1)S(1)}, s16[112,128]{1,0:T(8,128)(2,1)S(1)}, u32[]{:S(2)}, u32[]{:S(2)}) collective-permute-start(s16[112,128]{1,0:T(8,128)(2,1)S(1)} %get-tuple-element.29), channel_id=1, source_target_pairs={{0,128},{16,144},{32,160},{48,176},{64,192},{80,208},{96,224},{112... | collective-permute-start | bytes 86024 | tf_op jit(solution)/shard_map/ppermute | solution.py:292
  63.8 3.9 %collective-permute-start.14 = (s16[112,128]{1,0:T(8,128)(2,1)S(1)}, s16[112,128]{1,0:T(8,128)(2,1)S(1)}, u32[]{:S(2)}, u32[]{:S(2)}) collective-permute-start(s16[112,128]{1,0:T(8,128)(2,1)S(1)} %get-tuple-element.30), channel_id=1, source_target_pairs={{0,192},{16,208},{32,224},{48,240},{64,0},{80,16},{96,32},{112,48}... | collective-permute-start | bytes 86024 | tf_op jit(solution)/shard_map/ppermute | solution.py:292

commit v5 on v4

v5 whole, which is shorter than its diff:
```python
import functools

import jax
import jax.numpy as jnp
from jax import lax
from jax.experimental import pallas as pl
from jax.experimental.pallas import tpu as pltpu
from jax.sharding import PartitionSpec as P

BINS = 256
LEAVES = 64
RIDGE = 1.0
F32 = jnp.float32
BF16 = jnp.bfloat16
BLOCK = 1024
CONTRACT_LAST = (((1,), (1,)), ((), ()))


BIN_GROUPS = [32] * 8 + [16, 32]
OWN_GROUPS = [16] * 6


def encoded_rows(groups):
    return sum(groups) + 16


def starts_of(groups):
    return [sum(groups[:g]) for g in range(len(groups))]


def encode_into(out, value, groups):
    rows = sum(groups)
    tops = [
        jnp.max(jnp.abs(value[at : at + size, :]), axis=0, keepdims=True) for at, size in zip(starts_of(groups), groups)
    ]
    tops.append(jnp.zeros((16 - len(groups), 128), F32))
    exponent = jnp.ceil(jnp.log2(jnp.maximum(jnp.concatenate(tops, axis=0), 1e-30)))
    scale = jnp.exp2(14.0 - exponent)
    for g, (at, size) in enumerate(zip(starts_of(groups), groups)):
        scaled = value[at : at + size, :] * scale[g : g + 1, :]
        out[at : at + size, :] = jnp.round(scaled).astype(jnp.int32).astype(jnp.int16)
    out[rows : rows + 16, :] = exponent.astype(jnp.int32).astype(jnp.int16)


def decode(code, groups):
    whole = code[...].astype(jnp.int32).astype(F32)
    scale = jnp.exp2(whole[sum(groups) :, :] - 14.0)
    parts = [
        whole[at : at + size, :] * scale[g : g + 1, :] for g, (at, size) in enumerate(zip(starts_of(groups), groups))
    ]
    return jnp.concatenate(parts, axis=0)


def cells_place(block):
    return pl.multiple_of(cells_of(block) // 128, BLOCK // 128)


def one_row(tile):
    return jnp.concatenate([tile[r : r + 1, :] for r in range(tile.shape[0])], axis=1)


def cells_of(block):
    out_at = lax.axis_index("out")
    place = ((out_at & 1) ^ (block // 4)) * 4 + (((out_at >> 1) + block % 4) & 3)
    return pl.multiple_of(place * BLOCK, BLOCK)


def relative(value, size):
    rows_at = lax.axis_index("rows")
    return ((value - (rows_at >> 2) * (4 * size)) & (16 * size - 1)) ^ ((rows_at & 3) * size)


def gradient_kernel(
    pred, targ, weight_far, leaf_far, matrix_far, sketch_out, leaf_out,
    pred_here, targ_here, weight, leaf, matrix_t, sums, weights, weight_wide, arrived, small_arrived, *, blocks,
):
    small = [
        pltpu.make_async_copy(far, here, small_arrived.at[n])
        for n, (far, here) in enumerate([(weight_far, weight), (leaf_far, leaf), (matrix_far, matrix_t)])
    ]
    for copy in small:
        copy.start()
    copies = []
    for n, block in enumerate(blocks):
        rows = pl.ds(cells_of(block), BLOCK)
        pair = [
            pltpu.make_async_copy(pred.at[rows, :], pred_here.at[n], arrived.at[0, n]),
            pltpu.make_async_copy(targ.at[rows, :], targ_here.at[n], arrived.at[1, n]),
        ]
        for copy in pair:
            copy.start()
        copies.append(pair)
    for copy in small:
        copy.wait()
    weight_wide[...] = weight[...].astype(F32)
    for n, block in enumerate(blocks):
        tile = pl.ds(cells_place(block), BLOCK // 128)
        w_tile = weight_wide[tile, :]
        own = relative(one_row(leaf[tile, :]), 4)
        place = ((own >> 2) & 3) * 16 + (own >> 4) * 4 + (own & 3)
        onehot = jnp.where(lax.broadcasted_iota(jnp.int32, (LEAVES, BLOCK), 0) == place, 1.0, 0.0).astype(BF16)
        w_cols = jnp.transpose(w_tile)
        for copy in copies[n]:
            copy.wait()
        pieces = []
        for s in range(BLOCK // 128):
            rows = slice(128 * s, 128 * s + 128)
            diff = pred_here[n, rows, :].astype(F32) - targ_here[n, rows, :].astype(F32)
            pieces.append((w_cols[:, s : s + 1] * diff).astype(BF16))
        gradient = jnp.concatenate(pieces, axis=0)
        sketch_out[:, n * BLOCK : n * BLOCK + BLOCK] = lax.dot_general(
            matrix_t[...], gradient, CONTRACT_LAST, preferred_element_type=F32
        )
        added = jnp.dot(onehot, gradient, preferred_element_type=F32)
        w_rows = jnp.broadcast_to(one_row(w_tile).astype(BF16), (16, BLOCK))
        w_added = lax.dot_general(onehot, w_rows, CONTRACT_LAST, preferred_element_type=F32)
        if n == 0:
            sums[...] = added
            weights[...] = w_added
        else:
            sums[...] += added
            weights[...] += w_added
    for y in range(4):
        for z in range(4):
            top = 16 * y + 4 * z
            for h in range(2):
                at = 8 * z + 4 * h
                leaf_out[y, at : at + 4, :] = sums[top : top + 4, 128 * h : 128 * h + 128]
        leaf_out[y, 32:48, :] = jnp.broadcast_to(weights[16 * y : 16 * y + 16, 0:1], (16, 128))


def gradient(pred, targ, weight, leaf, matrix_t, blocks, room):
    genes = pred.shape[1]
    count = len(blocks)
    whole = pl.BlockSpec(memory_space=pltpu.VMEM)
    return pl.pallas_call(
        functools.partial(gradient_kernel, blocks=blocks),
        in_specs=[pl.BlockSpec(memory_space=pl.ANY)] * 5,
        out_specs=[whole, whole],
        scratch_shapes=[
            pltpu.VMEM((count, BLOCK, genes), BF16),
            pltpu.VMEM((count, BLOCK, genes), BF16),
            pltpu.VMEM(weight.shape, weight.dtype),
            pltpu.VMEM(leaf.shape, leaf.dtype),
            pltpu.VMEM(matrix_t.shape, matrix_t.dtype),
            pltpu.VMEM((LEAVES, genes), F32),
            pltpu.VMEM((LEAVES, 16), F32),
            pltpu.VMEM(weight.shape, F32),
            pltpu.SemaphoreType.DMA((2, count)),
            pltpu.SemaphoreType.DMA((3,)),
        ],
        out_shape=[
            jax.ShapeDtypeStruct((matrix_t.shape[0], count * BLOCK), F32),
            jax.ShapeDtypeStruct((4, 48, 128), F32),
        ],
        compiler_params=pltpu.CompilerParams(vmem_limit_bytes=room * 1024 * 1024),
        cost_estimate=pl.CostEstimate(flops=count * 500000000, bytes_accessed=count * 1500000, transcendentals=0),
        name="gradient",
    )(pred, targ, weight, leaf, matrix_t)


def histogram_products(feat, sketch, weight, weight_wide, blocks):
    wide = len(blocks) * BLOCK
    places = [pl.ds(cells_of(block), BLOCK) for block in blocks]
    sketch_all = sketch[...]
    weight_wide[...] = weight[...].astype(F32)
    tiles = [weight_wide[pl.ds(cells_place(block), BLOCK // 128), :] for block in blocks]
    w_row = jnp.concatenate([one_row(tile) for tile in tiles], axis=1)
    w_all = jnp.broadcast_to(w_row.astype(BF16), (16, wide))
    rows128 = lax.broadcasted_iota(jnp.int32, (128, wide), 0).astype(BF16)
    rows16 = lax.broadcasted_iota(jnp.int32, (16, wide), 0).astype(BF16)
    zero = jnp.zeros((), BF16)
    one = jnp.ones((), BF16)
    for f in range(16):
        own = relative(jnp.concatenate([feat[f : f + 1, place] for place in places], axis=1), 16)
        low = (own & 127).astype(F32).astype(BF16)
        top = own >> 7
        group = jnp.broadcast_to(top.astype(F32).astype(BF16), (32, wide))
        left = jnp.where(rows128 == low, one, zero)
        spot = (top * 8 + (f % 8)).astype(F32).astype(BF16)
        right = jnp.concatenate(
            [
                jnp.where(group == zero, sketch_all, zero),
                jnp.where(group == zero, zero, sketch_all),
                jnp.where(rows16 == spot, w_all, zero),
            ],
            axis=0,
        )
        yield f, lax.dot_general(left, right, CONTRACT_LAST, preferred_element_type=F32)


def histogram_part_kernel(feat, sketch, weight, *refs, blocks):
    held, hess, weight_wide = refs[-3:]
    before = refs[:-3]
    if before:
        hess[...] = before[1][...]
    for f, both in histogram_products(feat, sketch, weight, weight_wide, blocks):
        held[f] = both[:, 0:64] + before[0][f] if before else both[:, 0:64]
        if f % 8 == 0 and not before:
            hess[f // 8] = both[:, 64:80]
        else:
            hess[f // 8] += both[:, 64:80]


def histogram_last_kernel(
    feat, sketch, weight, held, hess_in, leaf_a, leaf_b, leaf_c, o0, o1, o2, o3, hess, s1, s2, s3, weight_wide, *, blocks
):
    targets = (o0, s1, s2, s3)
    hess[...] = hess_in[...]
    for f, both in histogram_products(feat, sketch, weight, weight_wide, blocks):
        total = held[f] + both[:, 0:64]
        for y in range(4):
            lanes = [total[16 * y : 16 * y + 16, :], total[64 + 16 * y : 80 + 16 * y, :]]
            targets[y][16 * f : 16 * f + 16, :] = jnp.concatenate(lanes, axis=1)
        hess[f // 8] += both[:, 64:80]
    for y in range(4):
        near, far = slice(16 * y, 16 * y + 16), slice(64 + 16 * y, 80 + 16 * y)
        lanes = [
            hess[g, (far if z & 1 else near), 8 * (z >> 1) : 8 * (z >> 1) + 8] for z in range(4) for g in range(2)
        ]
        leaf_part = leaf_a[y] + leaf_b[y] + leaf_c[y]
        targets[y][256:272, :] = jnp.concatenate(lanes + [leaf_part[32:48, 64:128]], axis=1)
        targets[y][272:304, :] = leaf_part[0:32, :]
        if y:
            encode_into((o1, o2, o3)[y - 1], targets[y][...], BIN_GROUPS)


def histogram_options(blocks):
    return dict(
        compiler_params=pltpu.CompilerParams(vmem_limit_bytes=24 * 1024 * 1024),
        cost_estimate=pl.CostEstimate(
            flops=len(blocks) * 1024 * 4096 * 256, bytes_accessed=len(blocks) * 300000, transcendentals=0
        ),
        name="histogram",
    )


def histogram_part(feat_t, sketch, weight, before, blocks):
    return pl.pallas_call(
        functools.partial(histogram_part_kernel, blocks=blocks),
        scratch_shapes=[pltpu.VMEM(weight.shape, F32)],
        out_shape=[jax.ShapeDtypeStruct((16, 128, 64), F32), jax.ShapeDtypeStruct((2, 128, 16), F32)],
        **histogram_options(blocks),
    )(feat_t, sketch, weight, *before)


def histogram_last(feat_t, sketch, weight, before, leaf_parts, blocks):
    return pl.pallas_call(
        functools.partial(histogram_last_kernel, blocks=blocks),
        scratch_shapes=[pltpu.VMEM((2, 128, 16), F32)] + [pltpu.VMEM((304, 128), F32)] * 3
        + [pltpu.VMEM(weight.shape, F32)],
        out_shape=[jax.ShapeDtypeStruct((304, 128), F32)]
        + [jax.ShapeDtypeStruct((encoded_rows(BIN_GROUPS), 128), jnp.int16)] * 3,
        **histogram_options(blocks),
    )(feat_t, sketch, weight, *before, *leaf_parts)


def regroup_kernel(a, b, c, d, o0, o1, o2, o3):
    codes = (o1, o2, o3)
    total = a[...] + decode(b, BIN_GROUPS) + decode(c, BIN_GROUPS) + decode(d, BIN_GROUPS)
    for z in range(4):
        lane = 64 * (z & 1) + 32 * (z >> 1)
        leaf_weights = jnp.concatenate([total[256 + 4 * z : 260 + 4 * z, 64:128]] * 4, axis=0)
        value = jnp.concatenate(
            [
                jnp.concatenate([total[64 * q : 64 * q + 64, lane : lane + 32] for q in range(4)], axis=1),
                jnp.concatenate(
                    [total[256:272, 16 * z : 16 * z + 16], jnp.zeros((16, 48), F32), leaf_weights], axis=1
                ),
                total[272 + 8 * z : 280 + 8 * z, :],
                jnp.zeros((8, 128), F32),
            ],
            axis=0,
        )
        if z:
            encode_into(codes[z - 1], value, OWN_GROUPS)
        else:
            o0[...] = value


def regroup(a, b, c, d):
    return pl.pallas_call(
        regroup_kernel,
        out_shape=[jax.ShapeDtypeStruct((96, 128), F32)]
        + [jax.ShapeDtypeStruct((encoded_rows(OWN_GROUPS), 128), jnp.int16)] * 3,
        compiler_params=pltpu.CompilerParams(vmem_limit_bytes=8 * 1024 * 1024),
        name="regroup",
    )(a, b, c, d)


def finish_kernel(a, b, c, d, grad_out, hess_out, leaf_out, rows, *, per_bin):
    total = a[...] + decode(b, OWN_GROUPS) + decode(c, OWN_GROUPS) + decode(d, OWN_GROUPS)
    for q in range(4):
        rows[64 * q : 64 * q + 64, 0:32] = total[0:64, 32 * q : 32 * q + 32]
    for i in range(16):
        grad_out[i] = rows[pl.ds(i, 16, stride=16), :][:, 0:32]
    hess_out[...] = total[64:80, 0:16] / per_bin
    values = -total[80:88, :] / (total[64:72, 64:65] + RIDGE)
    leaf_out[:, 0:128] = values[0:4]
    leaf_out[:, 128:256] = values[4:8]


def finish(a, b, c, d, per_bin):
    return pl.pallas_call(
        functools.partial(finish_kernel, per_bin=per_bin),
        out_shape=[
            jax.ShapeDtypeStruct((16, 16, 32), F32),
            jax.ShapeDtypeStruct((16, 16), F32),
            jax.ShapeDtypeStruct((4, 256), F32),
        ],
        scratch_shapes=[pltpu.VMEM((256, 128), F32)],
        compiler_params=pltpu.CompilerParams(vmem_limit_bytes=8 * 1024 * 1024),
        name="finish",
    )(a, b, c, d)


def swap(value, axis, flip):
    return lax.ppermute(value, axis, [(i, i ^ flip) for i in range(16)])


def shift(value, axis, unit, step):
    place = lambda i: (i // unit) % 4
    return lax.ppermute(
        value, axis, [(i, i + ((place(i) + step) % 4 - place(i)) * unit) for i in range(16)]
    )


def pack(value):
    top = jnp.max(jnp.abs(value), axis=0, keepdims=True)
    exponent = jnp.ceil(jnp.log2(jnp.maximum(top, 1e-30)))
    return jnp.concatenate([value * jnp.exp2(-exponent), exponent], axis=0).astype(jnp.float16)


def unpack(code):
    whole = code.astype(F32)
    return whole[:-1] * jnp.exp2(whole[-1:])


def per_device(predictions, targets, row_weight, features, leaf, sketch_matrix):
    cells = predictions.shape[0]
    weight = row_weight.reshape(cells // 128, 128)
    features_t = features.T
    args = (predictions, targets, weight, leaf.reshape(cells // 128, 128), sketch_matrix.T)
    other, leaf_a = gradient(*args, [5, 6, 7, 4], 58)
    arrived = swap(other, "out", 1)
    mine, leaf_b = gradient(*args, [1, 2, 3], 51)
    chip = mine + arrived[:, : 3 * BLOCK]
    codes = [pack(chip[:, BLOCK * (j - 1) : BLOCK * j]) for j in (2, 1, 3)]
    codes, matrix_t = lax.optimization_barrier((codes, args[-1]))
    far = [unpack(shift(code, "out", 2, j)) for code, j in zip(codes, (2, 1, 3))]
    last, leaf_c = gradient(*args[:-1], matrix_t, [0], 51)
    part = last + arrived[:, 3 * BLOCK :] + far[0] + far[1] + far[2]
    own = (part + unpack(swap(pack(part), "out", 8))).astype(BF16)
    held = histogram_part(features_t, own, weight, [], [0])
    near = jnp.concatenate([shift(own, "out", 2, -j) for j in (1, 2, 3)], axis=1)
    across = swap(jnp.concatenate([own, near], axis=1), "out", 1)
    held = histogram_part(features_t, near, weight, held, [1, 2, 3])
    slices = histogram_last(features_t, across, weight, held, (leaf_a, leaf_b, leaf_c), [4, 5, 6, 7])
    slices = regroup(slices[0], *[swap(slices[j], "rows", j) for j in (1, 2, 3)])
    return tuple(
        finish(slices[0], *[shift(slices[j], "rows", 4, j) for j in (1, 2, 3)], float(cells * 16 // BINS))
    )


def solution(mesh):
    return jax.shard_map(
        per_device,
        mesh=mesh,
        in_specs=(
            P("rows", "out"),
            P("rows", "out"),
            P("rows"),
            P("rows", "out"),
            P("rows"),
            P("out", None),
        ),
        out_specs=(P("rows", "out", None), P("rows", "out"), P("rows", "out")),
        check_vma=False,
    )
```

time: 68.7 us -> 64.9 us (0.945)
  waiting for transfers between devices: 22.4 us -> 17.4 us
  Pallas kernels: 18.5 us -> 20.8 us
  other arithmetic: 2.05 us -> 0.51 us
  local copies, waits for them, and re-layouts: 0.75 us -> 0.06 us
    ppermute x9, waiting for transfers between devices: 12.9 us -> 8.72 us  [shift(): lax.ppermute(value, axis, [(i, i + ((place(i) + step) % 4 - place(i)) * u...]
    pallas_call x4 -> x6, Pallas kernels: 17.5 us -> 19.8 us  [the longest x3 9.96 us: gradient(): pl.pallas_call(functools.partial(gradient_kernel, blocks=blocks), in_spec...]
    ppermute x6, starting transfers between devices: 10.7 us -> 12.4 us  [swap(): return lax.ppermute(value, axis, [(i, i ^ flip) for i in range(16)])]
    ppermute x9, starting transfers between devices: 13 us -> 11.9 us  [shift(): lax.ppermute(value, axis, [(i, i + ((place(i) + step) % 4 - place(i)) * u...]
    ppermute x6, waiting for transfers between devices: 9.54 us -> 8.63 us  [swap(): return lax.ppermute(value, axis, [(i, i ^ flip) for i in range(16)])]
    another operation x4 -> x2, other arithmetic: 0.84 us -> 0.06 us  [the longest x2 0.79 us: per_device(): per_cell = jnp.stack([row_weight.astype(F32), leaf.astype(F32)])]
    convert_element_type x1 -> x0, other arithmetic: 0.76 us -> none  [per_device(): per_cell = jnp.stack([row_weight.astype(F32), leaf.astype(F32)])]
    unnamed x4 -> x10, local copies, waits for them, and re-layouts: 0.72 us -> 0.03 us
  transfers between devices with their start and end apart: 15 -> 15, of which waited for: 11 -> 12; matrix products, arithmetic and copies ran while one was open for 0% -> 0% of each run, Pallas kernels for 13% -> 15%
where the time goes in v5:
time: 64.9 us; the launch traced here: 64 us
  starting transfers between devices  24.3 us (37%)
  Pallas kernels  20.8 us (32%)
  waiting for transfers between devices  17.4 us (27%)
  between operations  0.97 us (1%)
    ppermute x6, starting transfers between devices, swap(): return lax.ppermute(value, axis, [(i, i ^ flip) for i in range(16)])  12.4 us
    ppermute x9, starting transfers between devices, shift(): lax.ppermute(value, axis, [(i, i + ((place(i) + step) % 4 - place(i)) * u...  11.9 us
    pallas_call x3, Pallas kernels, gradient(): pl.pallas_call(functools.partial(gradient_kernel, blocks=blocks), in_spec...  9.96 us
    ppermute x9, waiting for transfers between devices, shift(): lax.ppermute(value, axis, [(i, i + ((place(i) + step) % 4 - place(i)) * u...  8.72 us
    ppermute x6, waiting for transfers between devices, swap(): return lax.ppermute(value, axis, [(i, i ^ flip) for i in range(16)])  8.63 us
    pallas_call x2, Pallas kernels, histogram_part(): pl.pallas_call(functools.partial(histogram_part_kernel, blocks=blocks), s...  5.01 us
    pallas_call x1, Pallas kernels, histogram_last(): pl.pallas_call(functools.partial(histogram_last_kernel, blocks=blocks), s...  4.82 us
  transfers between devices with their start and end apart: 15, of which 12 were waited for; matrix products, arithmetic and copies ran while one was open for 0% of the time, Pallas kernels for 15%

profile of v5, /device:TPU:6, one launch (start us, length us, event | category | flops | bytes accessed | tf_op | source)
XLA Modules:
  0.0 64.0 jit_solution(7270100809311902518)
XLA Ops:
  0.6 0.0 copy-start
  0.6 0.0 copy-start.1
  0.7 5.2 %gradient.4 = (f32[32,4096]{1,0:T(8,128)}, f32[4,48,128]{2,1,0:T(8,128)}) custom-call(bf16[8192,256]{1,0:T(8,128)(2,1)} %pred_.5, bf16[8192,256]{1,0:T(8,128)(2,1)} %targ.5, bf16[64,128]{1,0:T(8,128)(2,1)} %bitcast.14, s32[64,128]{1,0:T(8,128)} %bitcast.8, bf16[32,256]{1,0:T(8,128)(2,1)} %bitcast.11), custom_call_target="tpu_custom_call" | custom-call | flops 2000000000 | bytes 6000000 | tf_op jit(solution)/shard_map/gradient/pallas_call | solution.py:136
  5.8 0.1 collective-permute-start
  5.9 0.0 copy-done
  5.9 0.0 copy-done.1
  5.9 0.0 copy-done.2
  5.9 2.9 %gradient.3 = (f32[32,3072]{1,0:T(8,128)S(1)}, f32[4,48,128]{2,1,0:T(8,128)S(1)}) custom-call(bf16[8192,256]{1,0:T(8,128)(2,1)} %pred_.5, bf16[8192,256]{1,0:T(8,128)(2,1)} %targ.5, bf16[64,128]{1,0:T(8,128)(2,1)S(1)} %bitcast.15, s32[64,128]{1,0:T(8,128)S(1)} %bitcast.9, bf16[32,256]{1,0:T(8,128)(2,1)S(1)} %bitcast.12), custom_call_target="tpu_custom_call" | custom-call | flops 1500000000 | bytes 4500000 | tf_op jit(solution)/shard_map/gradient/pallas_call | solution.py:136
  8.9 0.0 collective-permute-done
  9.2 0.0 copy-start.3
  9.2 1.5 %collective-permute-start.1 = (f16[33,1024]{1,0:T(8,128)(2,1)S(1)}, f16[33,1024]{1,0:T(8,128)(2,1)S(1)}, u32[]{:S(2)}, u32[]{:S(2)}) collective-permute-start(f16[33,1024]{1,0:T(8,128)(2,1)S(1)} %pad_maximum_fusion.2), channel_id=1, source_target_pairs={{0,4},{1,5},{2,6},{3,7},{4,0},{5,1},{6,2},{7,3},{8,12},{9,13},{10,... | collective-permute-start | bytes 202760 | tf_op jit(solution)/shard_map/ppermute | solution.py:323
  10.7 2.1 %collective-permute-start.2 = (f16[33,1024]{1,0:T(8,128)(2,1)S(1)}, f16[33,1024]{1,0:T(8,128)(2,1)S(1)}, u32[]{:S(2)}, u32[]{:S(2)}) collective-permute-start(f16[33,1024]{1,0:T(8,128)(2,1)S(1)} %pad_maximum_fusion.3), channel_id=1, source_target_pairs={{0,2},{1,3},{2,4},{3,5},{4,6},{5,7},{6,0},{7,1},{8,10},{9,11},{10,... | collective-permute-start | bytes 202760 | tf_op jit(solution)/shard_map/ppermute | solution.py:323
  12.8 0.0 collective-permute-start.3
  12.8 1.9 %gradient.5 = (f32[32,1024]{1,0:T(8,128)S(1)}, f32[4,48,128]{2,1,0:T(8,128)S(1)}) custom-call(bf16[8192,256]{1,0:T(8,128)(2,1)} %pred_.5, bf16[8192,256]{1,0:T(8,128)(2,1)} %targ.5, bf16[64,128]{1,0:T(8,128)(2,1)S(1)} %bitcast.16, s32[64,128]{1,0:T(8,128)S(1)} %bitcast.10, bf16[32,256]{1,0:T(8,128)(2,1)S(1)} %bitcast.13), custom_call_target="tpu_custom_call" | custom-call | flops 500000000 | bytes 1500000 | tf_op jit(solution)/shard_map/gradient/pallas_call | solution.py:136
  14.7 1.2 %collective-permute-done.1 = f16[33,1024]{1,0:T(8,128)(2,1)S(1)} collective-permute-done((f16[33,1024]{1,0:T(8,128)(2,1)S(1)}, f16[33,1024]{1,0:T(8,128)(2,1)S(1)}, u32[]{:S(2)}, u32[]{:S(2)}) %collective-permute-start.1) | collective-permute-done | bytes 67616 | tf_op jit(solution)/shard_map/ppermute | solution.py:323
  16.0 0.9 %collective-permute-done.2 = f16[33,1024]{1,0:T(8,128)(2,1)S(1)} collective-permute-done((f16[33,1024]{1,0:T(8,128)(2,1)S(1)}, f16[33,1024]{1,0:T(8,128)(2,1)S(1)}, u32[]{:S(2)}, u32[]{:S(2)}) %collective-permute-start.2) | collective-permute-done | bytes 67616 | tf_op jit(solution)/shard_map/ppermute | solution.py:323
  16.9 1.6 %collective-permute-done.3 = f16[33,1024]{1,0:T(8,128)(2,1)S(1)} collective-permute-done((f16[33,1024]{1,0:T(8,128)(2,1)S(1)}, f16[33,1024]{1,0:T(8,128)(2,1)S(1)}, u32[]{:S(2)}, u32[]{:S(2)}) %collective-permute-start.3) | collective-permute-done | bytes 67616 | tf_op jit(solution)/shard_map/ppermute | solution.py:323
  18.5 0.1 abs_reduce_fusion
  18.7 7.3 %collective-permute-start.4 = (f16[33,1024]{1,0:T(8,128)(2,1)S(1)}, f16[33,1024]{1,0:T(8,128)(2,1)S(1)}, u32[]{:S(2)}, u32[]{:S(2)}) collective-permute-start(f16[33,1024]{1,0:T(8,128)(2,1)S(1)} %pad_maximum_fusion.5), channel_id=1, source_target_pairs={{0,8},{1,9},{2,10},{3,11},{4,12},{5,13},{6,14},{7,15},{8,0},{9,1},... | collective-permute-start | bytes 202760 | tf_op jit(solution)/shard_map/ppermute | solution.py:318
  25.9 2.5 %collective-permute-done.4 = f16[33,1024]{1,0:T(8,128)(2,1)S(1)} collective-permute-done((f16[33,1024]{1,0:T(8,128)(2,1)S(1)}, f16[33,1024]{1,0:T(8,128)(2,1)S(1)}, u32[]{:S(2)}, u32[]{:S(2)}) %collective-permute-start.4) | collective-permute-done | bytes 67616 | tf_op jit(solution)/shard_map/ppermute | solution.py:318
  28.5 0.4 collective-permute-start.7
  28.9 1.2 %collective-permute-start.6 = (bf16[32,1024]{1,0:T(8,128)(2,1)S(1)}, bf16[32,1024]{1,0:T(8,128)(2,1)S(1)}, u32[]{:S(2)}, u32[]{:S(2)}) collective-permute-start(bf16[32,1024]{1,0:T(8,128)(2,1)S(1)} %fusion.1.sketch), channel_id=1, source_target_pairs={{0,4},{1,5},{2,6},{3,7},{4,0},{5,1},{6,2},{7,3},{8,12},{9,13},{10,... | collective-permute-start | bytes 196616 | tf_op jit(solution)/shard_map/ppermute | solution.py:323
  30.1 0.9 %collective-permute-start.5 = (bf16[32,1024]{1,0:T(8,128)(2,1)S(1)}, bf16[32,1024]{1,0:T(8,128)(2,1)S(1)}, u32[]{:S(2)}, u32[]{:S(2)}) collective-permute-start(bf16[32,1024]{1,0:T(8,128)(2,1)S(1)} %fusion.1.sketch), channel_id=1, source_target_pairs={{0,6},{1,7},{2,0},{3,1},{4,2},{5,3},{6,4},{7,5},{8,14},{9,15},{10,... | collective-permute-start | bytes 196616 | tf_op jit(solution)/shard_map/ppermute | solution.py:323
  31.0 0.0 copy-done.3
  31.0 1.4 %histogram.3 = (f32[16,128,64]{2,1,0:T(8,128)S(1)}, f32[2,128,16]{2,1,0:T(8,128)S(1)}) custom-call(s32[16,8192]{1,0:T(8,128)S(1)} %bitcast.20, bf16[32,1024]{1,0:T(8,128)(2,1)S(1)} %fusion.1.sketch, bf16[64,128]{1,0:T(8,128)(2,1)S(1)} %bitcast.17), custom_call_target="tpu_custom_call" | custom-call | flops 1073741824 | bytes 300000 | tf_op jit(solution)/shard_map/histogram/pallas_call | solution.py:239
  32.4 0.5 collective-permute-done.7
  32.9 1.8 %collective-permute-done.6 = bf16[32,1024]{1,0:T(8,128)(2,1)S(1)} collective-permute-done((bf16[32,1024]{1,0:T(8,128)(2,1)S(1)}, bf16[32,1024]{1,0:T(8,128)(2,1)S(1)}, u32[]{:S(2)}, u32[]{:S(2)}) %collective-permute-start.6) | collective-permute-done | bytes 65568 | tf_op jit(solution)/shard_map/ppermute | solution.py:323
  34.7 0.9 %collective-permute-done.5 = bf16[32,1024]{1,0:T(8,128)(2,1)S(1)} collective-permute-done((bf16[32,1024]{1,0:T(8,128)(2,1)S(1)}, bf16[32,1024]{1,0:T(8,128)(2,1)S(1)}, u32[]{:S(2)}, u32[]{:S(2)}) %collective-permute-start.5) | collective-permute-done | bytes 65568 | tf_op jit(solution)/shard_map/ppermute | solution.py:323
  35.6 0.3 collective-permute-start.8
  35.9 0.0 copy-start.4
  35.9 3.6 %histogram.4 = (f32[16,128,64]{2,1,0:T(8,128)S(1)}, f32[2,128,16]{2,1,0:T(8,128)S(1)}) custom-call(s32[16,8192]{1,0:T(8,128)S(1)} %bitcast.21, bf16[32,3072]{1,0:T(8,128)(2,1)S(1)} %pad_maximum_fusion.1.sketch, bf16[64,128]{1,0:T(8,128)(2,1)S(1)} %bitcast.18, f32[16,128,64]{2,1,0:T(8,128)S(1)} %get-tuple-element.32.refs_0_, ...), custom_call_target="tpu_custom_call" | custom-call | flops 3221225472 | bytes 900000 | tf_op jit(solution)/shard_map/histogram/pallas_call | solution.py:239
  39.5 0.0 collective-permute-done.8.sketch
  39.5 0.0 copy-done.4
  39.5 4.8 %histogram.5 = (f32[304,128]{1,0:T(8,128)S(1)}, s16[320,128]{1,0:T(8,128)(2,1)S(1)}, s16[320,128]{1,0:T(8,128)(2,1)S(1)}, s16[320,128]{1,0:T(8,128)(2,1)S(1)}) custom-call(s32[16,8192]{1,0:T(8,128)S(1)} %bitcast.22, bf16[32,4096]{1,0:T(8,128)(2,1)S(1)} %collective-permute-done.8.sketch, bf16[64,128]{1,0:T(8,128)(2,1)S(1)} %bitcast.19, ...), custom_call_target="tpu_custom_call" | custom-call | flops 4294967296 | bytes 1200000 | tf_op jit(solution)/shard_map/histogram/pallas_call | solution.py:248
  44.4 1.7 %collective-permute-start.9 = (s16[320,128]{1,0:T(8,128)(2,1)S(1)}, s16[320,128]{1,0:T(8,128)(2,1)S(1)}, u32[]{:S(2)}, u32[]{:S(2)}) collective-permute-start(s16[320,128]{1,0:T(8,128)(2,1)S(1)} %get-tuple-element.40), channel_id=1, source_target_pairs={{0,16},{16,0},{32,48},{48,32},{64,80},{80,64},{96,112},{112,96},{1... | collective-permute-start | bytes 245768 | tf_op jit(solution)/shard_map/ppermute | solution.py:318
  46.0 2.9 %collective-permute-start.10 = (s16[320,128]{1,0:T(8,128)(2,1)S(1)}, s16[320,128]{1,0:T(8,128)(2,1)S(1)}, u32[]{:S(2)}, u32[]{:S(2)}) collective-permute-start(s16[320,128]{1,0:T(8,128)(2,1)S(1)} %get-tuple-element.41), channel_id=1, source_target_pairs={{0,32},{16,48},{32,0},{48,16},{64,96},{80,112},{96,64},{112,80},{1... | collective-permute-start | bytes 245768 | tf_op jit(solution)/shard_map/ppermute | solution.py:318
  48.9 0.2 collective-permute-start.11
  49.1 0.1 collective-permute-done.9.b
  49.3 4.3 %collective-permute-done.10.c = s16[320,128]{1,0:T(8,128)(2,1)S(1)} collective-permute-done((s16[320,128]{1,0:T(8,128)(2,1)S(1)}, s16[320,128]{1,0:T(8,128)(2,1)S(1)}, u32[]{:S(2)}, u32[]{:S(2)}) %collective-permute-start.10) | collective-permute-done | bytes 81952 | tf_op jit(solution)/shard_map/ppermute | solution.py:318
  53.6 1.7 %collective-permute-done.11.d = s16[320,128]{1,0:T(8,128)(2,1)S(1)} collective-permute-done((s16[320,128]{1,0:T(8,128)(2,1)S(1)}, s16[320,128]{1,0:T(8,128)(2,1)S(1)}, u32[]{:S(2)}, u32[]{:S(2)}) %collective-permute-start.11) | collective-permute-done | bytes 81952 | tf_op jit(solution)/shard_map/ppermute | solution.py:318
  55.2 0.2 regroup.1
  55.5 1.9 %collective-permute-start.12 = (s16[112,128]{1,0:T(8,128)(2,1)S(1)}, s16[112,128]{1,0:T(8,128)(2,1)S(1)}, u32[]{:S(2)}, u32[]{:S(2)}) collective-permute-start(s16[112,128]{1,0:T(8,128)(2,1)S(1)} %get-tuple-element.44), channel_id=1, source_target_pairs={{0,64},{16,80},{32,96},{48,112},{64,128},{80,144},{96,160},{112,17... | collective-permute-start | bytes 86024 | tf_op jit(solution)/shard_map/ppermute | solution.py:323
  57.4 2.0 %collective-permute-start.13 = (s16[112,128]{1,0:T(8,128)(2,1)S(1)}, s16[112,128]{1,0:T(8,128)(2,1)S(1)}, u32[]{:S(2)}, u32[]{:S(2)}) collective-permute-start(s16[112,128]{1,0:T(8,128)(2,1)S(1)} %get-tuple-element.45), channel_id=1, source_target_pairs={{0,128},{16,144},{32,160},{48,176},{64,192},{80,208},{96,224},{112... | collective-permute-start | bytes 86024 | tf_op jit(solution)/shard_map/ppermute | solution.py:323
  59.4 2.0 %collective-permute-start.14 = (s16[112,128]{1,0:T(8,128)(2,1)S(1)}, s16[112,128]{1,0:T(8,128)(2,1)S(1)}, u32[]{:S(2)}, u32[]{:S(2)}) collective-permute-start(s16[112,128]{1,0:T(8,128)(2,1)S(1)} %get-tuple-element.46), channel_id=1, source_target_pairs={{0,192},{16,208},{32,224},{48,240},{64,0},{80,16},{96,32},{112,48}... | collective-permute-start | bytes 86024 | tf_op jit(solution)/shard_map/ppermute | solution.py:323
  61.4 0.0 collective-permute-done.12.b
  61.4 0.9 %collective-permute-done.13.c = s16[112,128]{1,0:T(8,128)(2,1)S(1)} collective-permute-done((s16[112,128]{1,0:T(8,128)(2,1)S(1)}, s16[112,128]{1,0:T(8,128)(2,1)S(1)}, u32[]{:S(2)}, u32[]{:S(2)}) %collective-permute-start.13) | collective-permute-done | bytes 28704 | tf_op jit(solution)/shard_map/ppermute | solution.py:323
  62.3 1.0 %collective-permute-done.14.d = s16[112,128]{1,0:T(8,128)(2,1)S(1)} collective-permute-done((s16[112,128]{1,0:T(8,128)(2,1)S(1)}, s16[112,128]{1,0:T(8,128)(2,1)S(1)}, u32[]{:S(2)}, u32[]{:S(2)}) %collective-permute-start.14) | collective-permute-done | bytes 28704 | tf_op jit(solution)/shard_map/ppermute | solution.py:323
  63.2 0.8 %finish.1 = (f32[16,16,32]{2,1,0:T(8,128)}, f32[16,16]{1,0:T(8,128)}, f32[4,256]{1,0:T(4,128)}) custom-call(f32[96,128]{1,0:T(8,128)S(1)} %get-tuple-element.43.a, s16[112,128]{1,0:T(8,128)(2,1)S(1)} %collective-permute-done.12.b, s16[112,128]{1,0:T(8,128)(2,1)S(1)} %collective-permute-done.13.c, s16[112,128]{1,0:T(8,128)(2,1)S(1)} %collective-permute-done.14.d), custom_call_target="tpu_custom_call" | custom-call | tf_op jit(solution)/shard_map/finish/pallas_call | solution.py:304
  (27 shorter events, 0.5 us)
Async XLA Ops:
  0.6 5.3 %copy-start = (s32[8192]{0:T(1024)S(1)}, s32[8192]{0:T(1024)}, u32[]{:S(2)}) copy-start(s32[8192]{0:T(1024)} %param.10) | copy-start | bytes 98308
  0.6 5.3 %copy-start.1 = (bf16[256,32]{0,1:T(8,128)(2,1)S(1)}, bf16[256,32]{0,1:T(8,128)(2,1)}, u32[]{:S(2)}) copy-start(bf16[256,32]{0,1:T(8,128)(2,1)} %param.11) | copy-start | bytes 49156
  0.7 5.3 %copy-start.2 = (bf16[8192]{0:T(1024)(128)(2,1)S(1)}, bf16[8192]{0:T(1024)(128)(2,1)}, u32[]{:S(2)}) copy-start(bf16[8192]{0:T(1024)(128)(2,1)} %param.8) | copy-start | bytes 49156
  5.8 3.1 %collective-permute-start = (f32[32,4096]{1,0:T(8,128)}, f32[32,4096]{1,0:T(8,128)S(1)}, u32[]{:S(2)}, u32[]{:S(2)}) collective-permute-start(f32[32,4096]{1,0:T(8,128)} %get-tuple-element.26), channel_id=1, source_target_pairs={{0,1},{1,0},{2,3},{3,2},{4,5},{5,4},{6,7},{7,6},{8,9},{9,8},{10,11... | collective-permute-start | bytes 1572872 | tf_op jit(solution)/shard_map/ppermute | solution.py:318
  9.2 21.7 %copy-start.3 = (s32[8192,16]{0,1:T(8,128)S(1)}, s32[8192,16]{0,1:T(8,128)}, u32[]{:S(2)}) copy-start(s32[8192,16]{0,1:T(8,128)} %param.9) | copy-start | bytes 1572868
  9.2 6.7 %collective-permute-start.1 = (f16[33,1024]{1,0:T(8,128)(2,1)S(1)}, f16[33,1024]{1,0:T(8,128)(2,1)S(1)}, u32[]{:S(2)}, u32[]{:S(2)}) collective-permute-start(f16[33,1024]{1,0:T(8,128)(2,1)S(1)} %pad_maximum_fusion.2), channel_id=1, source_target_pairs={{0,4},{1,5},{2,6},{3,7},{4,0},{5,1},{6,2},{7,3},{8,12},{9,13},{10,... | collective-permute-start | bytes 202760 | tf_op jit(solution)/shard_map/ppermute | solution.py:323
  10.7 6.1 %collective-permute-start.2 = (f16[33,1024]{1,0:T(8,128)(2,1)S(1)}, f16[33,1024]{1,0:T(8,128)(2,1)S(1)}, u32[]{:S(2)}, u32[]{:S(2)}) collective-permute-start(f16[33,1024]{1,0:T(8,128)(2,1)S(1)} %pad_maximum_fusion.3), channel_id=1, source_target_pairs={{0,2},{1,3},{2,4},{3,5},{4,6},{5,7},{6,0},{7,1},{8,10},{9,11},{10,... | collective-permute-start | bytes 202760 | tf_op jit(solution)/shard_map/ppermute | solution.py:323
  12.8 5.7 %collective-permute-start.3 = (f16[33,1024]{1,0:T(8,128)(2,1)S(1)}, f16[33,1024]{1,0:T(8,128)(2,1)S(1)}, u32[]{:S(2)}, u32[]{:S(2)}) collective-permute-start(f16[33,1024]{1,0:T(8,128)(2,1)S(1)} %pad_maximum_fusion.4), channel_id=1, source_target_pairs={{0,6},{1,7},{2,0},{3,1},{4,2},{5,3},{6,4},{7,5},{8,14},{9,15},{10,... | collective-permute-start | bytes 202760 | tf_op jit(solution)/shard_map/ppermute | solution.py:323
  18.7 9.8 %collective-permute-start.4 = (f16[33,1024]{1,0:T(8,128)(2,1)S(1)}, f16[33,1024]{1,0:T(8,128)(2,1)S(1)}, u32[]{:S(2)}, u32[]{:S(2)}) collective-permute-start(f16[33,1024]{1,0:T(8,128)(2,1)S(1)} %pad_maximum_fusion.5), channel_id=1, source_target_pairs={{0,8},{1,9},{2,10},{3,11},{4,12},{5,13},{6,14},{7,15},{8,0},{9,1},... | collective-permute-start | bytes 202760 | tf_op jit(solution)/shard_map/ppermute | solution.py:318
  28.5 4.3 %collective-permute-start.7 = (bf16[32,1024]{1,0:T(8,128)(2,1)S(1)}, bf16[32,1024]{1,0:T(8,128)(2,1)S(1)}, u32[]{:S(2)}, u32[]{:S(2)}) collective-permute-start(bf16[32,1024]{1,0:T(8,128)(2,1)S(1)} %fusion.1.sketch), channel_id=1, source_target_pairs={{0,2},{1,3},{2,4},{3,5},{4,6},{5,7},{6,0},{7,1},{8,10},{9,11},{10,... | collective-permute-start | bytes 196616 | tf_op jit(solution)/shard_map/ppermute | solution.py:323
  28.9 5.8 %collective-permute-start.6 = (bf16[32,1024]{1,0:T(8,128)(2,1)S(1)}, bf16[32,1024]{1,0:T(8,128)(2,1)S(1)}, u32[]{:S(2)}, u32[]{:S(2)}) collective-permute-start(bf16[32,1024]{1,0:T(8,128)(2,1)S(1)} %fusion.1.sketch), channel_id=1, source_target_pairs={{0,4},{1,5},{2,6},{3,7},{4,0},{5,1},{6,2},{7,3},{8,12},{9,13},{10,... | collective-permute-start | bytes 196616 | tf_op jit(solution)/shard_map/ppermute | solution.py:323
  30.1 5.5 %collective-permute-start.5 = (bf16[32,1024]{1,0:T(8,128)(2,1)S(1)}, bf16[32,1024]{1,0:T(8,128)(2,1)S(1)}, u32[]{:S(2)}, u32[]{:S(2)}) collective-permute-start(bf16[32,1024]{1,0:T(8,128)(2,1)S(1)} %fusion.1.sketch), channel_id=1, source_target_pairs={{0,6},{1,7},{2,0},{3,1},{4,2},{5,3},{6,4},{7,5},{8,14},{9,15},{10,... | collective-permute-start | bytes 196616 | tf_op jit(solution)/shard_map/ppermute | solution.py:323
  35.6 3.9 %collective-permute-start.8 = (bf16[32,4096]{1,0:T(8,128)(2,1)S(1)}, bf16[32,4096]{1,0:T(8,128)(2,1)S(1)}, u32[]{:S(2)}, u32[]{:S(2)}) collective-permute-start(bf16[32,4096]{1,0:T(8,128)(2,1)S(1)} %pad_maximum_fusion), channel_id=1, source_target_pairs={{0,1},{1,0},{2,3},{3,2},{4,5},{5,4},{6,7},{7,6},{8,9},{9,8},{10,11... | collective-permute-start | bytes 786440 | tf_op jit(solution)/shard_map/ppermute | solution.py:318
  35.9 3.6 %copy-start.4 = (f32[4,48,128]{2,1,0:T(8,128)S(1)}, f32[4,48,128]{2,1,0:T(8,128)}, u32[]{:S(2)}) copy-start(f32[4,48,128]{2,1,0:T(8,128)} %get-tuple-element.36.leaf_a) | copy-start | bytes 294916
  44.4 4.9 %collective-permute-start.9 = (s16[320,128]{1,0:T(8,128)(2,1)S(1)}, s16[320,128]{1,0:T(8,128)(2,1)S(1)}, u32[]{:S(2)}, u32[]{:S(2)}) collective-permute-start(s16[320,128]{1,0:T(8,128)(2,1)S(1)} %get-tuple-element.40), channel_id=1, source_target_pairs={{0,16},{16,0},{32,48},{48,32},{64,80},{80,64},{96,112},{112,96},{1... | collective-permute-start | bytes 245768 | tf_op jit(solution)/shard_map/ppermute | solution.py:318
  46.0 7.6 %collective-permute-start.10 = (s16[320,128]{1,0:T(8,128)(2,1)S(1)}, s16[320,128]{1,0:T(8,128)(2,1)S(1)}, u32[]{:S(2)}, u32[]{:S(2)}) collective-permute-start(s16[320,128]{1,0:T(8,128)(2,1)S(1)} %get-tuple-element.41), channel_id=1, source_target_pairs={{0,32},{16,48},{32,0},{48,16},{64,96},{80,112},{96,64},{112,80},{1... | collective-permute-start | bytes 245768 | tf_op jit(solution)/shard_map/ppermute | solution.py:318
  48.9 6.3 %collective-permute-start.11 = (s16[320,128]{1,0:T(8,128)(2,1)S(1)}, s16[320,128]{1,0:T(8,128)(2,1)S(1)}, u32[]{:S(2)}, u32[]{:S(2)}) collective-permute-start(s16[320,128]{1,0:T(8,128)(2,1)S(1)} %get-tuple-element.42), channel_id=1, source_target_pairs={{0,48},{16,32},{32,16},{48,0},{64,112},{80,96},{96,80},{112,64},{1... | collective-permute-start | bytes 245768 | tf_op jit(solution)/shard_map/ppermute | solution.py:318
  55.5 5.9 %collective-permute-start.12 = (s16[112,128]{1,0:T(8,128)(2,1)S(1)}, s16[112,128]{1,0:T(8,128)(2,1)S(1)}, u32[]{:S(2)}, u32[]{:S(2)}) collective-permute-start(s16[112,128]{1,0:T(8,128)(2,1)S(1)} %get-tuple-element.44), channel_id=1, source_target_pairs={{0,64},{16,80},{32,96},{48,112},{64,128},{80,144},{96,160},{112,17... | collective-permute-start | bytes 86024 | tf_op jit(solution)/shard_map/ppermute | solution.py:323
  57.4 4.9 %collective-permute-start.13 = (s16[112,128]{1,0:T(8,128)(2,1)S(1)}, s16[112,128]{1,0:T(8,128)(2,1)S(1)}, u32[]{:S(2)}, u32[]{:S(2)}) collective-permute-start(s16[112,128]{1,0:T(8,128)(2,1)S(1)} %get-tuple-element.45), channel_id=1, source_target_pairs={{0,128},{16,144},{32,160},{48,176},{64,192},{80,208},{96,224},{112... | collective-permute-start | bytes 86024 | tf_op jit(solution)/shard_map/ppermute | solution.py:323
  59.4 3.9 %collective-permute-start.14 = (s16[112,128]{1,0:T(8,128)(2,1)S(1)}, s16[112,128]{1,0:T(8,128)(2,1)S(1)}, u32[]{:S(2)}, u32[]{:S(2)}) collective-permute-start(s16[112,128]{1,0:T(8,128)(2,1)S(1)} %get-tuple-element.46), channel_id=1, source_target_pairs={{0,192},{16,208},{32,224},{48,240},{64,0},{80,16},{96,32},{112,48}... | collective-permute-start | bytes 86024 | tf_op jit(solution)/shard_map/ppermute | solution.py:323

commit v6 on v5

--- a/solution.py
+++ b/solution.py
@@ -74,6 +74,7 @@
     pred, targ, weight_far, leaf_far, matrix_far, sketch_out, leaf_out,
     pred_here, targ_here, weight, leaf, matrix_t, sums, weights, weight_wide, arrived, small_arrived, *, blocks,
 ):
+    depth = 2 if len(blocks) == 4 else 3
     small = [
         pltpu.make_async_copy(far, here, small_arrived.at[n])
         for n, (far, here) in enumerate([(weight_far, weight), (leaf_far, leaf), (matrix_far, matrix_t)])
@@ -87,9 +88,10 @@
             pltpu.make_async_copy(pred.at[rows, :], pred_here.at[n], arrived.at[0, n]),
             pltpu.make_async_copy(targ.at[rows, :], targ_here.at[n], arrived.at[1, n]),
         ]
+        copies.append(pair)
+    for pair in copies[:depth]:
         for copy in pair:
             copy.start()
-        copies.append(pair)
     for copy in small:
         copy.wait()
     weight_wide[...] = weight[...].astype(F32)
@@ -102,6 +104,8 @@
         w_cols = jnp.transpose(w_tile)
         for copy in copies[n]:
             copy.wait()
+        for copy in copies[n + depth] if n + depth < len(blocks) else []:
+            copy.start()
         pieces = []
         for s in range(BLOCK // 128):
             rows = slice(128 * s, 128 * s + 128)
@@ -356,7 +360,7 @@
     across = swap(jnp.concatenate([own, near], axis=1), "out", 1)
     held = histogram_part(features_t, near, weight, held, [1, 2, 3])
     slices = histogram_last(features_t, across, weight, held, (leaf_a, leaf_b, leaf_c), [4, 5, 6, 7])
-    slices = regroup(slices[0], *[swap(slices[j], "rows", j) for j in (1, 2, 3)])
+    slices = regroup(slices[0], *[swap(slices[j], "rows", j) for j in (3, 2, 1)])
     return tuple(
         finish(slices[0], *[shift(slices[j], "rows", 4, j) for j in (1, 2, 3)], float(cells * 16 // BINS))
     )

time: 64.9 us -> 63.4 us (0.977)
  transfers between devices with their start and end apart: 15 -> 15, of which waited for: 12 -> 11; matrix products, arithmetic and copies ran while one was open for 0% -> 0% of each run, Pallas kernels for 15% -> 16%
where the time goes in v6:
time: 63.4 us; the launch traced here: 62.5 us
  starting transfers between devices  23.7 us (37%)
  Pallas kernels  20.4 us (32%)
  waiting for transfers between devices  16.9 us (27%)
  between operations  0.97 us (2%)
    ppermute x9, starting transfers between devices, shift(): lax.ppermute(value, axis, [(i, i + ((place(i) + step) % 4 - place(i)) * u...  11.8 us
    ppermute x6, starting transfers between devices, swap(): return lax.ppermute(value, axis, [(i, i ^ flip) for i in range(16)])  11.8 us
    pallas_call x3, Pallas kernels, gradient(): pl.pallas_call(functools.partial(gradient_kernel, blocks=blocks), in_spec...  9.54 us
    ppermute x9, waiting for transfers between devices, shift(): lax.ppermute(value, axis, [(i, i + ((place(i) + step) % 4 - place(i)) * u...  8.7 us
    ppermute x6, waiting for transfers between devices, swap(): return lax.ppermute(value, axis, [(i, i ^ flip) for i in range(16)])  8.22 us
    pallas_call x2, Pallas kernels, histogram_part(): pl.pallas_call(functools.partial(histogram_part_kernel, blocks=blocks), s...  5.03 us
    pallas_call x1, Pallas kernels, histogram_last(): pl.pallas_call(functools.partial(histogram_last_kernel, blocks=blocks), s...  4.82 us
  transfers between devices with their start and end apart: 15, of which 11 were waited for; matrix products, arithmetic and copies ran while one was open for 0% of the time, Pallas kernels for 16%

profile of v6, /device:TPU:6, one launch (start us, length us, event | category | flops | bytes accessed | tf_op | source)
XLA Modules:
  0.0 62.5 jit_solution(15859243374718872903)
XLA Ops:
  0.6 0.0 copy-start
  0.6 0.0 copy-start.1
  0.7 0.0 copy-start.2
  0.7 4.7 %gradient.4 = (f32[32,4096]{1,0:T(8,128)}, f32[4,48,128]{2,1,0:T(8,128)}) custom-call(bf16[8192,256]{1,0:T(8,128)(2,1)} %pred_.5, bf16[8192,256]{1,0:T(8,128)(2,1)} %targ.5, bf16[64,128]{1,0:T(8,128)(2,1)} %bitcast.14, s32[64,128]{1,0:T(8,128)} %bitcast.8, bf16[32,256]{1,0:T(8,128)(2,1)} %bitcast.11), custom_call_target="tpu_custom_call" | custom-call | flops 2000000000 | bytes 6000000 | tf_op jit(solution)/shard_map/gradient/pallas_call | solution.py:140
  5.4 0.1 collective-permute-start
  5.5 0.0 copy-done
  5.5 0.0 copy-done.1
  5.5 0.0 copy-done.2
  5.5 2.9 %gradient.3 = (f32[32,3072]{1,0:T(8,128)S(1)}, f32[4,48,128]{2,1,0:T(8,128)S(1)}) custom-call(bf16[8192,256]{1,0:T(8,128)(2,1)} %pred_.5, bf16[8192,256]{1,0:T(8,128)(2,1)} %targ.5, bf16[64,128]{1,0:T(8,128)(2,1)S(1)} %bitcast.15, s32[64,128]{1,0:T(8,128)S(1)} %bitcast.9, bf16[32,256]{1,0:T(8,128)(2,1)S(1)} %bitcast.12), custom_call_target="tpu_custom_call" | custom-call | flops 1500000000 | bytes 4500000 | tf_op jit(solution)/shard_map/gradient/pallas_call | solution.py:140
  8.5 0.0 collective-permute-done
  8.8 0.0 copy-start.3
  8.8 1.4 %collective-permute-start.1 = (f16[33,1024]{1,0:T(8,128)(2,1)S(1)}, f16[33,1024]{1,0:T(8,128)(2,1)S(1)}, u32[]{:S(2)}, u32[]{:S(2)}) collective-permute-start(f16[33,1024]{1,0:T(8,128)(2,1)S(1)} %pad_maximum_fusion.2), channel_id=1, source_target_pairs={{0,4},{1,5},{2,6},{3,7},{4,0},{5,1},{6,2},{7,3},{8,12},{9,13},{10,... | collective-permute-start | bytes 202760 | tf_op jit(solution)/shard_map/ppermute | solution.py:327
  10.2 2.1 %collective-permute-start.2 = (f16[33,1024]{1,0:T(8,128)(2,1)S(1)}, f16[33,1024]{1,0:T(8,128)(2,1)S(1)}, u32[]{:S(2)}, u32[]{:S(2)}) collective-permute-start(f16[33,1024]{1,0:T(8,128)(2,1)S(1)} %pad_maximum_fusion.3), channel_id=1, source_target_pairs={{0,2},{1,3},{2,4},{3,5},{4,6},{5,7},{6,0},{7,1},{8,10},{9,11},{10,... | collective-permute-start | bytes 202760 | tf_op jit(solution)/shard_map/ppermute | solution.py:327
  12.3 0.0 collective-permute-start.3
  12.3 1.9 %gradient.5 = (f32[32,1024]{1,0:T(8,128)S(1)}, f32[4,48,128]{2,1,0:T(8,128)S(1)}) custom-call(bf16[8192,256]{1,0:T(8,128)(2,1)} %pred_.5, bf16[8192,256]{1,0:T(8,128)(2,1)} %targ.5, bf16[64,128]{1,0:T(8,128)(2,1)S(1)} %bitcast.16, s32[64,128]{1,0:T(8,128)S(1)} %bitcast.10, bf16[32,256]{1,0:T(8,128)(2,1)S(1)} %bitcast.13), custom_call_target="tpu_custom_call" | custom-call | flops 500000000 | bytes 1500000 | tf_op jit(solution)/shard_map/gradient/pallas_call | solution.py:140
  14.2 1.3 %collective-permute-done.1 = f16[33,1024]{1,0:T(8,128)(2,1)S(1)} collective-permute-done((f16[33,1024]{1,0:T(8,128)(2,1)S(1)}, f16[33,1024]{1,0:T(8,128)(2,1)S(1)}, u32[]{:S(2)}, u32[]{:S(2)}) %collective-permute-start.1) | collective-permute-done | bytes 67616 | tf_op jit(solution)/shard_map/ppermute | solution.py:327
  15.6 0.9 %collective-permute-done.2 = f16[33,1024]{1,0:T(8,128)(2,1)S(1)} collective-permute-done((f16[33,1024]{1,0:T(8,128)(2,1)S(1)}, f16[33,1024]{1,0:T(8,128)(2,1)S(1)}, u32[]{:S(2)}, u32[]{:S(2)}) %collective-permute-start.2) | collective-permute-done | bytes 67616 | tf_op jit(solution)/shard_map/ppermute | solution.py:327
  16.5 1.5 %collective-permute-done.3 = f16[33,1024]{1,0:T(8,128)(2,1)S(1)} collective-permute-done((f16[33,1024]{1,0:T(8,128)(2,1)S(1)}, f16[33,1024]{1,0:T(8,128)(2,1)S(1)}, u32[]{:S(2)}, u32[]{:S(2)}) %collective-permute-start.3) | collective-permute-done | bytes 67616 | tf_op jit(solution)/shard_map/ppermute | solution.py:327
  18.0 0.1 abs_reduce_fusion
  18.2 7.3 %collective-permute-start.4 = (f16[33,1024]{1,0:T(8,128)(2,1)S(1)}, f16[33,1024]{1,0:T(8,128)(2,1)S(1)}, u32[]{:S(2)}, u32[]{:S(2)}) collective-permute-start(f16[33,1024]{1,0:T(8,128)(2,1)S(1)} %pad_maximum_fusion.5), channel_id=1, source_target_pairs={{0,8},{1,9},{2,10},{3,11},{4,12},{5,13},{6,14},{7,15},{8,0},{9,1},... | collective-permute-start | bytes 202760 | tf_op jit(solution)/shard_map/ppermute | solution.py:322
  25.4 2.5 %collective-permute-done.4 = f16[33,1024]{1,0:T(8,128)(2,1)S(1)} collective-permute-done((f16[33,1024]{1,0:T(8,128)(2,1)S(1)}, f16[33,1024]{1,0:T(8,128)(2,1)S(1)}, u32[]{:S(2)}, u32[]{:S(2)}) %collective-permute-start.4) | collective-permute-done | bytes 67616 | tf_op jit(solution)/shard_map/ppermute | solution.py:322
  28.0 0.4 collective-permute-start.7
  28.4 1.3 %collective-permute-start.6 = (bf16[32,1024]{1,0:T(8,128)(2,1)S(1)}, bf16[32,1024]{1,0:T(8,128)(2,1)S(1)}, u32[]{:S(2)}, u32[]{:S(2)}) collective-permute-start(bf16[32,1024]{1,0:T(8,128)(2,1)S(1)} %fusion.1.sketch), channel_id=1, source_target_pairs={{0,4},{1,5},{2,6},{3,7},{4,0},{5,1},{6,2},{7,3},{8,12},{9,13},{10,... | collective-permute-start | bytes 196616 | tf_op jit(solution)/shard_map/ppermute | solution.py:327
  29.7 0.8 %collective-permute-start.5 = (bf16[32,1024]{1,0:T(8,128)(2,1)S(1)}, bf16[32,1024]{1,0:T(8,128)(2,1)S(1)}, u32[]{:S(2)}, u32[]{:S(2)}) collective-permute-start(bf16[32,1024]{1,0:T(8,128)(2,1)S(1)} %fusion.1.sketch), channel_id=1, source_target_pairs={{0,6},{1,7},{2,0},{3,1},{4,2},{5,3},{6,4},{7,5},{8,14},{9,15},{10,... | collective-permute-start | bytes 196616 | tf_op jit(solution)/shard_map/ppermute | solution.py:327
  30.5 0.0 copy-done.3
  30.5 1.4 %histogram.3 = (f32[16,128,64]{2,1,0:T(8,128)S(1)}, f32[2,128,16]{2,1,0:T(8,128)S(1)}) custom-call(s32[16,8192]{1,0:T(8,128)S(1)} %bitcast.20, bf16[32,1024]{1,0:T(8,128)(2,1)S(1)} %fusion.1.sketch, bf16[64,128]{1,0:T(8,128)(2,1)S(1)} %bitcast.17), custom_call_target="tpu_custom_call" | custom-call | flops 1073741824 | bytes 300000 | tf_op jit(solution)/shard_map/histogram/pallas_call | solution.py:243
  31.9 0.5 collective-permute-done.7
  32.4 1.8 %collective-permute-done.6 = bf16[32,1024]{1,0:T(8,128)(2,1)S(1)} collective-permute-done((bf16[32,1024]{1,0:T(8,128)(2,1)S(1)}, bf16[32,1024]{1,0:T(8,128)(2,1)S(1)}, u32[]{:S(2)}, u32[]{:S(2)}) %collective-permute-start.6) | collective-permute-done | bytes 65568 | tf_op jit(solution)/shard_map/ppermute | solution.py:327
  34.2 1.0 %collective-permute-done.5 = bf16[32,1024]{1,0:T(8,128)(2,1)S(1)} collective-permute-done((bf16[32,1024]{1,0:T(8,128)(2,1)S(1)}, bf16[32,1024]{1,0:T(8,128)(2,1)S(1)}, u32[]{:S(2)}, u32[]{:S(2)}) %collective-permute-start.5) | collective-permute-done | bytes 65568 | tf_op jit(solution)/shard_map/ppermute | solution.py:327
  35.2 0.3 collective-permute-start.8
  35.5 0.0 copy-start.4
  35.5 3.6 %histogram.4 = (f32[16,128,64]{2,1,0:T(8,128)S(1)}, f32[2,128,16]{2,1,0:T(8,128)S(1)}) custom-call(s32[16,8192]{1,0:T(8,128)S(1)} %bitcast.21, bf16[32,3072]{1,0:T(8,128)(2,1)S(1)} %pad_maximum_fusion.1.sketch, bf16[64,128]{1,0:T(8,128)(2,1)S(1)} %bitcast.18, f32[16,128,64]{2,1,0:T(8,128)S(1)} %get-tuple-element.32.refs_0_, ...), custom_call_target="tpu_custom_call" | custom-call | flops 3221225472 | bytes 900000 | tf_op jit(solution)/shard_map/histogram/pallas_call | solution.py:243
  39.1 0.0 collective-permute-done.8.sketch
  39.1 4.8 %histogram.5 = (f32[304,128]{1,0:T(8,128)S(1)}, s16[320,128]{1,0:T(8,128)(2,1)S(1)}, s16[320,128]{1,0:T(8,128)(2,1)S(1)}, s16[320,128]{1,0:T(8,128)(2,1)S(1)}) custom-call(s32[16,8192]{1,0:T(8,128)S(1)} %bitcast.22, bf16[32,4096]{1,0:T(8,128)(2,1)S(1)} %collective-permute-done.8.sketch, bf16[64,128]{1,0:T(8,128)(2,1)S(1)} %bitcast.19, ...), custom_call_target="tpu_custom_call" | custom-call | flops 4294967296 | bytes 1200000 | tf_op jit(solution)/shard_map/histogram/pallas_call | solution.py:252
  43.9 3.1 %collective-permute-start.9 = (s16[320,128]{1,0:T(8,128)(2,1)S(1)}, s16[320,128]{1,0:T(8,128)(2,1)S(1)}, u32[]{:S(2)}, u32[]{:S(2)}) collective-permute-start(s16[320,128]{1,0:T(8,128)(2,1)S(1)} %get-tuple-element.40), channel_id=1, source_target_pairs={{0,48},{16,32},{32,16},{48,0},{64,112},{80,96},{96,80},{112,64},{1... | collective-permute-start | bytes 245768 | tf_op jit(solution)/shard_map/ppermute | solution.py:322
  47.0 0.6 %collective-permute-start.10 = (s16[320,128]{1,0:T(8,128)(2,1)S(1)}, s16[320,128]{1,0:T(8,128)(2,1)S(1)}, u32[]{:S(2)}, u32[]{:S(2)}) collective-permute-start(s16[320,128]{1,0:T(8,128)(2,1)S(1)} %get-tuple-element.41), channel_id=1, source_target_pairs={{0,32},{16,48},{32,0},{48,16},{64,96},{80,112},{96,64},{112,80},{1... | collective-permute-start | bytes 245768 | tf_op jit(solution)/shard_map/ppermute | solution.py:322
  47.7 0.5 collective-permute-start.11
  48.1 3.0 %collective-permute-done.9.b = s16[320,128]{1,0:T(8,128)(2,1)S(1)} collective-permute-done((s16[320,128]{1,0:T(8,128)(2,1)S(1)}, s16[320,128]{1,0:T(8,128)(2,1)S(1)}, u32[]{:S(2)}, u32[]{:S(2)}) %collective-permute-start.9) | collective-permute-done | bytes 81952 | tf_op jit(solution)/shard_map/ppermute | solution.py:322
  51.2 2.6 %collective-permute-done.10.c = s16[320,128]{1,0:T(8,128)(2,1)S(1)} collective-permute-done((s16[320,128]{1,0:T(8,128)(2,1)S(1)}, s16[320,128]{1,0:T(8,128)(2,1)S(1)}, u32[]{:S(2)}, u32[]{:S(2)}) %collective-permute-start.10) | collective-permute-done | bytes 81952 | tf_op jit(solution)/shard_map/ppermute | solution.py:322
  53.8 0.0 collective-permute-done.11.d
  53.8 0.2 regroup.1
  54.1 1.8 %collective-permute-start.12 = (s16[112,128]{1,0:T(8,128)(2,1)S(1)}, s16[112,128]{1,0:T(8,128)(2,1)S(1)}, u32[]{:S(2)}, u32[]{:S(2)}) collective-permute-start(s16[112,128]{1,0:T(8,128)(2,1)S(1)} %get-tuple-element.44), channel_id=1, source_target_pairs={{0,64},{16,80},{32,96},{48,112},{64,128},{80,144},{96,160},{112,17... | collective-permute-start | bytes 86024 | tf_op jit(solution)/shard_map/ppermute | solution.py:327
  55.9 2.0 %collective-permute-start.13 = (s16[112,128]{1,0:T(8,128)(2,1)S(1)}, s16[112,128]{1,0:T(8,128)(2,1)S(1)}, u32[]{:S(2)}, u32[]{:S(2)}) collective-permute-start(s16[112,128]{1,0:T(8,128)(2,1)S(1)} %get-tuple-element.45), channel_id=1, source_target_pairs={{0,128},{16,144},{32,160},{48,176},{64,192},{80,208},{96,224},{112... | collective-permute-start | bytes 86024 | tf_op jit(solution)/shard_map/ppermute | solution.py:327
  57.9 2.1 %collective-permute-start.14 = (s16[112,128]{1,0:T(8,128)(2,1)S(1)}, s16[112,128]{1,0:T(8,128)(2,1)S(1)}, u32[]{:S(2)}, u32[]{:S(2)}) collective-permute-start(s16[112,128]{1,0:T(8,128)(2,1)S(1)} %get-tuple-element.46), channel_id=1, source_target_pairs={{0,192},{16,208},{32,224},{48,240},{64,0},{80,16},{96,32},{112,48}... | collective-permute-start | bytes 86024 | tf_op jit(solution)/shard_map/ppermute | solution.py:327
  60.0 0.0 collective-permute-done.12.b
  60.0 0.7 %collective-permute-done.13.c = s16[112,128]{1,0:T(8,128)(2,1)S(1)} collective-permute-done((s16[112,128]{1,0:T(8,128)(2,1)S(1)}, s16[112,128]{1,0:T(8,128)(2,1)S(1)}, u32[]{:S(2)}, u32[]{:S(2)}) %collective-permute-start.13) | collective-permute-done | bytes 28704 | tf_op jit(solution)/shard_map/ppermute | solution.py:327
  60.7 1.1 %collective-permute-done.14.d = s16[112,128]{1,0:T(8,128)(2,1)S(1)} collective-permute-done((s16[112,128]{1,0:T(8,128)(2,1)S(1)}, s16[112,128]{1,0:T(8,128)(2,1)S(1)}, u32[]{:S(2)}, u32[]{:S(2)}) %collective-permute-start.14) | collective-permute-done | bytes 28704 | tf_op jit(solution)/shard_map/ppermute | solution.py:327
  61.8 0.8 %finish.1 = (f32[16,16,32]{2,1,0:T(8,128)}, f32[16,16]{1,0:T(8,128)}, f32[4,256]{1,0:T(4,128)}) custom-call(f32[96,128]{1,0:T(8,128)S(1)} %get-tuple-element.43.a, s16[112,128]{1,0:T(8,128)(2,1)S(1)} %collective-permute-done.12.b, s16[112,128]{1,0:T(8,128)(2,1)S(1)} %collective-permute-done.13.c, s16[112,128]{1,0:T(8,128)(2,1)S(1)} %collective-permute-done.14.d), custom_call_target="tpu_custom_call" | custom-call | tf_op jit(solution)/shard_map/finish/pallas_call | solution.py:308
  (27 shorter events, 0.5 us)
Async XLA Ops:
  0.6 4.9 %copy-start = (s32[8192]{0:T(1024)S(1)}, s32[8192]{0:T(1024)}, u32[]{:S(2)}) copy-start(s32[8192]{0:T(1024)} %param.10) | copy-start | bytes 98308
  0.6 4.9 %copy-start.1 = (bf16[256,32]{0,1:T(8,128)(2,1)S(1)}, bf16[256,32]{0,1:T(8,128)(2,1)}, u32[]{:S(2)}) copy-start(bf16[256,32]{0,1:T(8,128)(2,1)} %param.11) | copy-start | bytes 49156
  0.7 4.9 %copy-start.2 = (bf16[8192]{0:T(1024)(128)(2,1)S(1)}, bf16[8192]{0:T(1024)(128)(2,1)}, u32[]{:S(2)}) copy-start(bf16[8192]{0:T(1024)(128)(2,1)} %param.8) | copy-start | bytes 49156
  5.4 3.1 %collective-permute-start = (f32[32,4096]{1,0:T(8,128)}, f32[32,4096]{1,0:T(8,128)S(1)}, u32[]{:S(2)}, u32[]{:S(2)}) collective-permute-start(f32[32,4096]{1,0:T(8,128)} %get-tuple-element.26), channel_id=1, source_target_pairs={{0,1},{1,0},{2,3},{3,2},{4,5},{5,4},{6,7},{7,6},{8,9},{9,8},{10,11... | collective-permute-start | bytes 1572872 | tf_op jit(solution)/shard_map/ppermute | solution.py:322
  8.8 21.7 %copy-start.3 = (s32[8192,16]{0,1:T(8,128)S(1)}, s32[8192,16]{0,1:T(8,128)}, u32[]{:S(2)}) copy-start(s32[8192,16]{0,1:T(8,128)} %param.9) | copy-start | bytes 1572868
  8.8 6.7 %collective-permute-start.1 = (f16[33,1024]{1,0:T(8,128)(2,1)S(1)}, f16[33,1024]{1,0:T(8,128)(2,1)S(1)}, u32[]{:S(2)}, u32[]{:S(2)}) collective-permute-start(f16[33,1024]{1,0:T(8,128)(2,1)S(1)} %pad_maximum_fusion.2), channel_id=1, source_target_pairs={{0,4},{1,5},{2,6},{3,7},{4,0},{5,1},{6,2},{7,3},{8,12},{9,13},{10,... | collective-permute-start | bytes 202760 | tf_op jit(solution)/shard_map/ppermute | solution.py:327
  10.2 6.2 %collective-permute-start.2 = (f16[33,1024]{1,0:T(8,128)(2,1)S(1)}, f16[33,1024]{1,0:T(8,128)(2,1)S(1)}, u32[]{:S(2)}, u32[]{:S(2)}) collective-permute-start(f16[33,1024]{1,0:T(8,128)(2,1)S(1)} %pad_maximum_fusion.3), channel_id=1, source_target_pairs={{0,2},{1,3},{2,4},{3,5},{4,6},{5,7},{6,0},{7,1},{8,10},{9,11},{10,... | collective-permute-start | bytes 202760 | tf_op jit(solution)/shard_map/ppermute | solution.py:327
  12.3 5.7 %collective-permute-start.3 = (f16[33,1024]{1,0:T(8,128)(2,1)S(1)}, f16[33,1024]{1,0:T(8,128)(2,1)S(1)}, u32[]{:S(2)}, u32[]{:S(2)}) collective-permute-start(f16[33,1024]{1,0:T(8,128)(2,1)S(1)} %pad_maximum_fusion.4), channel_id=1, source_target_pairs={{0,6},{1,7},{2,0},{3,1},{4,2},{5,3},{6,4},{7,5},{8,14},{9,15},{10,... | collective-permute-start | bytes 202760 | tf_op jit(solution)/shard_map/ppermute | solution.py:327
  18.2 9.8 %collective-permute-start.4 = (f16[33,1024]{1,0:T(8,128)(2,1)S(1)}, f16[33,1024]{1,0:T(8,128)(2,1)S(1)}, u32[]{:S(2)}, u32[]{:S(2)}) collective-permute-start(f16[33,1024]{1,0:T(8,128)(2,1)S(1)} %pad_maximum_fusion.5), channel_id=1, source_target_pairs={{0,8},{1,9},{2,10},{3,11},{4,12},{5,13},{6,14},{7,15},{8,0},{9,1},... | collective-permute-start | bytes 202760 | tf_op jit(solution)/shard_map/ppermute | solution.py:322
  28.0 4.3 %collective-permute-start.7 = (bf16[32,1024]{1,0:T(8,128)(2,1)S(1)}, bf16[32,1024]{1,0:T(8,128)(2,1)S(1)}, u32[]{:S(2)}, u32[]{:S(2)}) collective-permute-start(bf16[32,1024]{1,0:T(8,128)(2,1)S(1)} %fusion.1.sketch), channel_id=1, source_target_pairs={{0,2},{1,3},{2,4},{3,5},{4,6},{5,7},{6,0},{7,1},{8,10},{9,11},{10,... | collective-permute-start | bytes 196616 | tf_op jit(solution)/shard_map/ppermute | solution.py:327
  28.4 5.8 %collective-permute-start.6 = (bf16[32,1024]{1,0:T(8,128)(2,1)S(1)}, bf16[32,1024]{1,0:T(8,128)(2,1)S(1)}, u32[]{:S(2)}, u32[]{:S(2)}) collective-permute-start(bf16[32,1024]{1,0:T(8,128)(2,1)S(1)} %fusion.1.sketch), channel_id=1, source_target_pairs={{0,4},{1,5},{2,6},{3,7},{4,0},{5,1},{6,2},{7,3},{8,12},{9,13},{10,... | collective-permute-start | bytes 196616 | tf_op jit(solution)/shard_map/ppermute | solution.py:327
  29.7 5.5 %collective-permute-start.5 = (bf16[32,1024]{1,0:T(8,128)(2,1)S(1)}, bf16[32,1024]{1,0:T(8,128)(2,1)S(1)}, u32[]{:S(2)}, u32[]{:S(2)}) collective-permute-start(bf16[32,1024]{1,0:T(8,128)(2,1)S(1)} %fusion.1.sketch), channel_id=1, source_target_pairs={{0,6},{1,7},{2,0},{3,1},{4,2},{5,3},{6,4},{7,5},{8,14},{9,15},{10,... | collective-permute-start | bytes 196616 | tf_op jit(solution)/shard_map/ppermute | solution.py:327
  35.2 3.9 %collective-permute-start.8 = (bf16[32,4096]{1,0:T(8,128)(2,1)S(1)}, bf16[32,4096]{1,0:T(8,128)(2,1)S(1)}, u32[]{:S(2)}, u32[]{:S(2)}) collective-permute-start(bf16[32,4096]{1,0:T(8,128)(2,1)S(1)} %pad_maximum_fusion), channel_id=1, source_target_pairs={{0,1},{1,0},{2,3},{3,2},{4,5},{5,4},{6,7},{7,6},{8,9},{9,8},{10,11... | collective-permute-start | bytes 786440 | tf_op jit(solution)/shard_map/ppermute | solution.py:322
  35.5 3.6 %copy-start.4 = (f32[4,48,128]{2,1,0:T(8,128)S(1)}, f32[4,48,128]{2,1,0:T(8,128)}, u32[]{:S(2)}) copy-start(f32[4,48,128]{2,1,0:T(8,128)} %get-tuple-element.36.leaf_a) | copy-start | bytes 294916
  43.9 7.2 %collective-permute-start.9 = (s16[320,128]{1,0:T(8,128)(2,1)S(1)}, s16[320,128]{1,0:T(8,128)(2,1)S(1)}, u32[]{:S(2)}, u32[]{:S(2)}) collective-permute-start(s16[320,128]{1,0:T(8,128)(2,1)S(1)} %get-tuple-element.40), channel_id=1, source_target_pairs={{0,48},{16,32},{32,16},{48,0},{64,112},{80,96},{96,80},{112,64},{1... | collective-permute-start | bytes 245768 | tf_op jit(solution)/shard_map/ppermute | solution.py:322
  47.0 6.8 %collective-permute-start.10 = (s16[320,128]{1,0:T(8,128)(2,1)S(1)}, s16[320,128]{1,0:T(8,128)(2,1)S(1)}, u32[]{:S(2)}, u32[]{:S(2)}) collective-permute-start(s16[320,128]{1,0:T(8,128)(2,1)S(1)} %get-tuple-element.41), channel_id=1, source_target_pairs={{0,32},{16,48},{32,0},{48,16},{64,96},{80,112},{96,64},{112,80},{1... | collective-permute-start | bytes 245768 | tf_op jit(solution)/shard_map/ppermute | solution.py:322
  47.7 6.2 %collective-permute-start.11 = (s16[320,128]{1,0:T(8,128)(2,1)S(1)}, s16[320,128]{1,0:T(8,128)(2,1)S(1)}, u32[]{:S(2)}, u32[]{:S(2)}) collective-permute-start(s16[320,128]{1,0:T(8,128)(2,1)S(1)} %get-tuple-element.42), channel_id=1, source_target_pairs={{0,16},{16,0},{32,48},{48,32},{64,80},{80,64},{96,112},{112,96},{1... | collective-permute-start | bytes 245768 | tf_op jit(solution)/shard_map/ppermute | solution.py:322
  54.1 5.9 %collective-permute-start.12 = (s16[112,128]{1,0:T(8,128)(2,1)S(1)}, s16[112,128]{1,0:T(8,128)(2,1)S(1)}, u32[]{:S(2)}, u32[]{:S(2)}) collective-permute-start(s16[112,128]{1,0:T(8,128)(2,1)S(1)} %get-tuple-element.44), channel_id=1, source_target_pairs={{0,64},{16,80},{32,96},{48,112},{64,128},{80,144},{96,160},{112,17... | collective-permute-start | bytes 86024 | tf_op jit(solution)/shard_map/ppermute | solution.py:327
  55.9 4.8 %collective-permute-start.13 = (s16[112,128]{1,0:T(8,128)(2,1)S(1)}, s16[112,128]{1,0:T(8,128)(2,1)S(1)}, u32[]{:S(2)}, u32[]{:S(2)}) collective-permute-start(s16[112,128]{1,0:T(8,128)(2,1)S(1)} %get-tuple-element.45), channel_id=1, source_target_pairs={{0,128},{16,144},{32,160},{48,176},{64,192},{80,208},{96,224},{112... | collective-permute-start | bytes 86024 | tf_op jit(solution)/shard_map/ppermute | solution.py:327
  57.9 3.9 %collective-permute-start.14 = (s16[112,128]{1,0:T(8,128)(2,1)S(1)}, s16[112,128]{1,0:T(8,128)(2,1)S(1)}, u32[]{:S(2)}, u32[]{:S(2)}) collective-permute-start(s16[112,128]{1,0:T(8,128)(2,1)S(1)} %get-tuple-element.46), channel_id=1, source_target_pairs={{0,192},{16,208},{32,224},{48,240},{64,0},{80,16},{96,32},{112,48}... | collective-permute-start | bytes 86024 | tf_op jit(solution)/shard_map/ppermute | solution.py:327
